TPU v7x, 32 devices: a whole 2x2x4 slice. The times are simulated.
32 devices in a mesh: group: 2 (over x), trade: 16 (over z, y, core).
Axes of the slice: x: 2, y: 2, z: 4, core: 2. Of those that a mesh axis runs over, the one named last changes fastest.
Arguments:
- factors: bfloat16 [128, 128], P(('group', 'trade')), parts along dimension 0, may hold values from -6 to 6
- loadings: float32 [32, 16], replicated, may hold values from -1.5 to 1.5
- trade_coef: bfloat16 [65536, 256], P(('group', 'trade')), parts along dimension 0, may hold values from -0.75 to 0.75
- basis_size: int32 [65536], P(('group', 'trade')), parts along dimension 0, may hold values from 4 to 32
- set_ids: int32 [65536], P(('group', 'trade')), parts along dimension 0, may hold values from 0 to 31
- live_count: int32 [32], P(('group', 'trade')), parts along dimension 0, may hold values from 1 to 2047, as said below
- netting_row: int32 [64], P('group'), parts along dimension 0, may hold values from 0 to 31, each once
- threshold: float32 [64], P(('group', 'trade')), parts along dimension 0, may hold values from 0.5 to 8
- margin_start: float32 [64, 64], P(('group', 'trade')), parts along dimension 0, may hold values from 0 to 3
Outputs:
- expected: float32 [64, 8], P(('group', 'trade')), parts along dimension 0
There are 2 independent parts, one for each index of `group`. A program takes and returns all parts, laid end to end along the dimension named above; an argument that names none is the same for every part. Nothing has to cross between parts.
Inputs may be any that keep to these rules, and one draw needn't show every extreme that they name: `live_count`: blocks b and b + 8 hold exactly 2048 live trades together.
All inputs are finite; a program needn't handle non-finite values.
Results may differ from a plain program's by a relative error of at most 0.00035.
Values may be sent and summed in bfloat16 or wider, within the bound.
No kernel may reach another device: no remote copies, remote signals or barrier semaphores. Data moves between devices by JAX's collectives and lax.ppermute only.
A program may use at most 64 MiB of HBM per device.

v0:
```python
import jax
import jax.numpy as jnp
from jax import lax
from jax.sharding import PartitionSpec as P

F = 16
K = 32
DATES = 8
LAG = 2


def positive_part(netted, margins, limits):
    row_total = netted.shape[0]
    path_count = netted.shape[2]
    margin = jnp.maximum(netted[:, : DATES - LAG] - limits[:, None, None], 0.0)
    held = jnp.broadcast_to(margins[:, None, :], (row_total, LAG, path_count))
    collateral = jnp.concatenate([held, margin], axis=1)
    return jnp.maximum(netted - collateral, 0.0)


def body(
    factors,
    loadings,
    trade_coef,
    basis_size,
    set_ids,
    live_count,
    netting_row,
    threshold,
    margin_start,
):
    part_rows = lax.all_gather(factors, "trade", axis=0, tiled=True)
    row_count = part_rows.shape[0]
    factor_cube = part_rows.astype(jnp.float32).reshape(row_count, DATES, F)
    loaded = jnp.einsum("pdf,kf->pdk", factor_cube, loadings, precision=lax.Precision.HIGHEST)
    basis_table = jnp.tanh(loaded).astype(jnp.bfloat16).reshape(row_count, DATES * K)
    path_total = basis_table.shape[0]
    basis_table = basis_table.reshape(path_total, DATES, K)
    set_total = netting_row.shape[0]
    slot_total = trade_coef.shape[0]
    live_now = live_count[0]
    trade_rows = netting_row[set_ids]
    basis_index = jnp.arange(K, dtype=jnp.int32)
    slot_index = jnp.arange(slot_total, dtype=jnp.int32)
    keep_mask = (basis_index[None, :] < basis_size[:, None]) & (slot_index < live_now)[:, None]
    coef_cube = trade_coef.reshape(slot_total, DATES, K)
    coef_used = jnp.where(keep_mask[:, None, :], coef_cube, jnp.zeros_like(coef_cube))
    slot_now = coef_used.shape[0]
    values = jnp.einsum("tdk,pdk->tdp", coef_used, basis_table, preferred_element_type=jnp.float32)
    values = values.astype(jnp.bfloat16).reshape(slot_now, DATES * path_total)
    set_index = jnp.arange(set_total, dtype=jnp.int32)
    onehot = (trade_rows[None, :] == set_index[:, None]).astype(jnp.bfloat16)
    netted = lax.psum_scatter(
        jnp.dot(onehot, values, preferred_element_type=jnp.float32),
        "trade",
        scatter_dimension=0,
        tiled=True,
    )
    netted = netted.reshape(threshold.shape[0], DATES, path_total)
    shortfall = jnp.sum(positive_part(netted, margin_start, threshold), axis=2)
    return shortfall / path_total


def solution(mesh):
    return jax.shard_map(
        body,
        mesh=mesh,
        in_specs=(
            P(("group", "trade"), None),
            P(),
            P(("group", "trade"), None),
            P(("group", "trade")),
            P(("group", "trade")),
            P(("group", "trade")),
            P("group"),
            P(("group", "trade")),
            P(("group", "trade"), None),
        ),
        out_specs=P(("group", "trade"), None),
        check_vma=False,
    )
```

profile of v0, /device:TPU:0, one launch (start us, length us, event | category | flops | bytes accessed | tf_op | source)
XLA Modules:
  0.0 149.2 jit_solution(146148267404146707)
XLA Ops:
  6.5 0.0 copy-start
  6.5 0.0 all-reduce.3.cloned.1.call-start
  6.5 1.8 %fusion.14 = (s32[1]{0:T(128)}, s32[1]{0:T(128)}, s32[1]{0:T(128)}, s32[1]{0:T(128)}, s32[1]{0:T(128)}, /*index=5*/s32[1]{0:T(128)}, s32[1]{0:T(128)}, s32[1]{0:...) fusion(s32[32]{0:T(128)} %param.15), kind=kLoop, calls=%fused_computation.25 | loop fusion | bytes 104 | tf_op jit(solution)/shard_map/gather | solution.py:42
  8.4 2.1 %fusion.13 = (s32[1]{0:T(128)}, s32[1]{0:T(128)}, s32[1]{0:T(128)}, s32[1]{0:T(128)}, s32[1]{0:T(128)}, /*index=5*/s32[1]{0:T(128)}, s32[1]{0:T(128)}, s32[1]{0:...) fusion(s32[32]{0:T(128)} %param.15), kind=kLoop, calls=%fused_computation.24 | loop fusion | bytes 152 | tf_op jit(solution)/shard_map/gather | solution.py:42
  10.4 23.4 %all-gather = bf16[16,4,128]{2,1,0:T(4,128)(2,1)S(1)} all-gather(bf16[1,4,128]{2,1,0:T(4,128)(2,1)} %bitcast.47), channel_id=1, replica_groups=mesh['group'=2,'trade'=16] {'trade'}, dimensions={0}, use_global_device_ids=true | all-gather | bytes 17408 | tf_op jit(solution)/shard_map/all_gather | solution.py:32
  33.8 0.1 reshape.48
  33.9 1.5 copy.13
  35.4 0.0 copy-start.2
  36.1 0.5 fusion
  36.6 0.1 fusion.5
  36.7 0.0 copy-start.5
  36.7 0.0 copy-start.4
  36.7 0.0 copy-start.3
  36.7 0.8 convolution_convert_fusion
  37.5 20.0 %select_select_fusion = s32[2048]{0:T(1024)S(1)} fusion(s32[2048]{0:T(1024)S(1)} %copy-done.2, s32[]{:T(128)} %bitcast, s32[]{:T(128)} %bitcast.1, s32[]{:T(128)} %bitcast.2, s32[]{:T(128)} %bitcast.3, s32[]{:T(128)} %bitcast.4, s32[]{:T(128)} %bitcast.5, s32[]{:T(128)} %bitcast.6, s32[]{:T(128)} %bitcast.7, s32[]{:T(128)} %bitcast.8, s32[]{:T(128)} %bitcast.9, ...), kind=kLoop, calls=%fused_computation.19 | loop fusion | flops 133120 | bytes 16512 | tf_op jit(solution)/shard_map/gather | solution.py:42
  57.5 1.3 fusion.4
  58.8 0.0 all-reduce.3.cloned.1.call-update
  58.9 0.6 dynamic-slice
  60.1 80.6 %all-reduce.3.cloned.1.call-done = f32[32,512]{1,0:T(8,128)} async-done(((f32[32,512]{1,0:T(8,128)}), f32[32,512]{1,0:T(8,128)}) %all-reduce.3.cloned.1.call-update) | async-done | bytes 65552
  140.8 0.7 constant_dynamic-slice_fusion
  141.5 0.1 reshape.51
  141.6 0.1 fusion.8
  141.6 0.1 fusion.10
  141.7 0.6 broadcast_multiply_fusion
  (9 shorter events, 0.0 us)
Async XLA Ops:
  6.5 29.6 %copy-start = (f32[32,16]{0,1:T(8,128)S(1)}, f32[32,16]{0,1:T(8,128)}, u32[]{:S(2)}) copy-start(f32[32,16]{0,1:T(8,128)} %param.10) | copy-start | bytes 6148
  6.5 30.1 %copy-start.1 = (s32[2048]{0:T(1024)S(1)}, s32[2048]{0:T(1024)}, u32[]{:S(2)}) copy-start(s32[2048]{0:T(1024)} %param.12) | copy-start | bytes 24580
  6.5 134.2 %all-reduce.3.cloned.1.call-start = ((), (), s32[]{:S(2)}) async-start(), calls=%async_computation | async-start | bytes 131072
  35.4 2.1 %copy-start.2 = (s32[2048]{0:T(1024)S(1)}, s32[2048]{0:T(1024)}, u32[]{:S(2)}) copy-start(s32[2048]{0:T(1024)} %param.13) | copy-start | bytes 24580
  36.7 22.2 %copy-start.5 = (u32[32]{0:T(128)S(1)}, u32[32]{0:T(128)}, u32[]{:S(2)}) copy-start(u32[32]{0:T(128)} %constant.51) | copy-start | bytes 388
  36.7 104.9 %copy-start.4 = (f32[2]{0:T(128)S(1)}, f32[2]{0:T(128)}, u32[]{:S(2)}) copy-start(f32[2]{0:T(128)} %param.16) | copy-start | bytes 28
  36.7 104.9 %copy-start.3 = (f32[2,64]{1,0:T(2,128)S(1)}, f32[2,64]{1,0:T(2,128)}, u32[]{:S(2)}) copy-start(f32[2,64]{1,0:T(2,128)} %param.17) | copy-start | bytes 1540
Sparse Core Ops, SparseCore 0:
  59.0 81.7 all-reduce.2
where the time goes:
time: 151 us; the launch traced here: 149 us
  waiting for transfers between devices  80.7 us (53%)
  blocking collectives  23.4 us (15%)
  other arithmetic  20.8 us (14%)
  between operations  14.8 us (10%)
  local copies, waits for them, and re-layouts  6.92 us (5%)
  matrix products  2.57 us (2%)
    unnamed x2, waiting for transfers between devices  80.7 us
    all_gather x1, blocking collectives, body(): part_rows = lax.all_gather(factors, 'trade', axis=0, tiled=True)  23.4 us
    gather x1, other arithmetic, body(): trade_rows = netting_row[set_ids]  20 us
    gather x2, local copies, waits for them, and re-layouts, body(): trade_rows = netting_row[set_ids]  3.89 us
  transfers between devices with their start and end apart: 1, of which 1 were waited for; matrix products, arithmetic and copies ran while one was open for 0% of the time, Pallas kernels for 0%

commit v1 on v0

v1 whole, which is shorter than its diff:
```python
import jax
import jax.numpy as jnp
from jax import lax
from jax.sharding import PartitionSpec as P

F = 16
K = 32
DATES = 8
LAG = 2


def swap(x, bit, count):
    return lax.ppermute(x, "trade", [(i, i ^ bit) for i in range(count)])


def gather_paths(x, count):
    me = lax.axis_index("trade")
    bit = 1
    while bit < count:
        other = swap(x, bit, count)
        upper = (me & bit) != 0
        x = jnp.concatenate([jnp.where(upper, other, x), jnp.where(upper, x, other)], axis=0)
        bit *= 2
    return x


def bit_reversed(index, count):
    result = jnp.zeros_like(index)
    bit = 1
    while bit < count:
        result = result * 2 + (index & 1)
        index = index >> 1
        bit *= 2
    return result


def scatter_sums(x, count):
    bit = 1
    while bit < count:
        half = x.shape[0] // 2
        x = x[:half] + swap(x[half:], bit, count)
        bit *= 2
    return x


def body(
    factors,
    loadings,
    trade_coef,
    basis_size,
    set_ids,
    live_count,
    netting_row,
    threshold,
    margin_start,
    *,
    count,
):
    me = lax.axis_index("trade")
    own_rows = threshold.shape[0]
    set_total = netting_row.shape[0]
    slot_total = trade_coef.shape[0]

    coef_cube = trade_coef.reshape(slot_total, DATES, K)
    basis_index = jnp.arange(K, dtype=jnp.int32)
    keep_mask = basis_index[None, :] < basis_size[:, None]
    coef_used = jnp.where(keep_mask[:, None, :], coef_cube, jnp.zeros_like(coef_cube))

    place = jnp.arange(set_total, dtype=jnp.int32)
    row_at = (bit_reversed(place // own_rows, count) ^ me) * own_rows + place % own_rows
    set_at = jnp.sum(jnp.where(row_at[:, None] == netting_row[None, :], place[None, :], 0), axis=1)
    slot_index = jnp.arange(slot_total, dtype=jnp.int32)
    live = slot_index < live_count[0]
    onehot = ((set_ids[None, :] == set_at[:, None]) & live[None, :]).astype(jnp.bfloat16)

    paths = gather_paths(factors, count)
    path_total = paths.shape[0]
    factor_cube = paths.astype(jnp.float32).reshape(path_total, DATES, F)
    loaded = jnp.einsum("pdf,kf->pdk", factor_cube, loadings, precision=lax.Precision.HIGHEST)
    basis_table = jnp.tanh(loaded).astype(jnp.bfloat16)
    values = jnp.einsum("tdk,pdk->tdp", coef_used, basis_table, preferred_element_type=jnp.float32)
    values = values.astype(jnp.bfloat16).reshape(slot_total, DATES * path_total)
    netted = jnp.dot(onehot, values, preferred_element_type=jnp.float32)
    netted = scatter_sums(netted, count).reshape(own_rows, DATES, path_total)

    margin = jnp.maximum(netted[:, : DATES - LAG] - threshold[:, None, None], 0.0)
    held = jnp.broadcast_to(margin_start[:, None, :], (own_rows, LAG, path_total))
    collateral = jnp.concatenate([held, margin], axis=1)
    shortfall = jnp.sum(jnp.maximum(netted - collateral, 0.0), axis=2)
    return shortfall / path_total


def solution(mesh):
    count = mesh.shape["trade"]

    def local(*args):
        return body(*args, count=count)

    return jax.shard_map(
        local,
        mesh=mesh,
        in_specs=(
            P(("group", "trade"), None),
            P(),
            P(("group", "trade"), None),
            P(("group", "trade")),
            P(("group", "trade")),
            P(("group", "trade")),
            P("group"),
            P(("group", "trade")),
            P(("group", "trade"), None),
        ),
        out_specs=P(("group", "trade"), None),
        check_vma=False,
    )
```

time: 151 us -> 31.9 us (0.21); the launches traced: 149 us -> 31.7 us
  waiting for transfers between devices: 80.7 us -> 8.72 us
  blocking collectives: 23.4 us -> 0 us
  other arithmetic: 20.8 us -> 3.17 us
  starting transfers between devices: 0.01 us -> 15.6 us
  between operations: 14.8 us -> 0.78 us
  local copies, waits for them, and re-layouts: 6.92 us -> 1.74 us
    unnamed x2 -> x0, waiting for transfers between devices: 80.7 us -> none
    all_gather x1 -> x0, blocking collectives: 23.4 us -> none  [body(): part_rows = lax.all_gather(factors, 'trade', axis=0, tiled=True)]
    gather x1 -> x0, other arithmetic: 20 us -> none  [body(): trade_rows = netting_row[set_ids]]
    ppermute x0 -> x8, starting transfers between devices: none -> 15.6 us  [swap(): return lax.ppermute(x, 'trade', [(i, i ^ bit) for i in range(count)])]
    ppermute x0 -> x8, waiting for transfers between devices: none -> 8.72 us  [swap(): return lax.ppermute(x, 'trade', [(i, i ^ bit) for i in range(count)])]
    gather x2 -> x0, local copies, waits for them, and re-layouts: 3.89 us -> none  [body(): trade_rows = netting_row[set_ids]]
  transfers between devices with their start and end apart: 1 -> 8, of which waited for: 1 -> 8; matrix products, arithmetic and copies ran while one was open for 0% -> 10% of each run, Pallas kernels for 0% -> 0%
where the time goes in v1:
time: 31.9 us; the launch traced here: 31.7 us
  starting transfers between devices  15.6 us (49%)
  waiting for transfers between devices  8.72 us (27%)
  other arithmetic  3.17 us (10%)
  local copies, waits for them, and re-layouts  1.74 us (5%)
  matrix products  1.73 us (5%)
  between operations  0.78 us (2%)
    ppermute x8, starting transfers between devices, swap(): return lax.ppermute(x, 'trade', [(i, i ^ bit) for i in range(count)])  15.6 us
    ppermute x8, waiting for transfers between devices, swap(): return lax.ppermute(x, 'trade', [(i, i ^ bit) for i in range(count)])  8.72 us
    unnamed x9, local copies, waits for them, and re-layouts  1.5 us
    reduce_sum x1, other arithmetic, body(): jnp.sum(jnp.where(row_at[:, None] == netting_row[None, :], place[None, :]...  0.83 us
    dot_general x1, matrix products, body(): jnp.einsum('tdk,pdk->tdp', coef_used, basis_table, preferred_element_type...  0.75 us
    lt x1, other arithmetic, body(): keep_mask = basis_index[None, :] < basis_size[:, None]  0.74 us
    dot_general x1, matrix products, body(): netted = jnp.dot(onehot, values, preferred_element_type=jnp.float32)  0.72 us
    select_n x4, other arithmetic, gather_paths(): jnp.where(upper, other, x)  0.71 us
  transfers between devices with their start and end apart: 8, of which 8 were waited for; matrix products, arithmetic and copies ran while one was open for 10% of the time, Pallas kernels for 0%

profile of v1, /device:TPU:0, one launch (start us, length us, event | category | flops | bytes accessed | tf_op | source)
XLA Modules:
  0.0 31.7 jit_solution(9936633316875493093)
XLA Ops:
  0.0 0.5 %collective-permute-start = (bf16[4,128]{1,0:T(4,128)(2,1)}, bf16[4,128]{1,0:T(4,128)(2,1)S(1)}, u32[]{:S(2)}, u32[]{:S(2)}) collective-permute-start(bf16[4,128]{1,0:T(4,128)(2,1)} %param.9), channel_id=1, source_target_pairs={{0,1},{1,0},{2,3},{3,2},{4,5},{5,4},{6,7},{7,6},{8,9},{9,8},{10,11... | collective-permute-start | bytes 3080 | tf_op jit(solution)/shard_map/ppermute | solution.py:13
  0.5 0.7 %iota_compare_fusion = pred[2048,32]{0,1:T(8,128)(4,1)S(1)} fusion(s32[2048]{0:T(1024)} %param.12), kind=kLoop, calls=%fused_computation.6 | loop fusion | flops 65536 | bytes 73728 | tf_op jit(solution)/shard_map/lt | solution.py:66
  1.2 0.3 collective-permute-done
  1.5 0.7 %broadcast_select_fusion.7 = (bf16[4,128]{1,0:T(4,128)(2,1)S(1)}, bf16[4,128]{1,0:T(4,128)(2,1)S(1)}) fusion(bf16[4,128]{1,0:T(4,128)(2,1)S(1)} %collective-permute-done, bf16[4,128]{1,0:T(4,128)(2,1)} %param.9, pred[]{:T(512)S(6)} %ne.59), kind=kLoop, calls=%fused_computation.41 | loop fusion | flops 1024 | bytes 4097 | tf_op jit(solution)/shard_map/jit(_where)/select_n | solution.py:22
  2.2 2.9 %collective-permute-start.1 = (bf16[8,128]{1,0:T(8,128)(2,1)S(1)}, bf16[8,128]{1,0:T(8,128)(2,1)S(1)}, u32[]{:S(2)}, u32[]{:S(2)}) collective-permute-start(bf16[8,128]{1,0:T(8,128)(2,1)S(1)} %pad_maximum_fusion.3), channel_id=1, source_target_pairs={{0,2},{1,3},{2,0},{3,1},{4,6},{5,7},{6,4},{7,5},{8,10},{9,11},{10,... | collective-permute-start | bytes 6152 | tf_op jit(solution)/shard_map/ppermute | solution.py:13
  5.1 1.5 %collective-permute-done.1 = bf16[8,128]{1,0:T(8,128)(2,1)S(1)} collective-permute-done((bf16[8,128]{1,0:T(8,128)(2,1)S(1)}, bf16[8,128]{1,0:T(8,128)(2,1)S(1)}, u32[]{:S(2)}, u32[]{:S(2)}) %collective-permute-start.1) | collective-permute-done | bytes 2080 | tf_op jit(solution)/shard_map/ppermute | solution.py:13
  6.7 2.1 %collective-permute-start.2 = (bf16[16,128]{1,0:T(8,128)(2,1)S(1)}, bf16[16,128]{1,0:T(8,128)(2,1)S(1)}, u32[]{:S(2)}, u32[]{:S(2)}) collective-permute-start(bf16[16,128]{1,0:T(8,128)(2,1)S(1)} %pad_maximum_fusion.2), channel_id=1, source_target_pairs={{0,4},{1,5},{2,6},{3,7},{4,0},{5,1},{6,2},{7,3},{8,12},{9,13},{10,... | collective-permute-start | bytes 12296 | tf_op jit(solution)/shard_map/ppermute | solution.py:13
  8.8 0.8 %select_reduce_fusion = s32[32]{0:T(128)S(1)} fusion(s32[32]{0:T(128)} %param.15, s32[32]{0:T(128)S(1)} %fusion.14), kind=kLoop, calls=%fused_computation.18 | loop fusion | flops 3040 | bytes 384 | tf_op jit(solution)/shard_map/reduce_sum | solution.py:71
  10.4 0.1 copy.19
  10.5 3.1 %collective-permute-start.3 = (bf16[32,128]{0,1:T(8,128)(2,1)S(1)}, bf16[32,128]{0,1:T(8,128)(2,1)S(1)}, u32[]{:S(2)}, u32[]{:S(2)}) collective-permute-start(bf16[32,128]{0,1:T(8,128)(2,1)S(1)} %copy.19), channel_id=1, source_target_pairs={{0,8},{1,9},{2,10},{3,11},{4,12},{5,13},{6,14},{7,15},{8,0},{9,1},... | collective-permute-start | bytes 24584 | tf_op jit(solution)/shard_map/ppermute | solution.py:13
  13.6 1.5 %copy.22 = bf16[2048,256]{0,1:T(8,128)(2,1)S(1)} copy(bf16[2048,256]{1,0:T(8,128)(2,1)} %param.11) | data formatting | bytes 2097152 | tf_op args[2]
  15.1 0.4 %collective-permute-done.3 = bf16[32,128]{0,1:T(8,128)(2,1)S(1)} collective-permute-done((bf16[32,128]{0,1:T(8,128)(2,1)S(1)}, bf16[32,128]{0,1:T(8,128)(2,1)S(1)}, u32[]{:S(2)}, u32[]{:S(2)}) %collective-permute-start.3) | collective-permute-done | bytes 8224 | tf_op jit(solution)/shard_map/ppermute | solution.py:13
  15.6 0.3 fusion
  15.9 0.8 %convolution_convert_fusion = bf16[8,64,2048]{2,1,0:T(8,128)(2,1)S(1)} fusion(bf16[64,8,32]{0,2,1:T(8,128)(2,1)S(1)} %fusion, bf16[2048,8,32]{0,2,1:T(8,128)(2,1)S(1)} %bitcast.14, pred[2048,32]{0,1:T(8,128)(4,1)S(1)} %iota_compare_fusion), kind=kOutput, calls=%fused_computation | convolution fusion | flops 68681728 | bytes 3244032 | tf_op jit(solution)/shard_map/tdk,pdk->tdp/dot_general | solution.py:81
  16.7 0.7 %fusion.4 = f32[32,512]{1,0:T(8,128)S(1)} fusion(bf16[2048,512]{0,1:T(8,128)(2,1)S(1)} %bitcast.13, s32[2048]{0:T(1024)S(1)} %copy-done.1, s32[32]{0:T(128)S(1)} %select_reduce_fusion, pred[2048]{0:T(1024)(128)(4,1)S(1)} %iota_compare_fusion.1), kind=kOutput, calls=%fused_computation.7 | convolution fusion | flops 67239936 | bytes 2173056 | tf_op jit(solution)/shard_map/dot_general | solution.py:83
  17.5 1.2 %collective-permute-done.4 = f32[16,512]{1,0:T(8,128)S(1)} collective-permute-done((f32[16,512]{1,0:T(8,128)S(1)}, f32[16,512]{1,0:T(8,128)S(1)}, u32[]{:S(2)}, u32[]{:S(2)}) %collective-permute-start.4) | collective-permute-done | bytes 32800 | tf_op jit(solution)/shard_map/ppermute | solution.py:13
  18.7 1.9 %collective-permute-start.5 = (f32[8,512]{1,0:T(8,128)S(1)}, f32[8,512]{1,0:T(8,128)S(1)}, u32[]{:S(2)}, u32[]{:S(2)}) collective-permute-start(f32[8,512]{1,0:T(8,128)S(1)} %slice.39), channel_id=1, source_target_pairs={{0,2},{1,3},{2,0},{3,1},{4,6},{5,7},{6,4},{7,5},{8,10},{9,11},{10,... | collective-permute-start | bytes 49160 | tf_op jit(solution)/shard_map/ppermute | solution.py:13
  20.6 1.9 %collective-permute-done.5 = f32[8,512]{1,0:T(8,128)S(1)} collective-permute-done((f32[8,512]{1,0:T(8,128)S(1)}, f32[8,512]{1,0:T(8,128)S(1)}, u32[]{:S(2)}, u32[]{:S(2)}) %collective-permute-start.5) | collective-permute-done | bytes 16416 | tf_op jit(solution)/shard_map/ppermute | solution.py:13
  22.5 2.0 %collective-permute-start.6 = (f32[4,512]{1,0:T(4,128)S(1)}, f32[4,512]{1,0:T(4,128)S(1)}, u32[]{:S(2)}, u32[]{:S(2)}) collective-permute-start(f32[4,512]{1,0:T(4,128)S(1)} %slice.41), channel_id=1, source_target_pairs={{0,4},{1,5},{2,6},{3,7},{4,0},{5,1},{6,2},{7,3},{8,12},{9,13},{10,... | collective-permute-start | bytes 24584 | tf_op jit(solution)/shard_map/ppermute | solution.py:13
  24.5 1.7 %collective-permute-done.6 = f32[4,512]{1,0:T(4,128)S(1)} collective-permute-done((f32[4,512]{1,0:T(4,128)S(1)}, f32[4,512]{1,0:T(4,128)S(1)}, u32[]{:S(2)}, u32[]{:S(2)}) %collective-permute-start.6) | collective-permute-done | bytes 8224 | tf_op jit(solution)/shard_map/ppermute | solution.py:13
  26.3 3.0 %collective-permute-start.7 = (f32[2,512]{1,0:T(2,128)S(1)}, f32[2,512]{1,0:T(2,128)S(1)}, u32[]{:S(2)}, u32[]{:S(2)}) collective-permute-start(f32[2,512]{1,0:T(2,128)S(1)} %slice.43), channel_id=1, source_target_pairs={{0,8},{1,9},{2,10},{3,11},{4,12},{5,13},{6,14},{7,15},{8,0},{9,1},... | collective-permute-start | bytes 12296 | tf_op jit(solution)/shard_map/ppermute | solution.py:13
  29.3 1.6 %collective-permute-done.7 = f32[2,512]{1,0:T(2,128)S(1)} collective-permute-done((f32[2,512]{1,0:T(2,128)S(1)}, f32[2,512]{1,0:T(2,128)S(1)}, u32[]{:S(2)}, u32[]{:S(2)}) %collective-permute-start.7) | collective-permute-done | bytes 4128 | tf_op jit(solution)/shard_map/ppermute | solution.py:13
  31.0 0.1 fusion.12
  31.1 0.6 %broadcast_multiply_fusion = f32[2,8]{1,0:T(2,128)} fusion(f32[2,8]{1,0:T(2,128)S(1)} %fusion.12), kind=kLoop, calls=%fused_computation.43 | loop fusion | flops 16 | bytes 128 | tf_op jit(solution)/shard_map/div | solution.py:90
  (30 shorter events, 0.5 us)
Async XLA Ops:
  0.0 15.6 %copy-start = (f32[32,16]{0,1:T(8,128)S(1)}, f32[32,16]{0,1:T(8,128)}, u32[]{:S(2)}) copy-start(f32[32,16]{0,1:T(8,128)} %param.10) | copy-start | bytes 6148
  0.0 1.5 %collective-permute-start = (bf16[4,128]{1,0:T(4,128)(2,1)}, bf16[4,128]{1,0:T(4,128)(2,1)S(1)}, u32[]{:S(2)}, u32[]{:S(2)}) collective-permute-start(bf16[4,128]{1,0:T(4,128)(2,1)} %param.9), channel_id=1, source_target_pairs={{0,1},{1,0},{2,3},{3,2},{4,5},{5,4},{6,7},{7,6},{8,9},{9,8},{10,11... | collective-permute-start | bytes 3080 | tf_op jit(solution)/shard_map/ppermute | solution.py:13
  2.2 4.5 %collective-permute-start.1 = (bf16[8,128]{1,0:T(8,128)(2,1)S(1)}, bf16[8,128]{1,0:T(8,128)(2,1)S(1)}, u32[]{:S(2)}, u32[]{:S(2)}) collective-permute-start(bf16[8,128]{1,0:T(8,128)(2,1)S(1)} %pad_maximum_fusion.3), channel_id=1, source_target_pairs={{0,2},{1,3},{2,0},{3,1},{4,6},{5,7},{6,4},{7,5},{8,10},{9,11},{10,... | collective-permute-start | bytes 6152 | tf_op jit(solution)/shard_map/ppermute | solution.py:13
  6.7 3.7 %collective-permute-start.2 = (bf16[16,128]{1,0:T(8,128)(2,1)S(1)}, bf16[16,128]{1,0:T(8,128)(2,1)S(1)}, u32[]{:S(2)}, u32[]{:S(2)}) collective-permute-start(bf16[16,128]{1,0:T(8,128)(2,1)S(1)} %pad_maximum_fusion.2), channel_id=1, source_target_pairs={{0,4},{1,5},{2,6},{3,7},{4,0},{5,1},{6,2},{7,3},{8,12},{9,13},{10,... | collective-permute-start | bytes 12296 | tf_op jit(solution)/shard_map/ppermute | solution.py:13
  10.5 5.0 %collective-permute-start.3 = (bf16[32,128]{0,1:T(8,128)(2,1)S(1)}, bf16[32,128]{0,1:T(8,128)(2,1)S(1)}, u32[]{:S(2)}, u32[]{:S(2)}) collective-permute-start(bf16[32,128]{0,1:T(8,128)(2,1)S(1)} %copy.19), channel_id=1, source_target_pairs={{0,8},{1,9},{2,10},{3,11},{4,12},{5,13},{6,14},{7,15},{8,0},{9,1},... | collective-permute-start | bytes 24584 | tf_op jit(solution)/shard_map/ppermute | solution.py:13
  15.1 1.6 %copy-start.1 = (s32[2048]{0:T(1024)S(1)}, s32[2048]{0:T(1024)}, u32[]{:S(2)}) copy-start(s32[2048]{0:T(1024)} %param.13) | copy-start | bytes 24580
  15.9 15.0 %copy-start.3 = (f32[2]{0:T(128)S(1)}, f32[2]{0:T(128)}, u32[]{:S(2)}) copy-start(f32[2]{0:T(128)} %param.16) | copy-start | bytes 28
  15.9 15.1 %copy-start.2 = (f32[2,64]{1,0:T(2,128)S(1)}, f32[2,64]{1,0:T(2,128)}, u32[]{:S(2)}) copy-start(f32[2,64]{1,0:T(2,128)} %param.17) | copy-start | bytes 1540
  17.4 1.3 %collective-permute-start.4 = (f32[16,512]{1,0:T(8,128)S(1)}, f32[16,512]{1,0:T(8,128)S(1)}, u32[]{:S(2)}, u32[]{:S(2)}) collective-permute-start(f32[16,512]{1,0:T(8,128)S(1)} %slice.37), channel_id=1, source_target_pairs={{0,1},{1,0},{2,3},{3,2},{4,5},{5,4},{6,7},{7,6},{8,9},{9,8},{10,11... | collective-permute-start | bytes 98312 | tf_op jit(solution)/shard_map/ppermute | solution.py:13
  18.7 3.8 %collective-permute-start.5 = (f32[8,512]{1,0:T(8,128)S(1)}, f32[8,512]{1,0:T(8,128)S(1)}, u32[]{:S(2)}, u32[]{:S(2)}) collective-permute-start(f32[8,512]{1,0:T(8,128)S(1)} %slice.39), channel_id=1, source_target_pairs={{0,2},{1,3},{2,0},{3,1},{4,6},{5,7},{6,4},{7,5},{8,10},{9,11},{10,... | collective-permute-start | bytes 49160 | tf_op jit(solution)/shard_map/ppermute | solution.py:13
  22.5 3.7 %collective-permute-start.6 = (f32[4,512]{1,0:T(4,128)S(1)}, f32[4,512]{1,0:T(4,128)S(1)}, u32[]{:S(2)}, u32[]{:S(2)}) collective-permute-start(f32[4,512]{1,0:T(4,128)S(1)} %slice.41), channel_id=1, source_target_pairs={{0,4},{1,5},{2,6},{3,7},{4,0},{5,1},{6,2},{7,3},{8,12},{9,13},{10,... | collective-permute-start | bytes 24584 | tf_op jit(solution)/shard_map/ppermute | solution.py:13
  26.3 4.6 %collective-permute-start.7 = (f32[2,512]{1,0:T(2,128)S(1)}, f32[2,512]{1,0:T(2,128)S(1)}, u32[]{:S(2)}, u32[]{:S(2)}) collective-permute-start(f32[2,512]{1,0:T(2,128)S(1)} %slice.43), channel_id=1, source_target_pairs={{0,8},{1,9},{2,10},{3,11},{4,12},{5,13},{6,14},{7,15},{8,0},{9,1},... | collective-permute-start | bytes 12296 | tf_op jit(solution)/shard_map/ppermute | solution.py:13

commit v2 on v1

--- a/solution.py
+++ b/solution.py
@@ -10,7 +10,7 @@
 
 
 def swap(x, bit, count):
-    return lax.ppermute(x, "trade", [(i, i ^ bit) for i in range(count)])
+    return lax.ppermute(x, "trade", [(i, i ^ (bit | 1)) for i in range(count)])
 
 
 def gather_paths(x, count):
@@ -24,13 +24,14 @@
     return x
 
 
-def bit_reversed(index, count):
+def offsets(index, count):
     result = jnp.zeros_like(index)
     bit = 1
+    top = count // 2
     while bit < count:
-        result = result * 2 + (index & 1)
-        index = index >> 1
+        result = result ^ jnp.where((index & top) != 0, bit | 1, 0)
         bit *= 2
+        top //= 2
     return result
 
 
@@ -67,7 +68,7 @@
     coef_used = jnp.where(keep_mask[:, None, :], coef_cube, jnp.zeros_like(coef_cube))
 
     place = jnp.arange(set_total, dtype=jnp.int32)
-    row_at = (bit_reversed(place // own_rows, count) ^ me) * own_rows + place % own_rows
+    row_at = (offsets(place // own_rows, count) ^ me) * own_rows + place % own_rows
     set_at = jnp.sum(jnp.where(row_at[:, None] == netting_row[None, :], place[None, :], 0), axis=1)
     slot_index = jnp.arange(slot_total, dtype=jnp.int32)
     live = slot_index < live_count[0]

time: 31.9 us -> 29.2 us (0.915)
  waiting for transfers between devices: 8.72 us -> 7.1 us
  starting transfers between devices: 15.6 us -> 14.5 us
    ppermute x8, waiting for transfers between devices: 8.72 us -> 7.1 us  [swap(): return lax.ppermute(x, 'trade', [(i, i ^ (bit | 1)) for i in range(count)])]
    ppermute x8, starting transfers between devices: 15.6 us -> 14.5 us  [swap(): return lax.ppermute(x, 'trade', [(i, i ^ (bit | 1)) for i in range(count)])]
  transfers between devices with their start and end apart: 8 -> 8, of which waited for: 8 -> 7; matrix products, arithmetic and copies ran while one was open for 10% -> 11% of each run, Pallas kernels for 0% -> 0%
where the time goes in v2:
time: 29.2 us; the launch traced here: 29 us
  starting transfers between devices  14.5 us (50%)
  waiting for transfers between devices  7.1 us (24%)
  other arithmetic  3.16 us (11%)
  local copies, waits for them, and re-layouts  1.74 us (6%)
  matrix products  1.73 us (6%)
  between operations  0.78 us (3%)
    ppermute x8, starting transfers between devices, swap(): return lax.ppermute(x, 'trade', [(i, i ^ (bit | 1)) for i in range(count)])  14.5 us
    ppermute x8, waiting for transfers between devices, swap(): return lax.ppermute(x, 'trade', [(i, i ^ (bit | 1)) for i in range(count)])  7.1 us
    unnamed x9, local copies, waits for them, and re-layouts  1.5 us
    reduce_sum x1, other arithmetic, body(): jnp.sum(jnp.where(row_at[:, None] == netting_row[None, :], place[None, :]...  0.83 us
    dot_general x1, matrix products, body(): jnp.einsum('tdk,pdk->tdp', coef_used, basis_table, preferred_element_type...  0.75 us
    lt x1, other arithmetic, body(): keep_mask = basis_index[None, :] < basis_size[:, None]  0.74 us
    dot_general x1, matrix products, body(): netted = jnp.dot(onehot, values, preferred_element_type=jnp.float32)  0.72 us
    select_n x4, other arithmetic, gather_paths(): jnp.where(upper, other, x)  0.71 us
  transfers between devices with their start and end apart: 8, of which 7 were waited for; matrix products, arithmetic and copies ran while one was open for 11% of the time, Pallas kernels for 0%

profile of v2, /device:TPU:0, one launch (start us, length us, event | category | flops | bytes accessed | tf_op | source)
XLA Modules:
  0.0 29.0 jit_solution(8082133979244042036)
XLA Ops:
  0.0 0.5 %collective-permute-start = (bf16[4,128]{1,0:T(4,128)(2,1)}, bf16[4,128]{1,0:T(4,128)(2,1)S(1)}, u32[]{:S(2)}, u32[]{:S(2)}) collective-permute-start(bf16[4,128]{1,0:T(4,128)(2,1)} %param.9), channel_id=1, source_target_pairs={{0,1},{1,0},{2,3},{3,2},{4,5},{5,4},{6,7},{7,6},{8,9},{9,8},{10,11... | collective-permute-start | bytes 3080 | tf_op jit(solution)/shard_map/ppermute | solution.py:13
  0.5 0.7 %iota_compare_fusion = pred[2048,32]{0,1:T(8,128)(4,1)S(1)} fusion(s32[2048]{0:T(1024)} %param.12), kind=kLoop, calls=%fused_computation.6 | loop fusion | flops 65536 | bytes 73728 | tf_op jit(solution)/shard_map/lt | solution.py:67
  1.2 0.3 collective-permute-done
  1.5 0.7 %broadcast_select_fusion.7 = (bf16[4,128]{1,0:T(4,128)(2,1)S(1)}, bf16[4,128]{1,0:T(4,128)(2,1)S(1)}) fusion(bf16[4,128]{1,0:T(4,128)(2,1)S(1)} %collective-permute-done, bf16[4,128]{1,0:T(4,128)(2,1)} %param.9, pred[]{:T(512)S(6)} %ne.91), kind=kLoop, calls=%fused_computation.45 | loop fusion | flops 1024 | bytes 4097 | tf_op jit(solution)/shard_map/jit(_where)/select_n | solution.py:22
  2.2 2.7 %collective-permute-start.1 = (bf16[8,128]{1,0:T(8,128)(2,1)S(1)}, bf16[8,128]{1,0:T(8,128)(2,1)S(1)}, u32[]{:S(2)}, u32[]{:S(2)}) collective-permute-start(bf16[8,128]{1,0:T(8,128)(2,1)S(1)} %pad_maximum_fusion.3), channel_id=1, source_target_pairs={{0,3},{1,2},{2,1},{3,0},{4,7},{5,6},{6,5},{7,4},{8,11},{9,10},{10,... | collective-permute-start | bytes 6152 | tf_op jit(solution)/shard_map/ppermute | solution.py:13
  4.9 1.3 %collective-permute-done.1 = bf16[8,128]{1,0:T(8,128)(2,1)S(1)} collective-permute-done((bf16[8,128]{1,0:T(8,128)(2,1)S(1)}, bf16[8,128]{1,0:T(8,128)(2,1)S(1)}, u32[]{:S(2)}, u32[]{:S(2)}) %collective-permute-start.1) | collective-permute-done | bytes 2080 | tf_op jit(solution)/shard_map/ppermute | solution.py:13
  6.2 1.8 %collective-permute-start.2 = (bf16[16,128]{1,0:T(8,128)(2,1)S(1)}, bf16[16,128]{1,0:T(8,128)(2,1)S(1)}, u32[]{:S(2)}, u32[]{:S(2)}) collective-permute-start(bf16[16,128]{1,0:T(8,128)(2,1)S(1)} %pad_maximum_fusion.2), channel_id=1, source_target_pairs={{0,5},{1,4},{2,7},{3,6},{4,1},{5,0},{6,3},{7,2},{8,13},{9,12},{10,... | collective-permute-start | bytes 12296 | tf_op jit(solution)/shard_map/ppermute | solution.py:13
  8.0 0.8 %select_reduce_fusion = s32[32]{0:T(128)S(1)} fusion(s32[32]{0:T(128)} %param.15, s32[32]{0:T(128)S(1)} %fusion.14), kind=kLoop, calls=%fused_computation.18 | loop fusion | flops 3040 | bytes 384 | tf_op jit(solution)/shard_map/reduce_sum | solution.py:72
  9.6 0.1 copy.19
  9.7 2.6 %collective-permute-start.3 = (bf16[32,128]{0,1:T(8,128)(2,1)S(1)}, bf16[32,128]{0,1:T(8,128)(2,1)S(1)}, u32[]{:S(2)}, u32[]{:S(2)}) collective-permute-start(bf16[32,128]{0,1:T(8,128)(2,1)S(1)} %copy.19), channel_id=1, source_target_pairs={{0,9},{1,8},{2,11},{3,10},{4,13},{5,12},{6,15},{7,14},{8,1},{9,0},... | collective-permute-start | bytes 24584 | tf_op jit(solution)/shard_map/ppermute | solution.py:13
  12.3 1.5 %copy.22 = bf16[2048,256]{0,1:T(8,128)(2,1)S(1)} copy(bf16[2048,256]{1,0:T(8,128)(2,1)} %param.11) | data formatting | bytes 2097152 | tf_op args[2]
  13.8 0.2 collective-permute-done.3
  14.1 0.3 fusion
  14.4 0.8 %convolution_convert_fusion = bf16[8,64,2048]{2,1,0:T(8,128)(2,1)S(1)} fusion(bf16[64,8,32]{0,2,1:T(8,128)(2,1)S(1)} %fusion, bf16[2048,8,32]{0,2,1:T(8,128)(2,1)S(1)} %bitcast.14, pred[2048,32]{0,1:T(8,128)(4,1)S(1)} %iota_compare_fusion), kind=kOutput, calls=%fused_computation | convolution fusion | flops 68681728 | bytes 3244032 | tf_op jit(solution)/shard_map/tdk,pdk->tdp/dot_general | solution.py:82
  15.2 0.7 %fusion.4 = f32[32,512]{1,0:T(8,128)S(1)} fusion(bf16[2048,512]{0,1:T(8,128)(2,1)S(1)} %bitcast.13, s32[2048]{0:T(1024)S(1)} %copy-done.1, s32[32]{0:T(128)S(1)} %select_reduce_fusion, pred[2048]{0:T(1024)(128)(4,1)S(1)} %iota_compare_fusion.1), kind=kOutput, calls=%fused_computation.7 | convolution fusion | flops 67239936 | bytes 2173056 | tf_op jit(solution)/shard_map/dot_general | solution.py:84
  15.9 0.4 %collective-permute-start.4 = (f32[16,512]{1,0:T(8,128)S(1)}, f32[16,512]{1,0:T(8,128)S(1)}, u32[]{:S(2)}, u32[]{:S(2)}) collective-permute-start(f32[16,512]{1,0:T(8,128)S(1)} %slice.37), channel_id=1, source_target_pairs={{0,1},{1,0},{2,3},{3,2},{4,5},{5,4},{6,7},{7,6},{8,9},{9,8},{10,11... | collective-permute-start | bytes 98312 | tf_op jit(solution)/shard_map/ppermute | solution.py:13
  16.3 0.9 %collective-permute-done.4 = f32[16,512]{1,0:T(8,128)S(1)} collective-permute-done((f32[16,512]{1,0:T(8,128)S(1)}, f32[16,512]{1,0:T(8,128)S(1)}, u32[]{:S(2)}, u32[]{:S(2)}) %collective-permute-start.4) | collective-permute-done | bytes 32800 | tf_op jit(solution)/shard_map/ppermute | solution.py:13
  17.2 1.5 %collective-permute-start.5 = (f32[8,512]{1,0:T(8,128)S(1)}, f32[8,512]{1,0:T(8,128)S(1)}, u32[]{:S(2)}, u32[]{:S(2)}) collective-permute-start(f32[8,512]{1,0:T(8,128)S(1)} %slice.39), channel_id=1, source_target_pairs={{0,3},{1,2},{2,1},{3,0},{4,7},{5,6},{6,5},{7,4},{8,11},{9,10},{10,... | collective-permute-start | bytes 49160 | tf_op jit(solution)/shard_map/ppermute | solution.py:13
  18.7 1.7 %collective-permute-done.5 = f32[8,512]{1,0:T(8,128)S(1)} collective-permute-done((f32[8,512]{1,0:T(8,128)S(1)}, f32[8,512]{1,0:T(8,128)S(1)}, u32[]{:S(2)}, u32[]{:S(2)}) %collective-permute-start.5) | collective-permute-done | bytes 16416 | tf_op jit(solution)/shard_map/ppermute | solution.py:13
  20.4 1.7 %collective-permute-start.6 = (f32[4,512]{1,0:T(4,128)S(1)}, f32[4,512]{1,0:T(4,128)S(1)}, u32[]{:S(2)}, u32[]{:S(2)}) collective-permute-start(f32[4,512]{1,0:T(4,128)S(1)} %slice.41), channel_id=1, source_target_pairs={{0,5},{1,4},{2,7},{3,6},{4,1},{5,0},{6,3},{7,2},{8,13},{9,12},{10,... | collective-permute-start | bytes 24584 | tf_op jit(solution)/shard_map/ppermute | solution.py:13
  22.2 1.4 %collective-permute-done.6 = f32[4,512]{1,0:T(4,128)S(1)} collective-permute-done((f32[4,512]{1,0:T(4,128)S(1)}, f32[4,512]{1,0:T(4,128)S(1)}, u32[]{:S(2)}, u32[]{:S(2)}) %collective-permute-start.6) | collective-permute-done | bytes 8224 | tf_op jit(solution)/shard_map/ppermute | solution.py:13
  23.6 3.3 %collective-permute-start.7 = (f32[2,512]{1,0:T(2,128)S(1)}, f32[2,512]{1,0:T(2,128)S(1)}, u32[]{:S(2)}, u32[]{:S(2)}) collective-permute-start(f32[2,512]{1,0:T(2,128)S(1)} %slice.43), channel_id=1, source_target_pairs={{0,9},{1,8},{2,11},{3,10},{4,13},{5,12},{6,15},{7,14},{8,1},{9,0},... | collective-permute-start | bytes 12296 | tf_op jit(solution)/shard_map/ppermute | solution.py:13
  26.8 1.3 %collective-permute-done.7 = f32[2,512]{1,0:T(2,128)S(1)} collective-permute-done((f32[2,512]{1,0:T(2,128)S(1)}, f32[2,512]{1,0:T(2,128)S(1)}, u32[]{:S(2)}, u32[]{:S(2)}) %collective-permute-start.7) | collective-permute-done | bytes 4128 | tf_op jit(solution)/shard_map/ppermute | solution.py:13
  28.4 0.6 %broadcast_multiply_fusion = f32[2,8]{1,0:T(2,128)} fusion(f32[2,8]{1,0:T(2,128)S(1)} %fusion.12), kind=kLoop, calls=%fused_computation.50 | loop fusion | flops 16 | bytes 128 | tf_op jit(solution)/shard_map/div | solution.py:91
  (30 shorter events, 0.5 us)
Async XLA Ops:
  0.0 14.1 %copy-start = (f32[32,16]{0,1:T(8,128)S(1)}, f32[32,16]{0,1:T(8,128)}, u32[]{:S(2)}) copy-start(f32[32,16]{0,1:T(8,128)} %param.10) | copy-start | bytes 6148
  0.0 1.5 %collective-permute-start = (bf16[4,128]{1,0:T(4,128)(2,1)}, bf16[4,128]{1,0:T(4,128)(2,1)S(1)}, u32[]{:S(2)}, u32[]{:S(2)}) collective-permute-start(bf16[4,128]{1,0:T(4,128)(2,1)} %param.9), channel_id=1, source_target_pairs={{0,1},{1,0},{2,3},{3,2},{4,5},{5,4},{6,7},{7,6},{8,9},{9,8},{10,11... | collective-permute-start | bytes 3080 | tf_op jit(solution)/shard_map/ppermute | solution.py:13
  2.2 4.0 %collective-permute-start.1 = (bf16[8,128]{1,0:T(8,128)(2,1)S(1)}, bf16[8,128]{1,0:T(8,128)(2,1)S(1)}, u32[]{:S(2)}, u32[]{:S(2)}) collective-permute-start(bf16[8,128]{1,0:T(8,128)(2,1)S(1)} %pad_maximum_fusion.3), channel_id=1, source_target_pairs={{0,3},{1,2},{2,1},{3,0},{4,7},{5,6},{6,5},{7,4},{8,11},{9,10},{10,... | collective-permute-start | bytes 6152 | tf_op jit(solution)/shard_map/ppermute | solution.py:13
  6.2 3.3 %collective-permute-start.2 = (bf16[16,128]{1,0:T(8,128)(2,1)S(1)}, bf16[16,128]{1,0:T(8,128)(2,1)S(1)}, u32[]{:S(2)}, u32[]{:S(2)}) collective-permute-start(bf16[16,128]{1,0:T(8,128)(2,1)S(1)} %pad_maximum_fusion.2), channel_id=1, source_target_pairs={{0,5},{1,4},{2,7},{3,6},{4,1},{5,0},{6,3},{7,2},{8,13},{9,12},{10,... | collective-permute-start | bytes 12296 | tf_op jit(solution)/shard_map/ppermute | solution.py:13
  9.7 4.3 %collective-permute-start.3 = (bf16[32,128]{0,1:T(8,128)(2,1)S(1)}, bf16[32,128]{0,1:T(8,128)(2,1)S(1)}, u32[]{:S(2)}, u32[]{:S(2)}) collective-permute-start(bf16[32,128]{0,1:T(8,128)(2,1)S(1)} %copy.19), channel_id=1, source_target_pairs={{0,9},{1,8},{2,11},{3,10},{4,13},{5,12},{6,15},{7,14},{8,1},{9,0},... | collective-permute-start | bytes 24584 | tf_op jit(solution)/shard_map/ppermute | solution.py:13
  13.8 1.4 %copy-start.1 = (s32[2048]{0:T(1024)S(1)}, s32[2048]{0:T(1024)}, u32[]{:S(2)}) copy-start(s32[2048]{0:T(1024)} %param.13) | copy-start | bytes 24580
  14.4 13.9 %copy-start.3 = (f32[2]{0:T(128)S(1)}, f32[2]{0:T(128)}, u32[]{:S(2)}) copy-start(f32[2]{0:T(128)} %param.16) | copy-start | bytes 28
  14.4 14.0 %copy-start.2 = (f32[2,64]{1,0:T(2,128)S(1)}, f32[2,64]{1,0:T(2,128)}, u32[]{:S(2)}) copy-start(f32[2,64]{1,0:T(2,128)} %param.17) | copy-start | bytes 1540
  15.9 1.3 %collective-permute-start.4 = (f32[16,512]{1,0:T(8,128)S(1)}, f32[16,512]{1,0:T(8,128)S(1)}, u32[]{:S(2)}, u32[]{:S(2)}) collective-permute-start(f32[16,512]{1,0:T(8,128)S(1)} %slice.37), channel_id=1, source_target_pairs={{0,1},{1,0},{2,3},{3,2},{4,5},{5,4},{6,7},{7,6},{8,9},{9,8},{10,11... | collective-permute-start | bytes 98312 | tf_op jit(solution)/shard_map/ppermute | solution.py:13
  17.2 3.2 %collective-permute-start.5 = (f32[8,512]{1,0:T(8,128)S(1)}, f32[8,512]{1,0:T(8,128)S(1)}, u32[]{:S(2)}, u32[]{:S(2)}) collective-permute-start(f32[8,512]{1,0:T(8,128)S(1)} %slice.39), channel_id=1, source_target_pairs={{0,3},{1,2},{2,1},{3,0},{4,7},{5,6},{6,5},{7,4},{8,11},{9,10},{10,... | collective-permute-start | bytes 49160 | tf_op jit(solution)/shard_map/ppermute | solution.py:13
  20.4 3.1 %collective-permute-start.6 = (f32[4,512]{1,0:T(4,128)S(1)}, f32[4,512]{1,0:T(4,128)S(1)}, u32[]{:S(2)}, u32[]{:S(2)}) collective-permute-start(f32[4,512]{1,0:T(4,128)S(1)} %slice.41), channel_id=1, source_target_pairs={{0,5},{1,4},{2,7},{3,6},{4,1},{5,0},{6,3},{7,2},{8,13},{9,12},{10,... | collective-permute-start | bytes 24584 | tf_op jit(solution)/shard_map/ppermute | solution.py:13
  23.6 4.6 %collective-permute-start.7 = (f32[2,512]{1,0:T(2,128)S(1)}, f32[2,512]{1,0:T(2,128)S(1)}, u32[]{:S(2)}, u32[]{:S(2)}) collective-permute-start(f32[2,512]{1,0:T(2,128)S(1)} %slice.43), channel_id=1, source_target_pairs={{0,9},{1,8},{2,11},{3,10},{4,13},{5,12},{6,15},{7,14},{8,1},{9,0},... | collective-permute-start | bytes 12296 | tf_op jit(solution)/shard_map/ppermute | solution.py:13

commit v3 on v2

v3 whole, which is shorter than its diff:
```python
import jax
import jax.numpy as jnp
from jax import lax
from jax.experimental import pallas as pl
from jax.experimental.pallas import tpu as pltpu
from jax.sharding import PartitionSpec as P

F = 16
K = 32
DATES = 8
LAG = 2
LANES = 128
PATH_BLOCK = 32
SLOT_BLOCK = 1024
VMEM = pl.BlockSpec(memory_space=pltpu.VMEM)
SMEM = pl.BlockSpec(memory_space=pltpu.SMEM)


def call(kernel, outs, specs, flops, args):
    sizes = [a.size * a.dtype.itemsize for a in (*args, *outs)]
    return pl.pallas_call(
        kernel,
        out_shape=outs,
        in_specs=specs,
        out_specs=[VMEM] * len(outs),
        compiler_params=pltpu.CompilerParams(vmem_limit_bytes=24 * 2**20),
        cost_estimate=pl.CostEstimate(flops=flops, bytes_accessed=sum(sizes), transcendentals=0),
    )(*args)


def swap(x, bit, count):
    return lax.ppermute(x, "trade", [(i, i ^ (bit | 1)) for i in range(count)])


def join(own, other, bit):
    upper = (lax.axis_index("trade") & bit) != 0
    return jnp.concatenate([jnp.where(upper, other, own), jnp.where(upper, own, other)], axis=0)


def offsets(index, count):
    result = jnp.zeros_like(index)
    bit = 1
    top = count // 2
    while bit < count:
        result = result ^ jnp.where((index & top) != 0, bit | 1, 0)
        bit *= 2
        top //= 2
    return result


def scatter_sums(kept, sent, count):
    bit = 1
    while bit < count // 2:
        x = kept + swap(sent, bit, count)
        half = x.shape[0] // 2
        kept, sent = x[:half], x[half:]
        bit *= 2
    near = sent.shape[1] // 2
    return kept + swap(jnp.concatenate([sent[:, near:], sent[:, :near]], axis=1), bit, count)


def copy_kernel(factors_ref, own_ref):
    own_ref[...] = factors_ref[...]


def rows_kernel(
    count, me_ref, live_ref, limit_ref, loadings_ref, ids_ref, owner_ref, limits_ref, split_ref, onehot_ref
):
    own_rows = limits_ref.shape[0]
    for r in range(own_rows):
        limits_ref[r : r + 1, :] = jnp.full((1, LANES), limit_ref[r])
    set_total = owner_ref.shape[1]
    place = lax.broadcasted_iota(jnp.int32, (set_total, 1), 0)
    block = lax.shift_right_logical(place, own_rows.bit_length() - 1)
    row_at = (offsets(block, count) ^ me_ref[0]) * own_rows + (place & (own_rows - 1))
    sets = lax.broadcasted_iota(jnp.int32, (set_total, set_total), 1)
    set_at = jnp.sum(jnp.where(row_at == owner_ref[...], sets, 0), axis=1, keepdims=True)
    lane = lax.broadcasted_iota(jnp.int32, (1, LANES), 1)
    live = live_ref[0]
    for c in range(ids_ref.shape[0]):
        ids = jnp.where(lane + c * LANES < live, ids_ref[c : c + 1, :], -1)
        hit = jnp.where(ids == set_at, 1.0, 0.0)
        onehot_ref[:, c * LANES : (c + 1) * LANES] = hit.astype(jnp.bfloat16)
    tall = jnp.concatenate([loadings_ref[...].T] * DATES, axis=0)
    wide = jnp.concatenate([tall] * DATES, axis=1)
    row = lax.broadcasted_iota(jnp.int32, wide.shape, 0) // K
    column = lax.broadcasted_iota(jnp.int32, wide.shape, 1) // F
    rest = jnp.where(row == column, wide, 0.0)
    for i in range(3):
        part = rest.astype(jnp.bfloat16)
        split_ref[i] = part
        rest = rest - part.astype(jnp.float32)


def coef_kernel(coef_ref, size_ref, used_ref):
    sizes = size_ref[...].astype(jnp.float32).T
    width = coef_ref.shape[1]
    basis = (lax.broadcasted_iota(jnp.int32, (1, width), 1) & (K - 1)).astype(jnp.float32)
    for c in range(size_ref.shape[0]):
        rows = slice(c * LANES, (c + 1) * LANES)
        coef = coef_ref[rows, :].astype(jnp.float32)
        used_ref[rows, :] = jnp.where(basis < sizes[:, c : c + 1], coef, 0.0).astype(jnp.bfloat16)


def net_block(paths, split_ref, used_ref, onehot_ref):
    total = paths.shape[0]
    tiled = jnp.concatenate([paths] * DATES, axis=0)
    contract = (((1,), (1,)), ((), ()))
    loaded = sum(
        lax.dot_general(split_ref[i], tiled, contract, preferred_element_type=jnp.float32) for i in (2, 1, 0)
    )
    row = lax.broadcasted_iota(jnp.int32, loaded.shape, 0) // K
    column = lax.broadcasted_iota(jnp.int32, loaded.shape, 1) // total
    table = jnp.where(row == column, jnp.tanh(loaded), 0.0).astype(jnp.bfloat16)
    slots = used_ref.shape[0]
    step = min(SLOT_BLOCK, slots)
    result = jnp.zeros((onehot_ref.shape[0], DATES * total), jnp.float32)
    for at in range(0, slots, step):
        values = jnp.dot(used_ref[at : at + step, :], table, preferred_element_type=jnp.float32)
        values = values.astype(jnp.bfloat16)
        result = result + jnp.dot(onehot_ref[:, at : at + step], values, preferred_element_type=jnp.float32)
    return result


def near_kernel(paths_ref, split_ref, used_ref, onehot_ref, net_ref):
    block = min(PATH_BLOCK, paths_ref.shape[0])
    for b in range(paths_ref.shape[0] // block):
        net = net_block(paths_ref[b * block : (b + 1) * block, :], split_ref, used_ref, onehot_ref)
        net_ref[:, b * DATES * block : (b + 1) * DATES * block] = net


def far_kernel(paths_ref, split_ref, used_ref, onehot_ref, near_ref, kept_ref, sent_ref):
    half = kept_ref.shape[0]
    width = near_ref.shape[1]
    kept_ref[:, :width] = near_ref[:half, :]
    sent_ref[:, :width] = near_ref[half:, :]
    block = min(PATH_BLOCK, paths_ref.shape[0])
    for b in range(paths_ref.shape[0] // block):
        net = net_block(paths_ref[b * block : (b + 1) * block, :], split_ref, used_ref, onehot_ref)
        at = slice(width + b * DATES * block, width + (b + 1) * DATES * block)
        sent_ref[:, at] = net[half:, :]
        kept_ref[:, at] = net[:half, :]


def body(
    factors,
    loadings,
    trade_coef,
    basis_size,
    set_ids,
    live_count,
    netting_row,
    threshold,
    margin_start,
    *,
    count,
):
    me = lax.axis_index("trade")
    own_rows = threshold.shape[0]
    set_total = netting_row.shape[0]
    slot_total, width = trade_coef.shape
    shape = jax.ShapeDtypeStruct
    f32, bf16 = jnp.float32, jnp.bfloat16

    (own,) = call(copy_kernel, [shape(factors.shape, bf16)], [VMEM], 10**6, (factors,))
    near = join(own, swap(factors, 1, count), 1)
    sizes = basis_size.reshape(-1, LANES)
    sizes, near = lax.optimization_barrier((sizes, near))
    (used,) = call(coef_kernel, [shape(trade_coef.shape, bf16)], [VMEM, VMEM], 10**8, (trade_coef, sizes))
    near = join(near, swap(near, 2, count), 2)
    ids = set_ids.reshape(-1, LANES)
    ids, near = lax.optimization_barrier((ids, near))
    limits, split, onehot = call(
        lambda *refs: rows_kernel(count, *refs),
        [shape((own_rows, LANES), f32), shape((3, DATES * K, DATES * F), bf16), shape((set_total, slot_total), bf16)],
        [SMEM, SMEM, SMEM, VMEM, VMEM, VMEM],
        10**8,
        (me.astype(jnp.int32).reshape(1), live_count, threshold, loadings.T, ids, netting_row.reshape(1, -1)),
    )
    bit = 4
    while bit < count // 2:
        near = join(near, swap(near, bit, count), bit)
        bit *= 2
    far = swap(near, bit, count)
    side_total = near.shape[0]
    columns = DATES * side_total
    work = 2 * columns * slot_total * (width + set_total)
    (near_net,) = call(
        near_kernel, [shape((set_total, columns), f32)], [VMEM] * 4, work, (near, split, used, onehot)
    )
    kept, sent = call(
        far_kernel,
        [shape((set_total // 2, 2 * columns), f32)] * 2,
        [VMEM] * 5,
        work,
        (far, split, used, onehot, near_net),
    )
    netted = scatter_sums(kept, sent, count)

    upper = (me & (count // 2)) != 0
    flipped = jnp.concatenate([margin_start[:, side_total:], margin_start[:, :side_total]], axis=1)
    start = jnp.where(upper, flipped, margin_start)

    block = min(PATH_BLOCK, side_total)
    netted = netted.reshape(own_rows, -1, DATES, block)
    start = start.reshape(own_rows, -1, 1, block)
    margin = jnp.maximum(netted[:, :, : DATES - LAG] - limits[:, :1, None, None], 0.0)
    held = jnp.broadcast_to(start, (own_rows, start.shape[1], LAG, block))
    collateral = jnp.concatenate([held, margin], axis=2)
    shortfall = jnp.sum(jnp.maximum(netted - collateral, 0.0), axis=(1, 3))
    return shortfall / (2 * side_total)


def solution(mesh):
    count = mesh.shape["trade"]

    def local(*args):
        return body(*args, count=count)

    return jax.shard_map(
        local,
        mesh=mesh,
        in_specs=(
            P(("group", "trade"), None),
            P(),
            P(("group", "trade"), None),
            P(("group", "trade")),
            P(("group", "trade")),
            P(("group", "trade")),
            P("group"),
            P(("group", "trade")),
            P(("group", "trade"), None),
        ),
        out_specs=P(("group", "trade"), None),
        check_vma=False,
    )
```

time: 29.2 us -> 26.8 us (0.918)
  Pallas kernels: 0 us -> 3.2 us
  other arithmetic: 3.16 us -> 0.89 us
  matrix products: 1.73 us -> 0 us
  starting transfers between devices: 14.5 us -> 13.1 us
  waiting for transfers between devices: 7.1 us -> 6.31 us
  local copies, waits for them, and re-layouts: 1.74 us -> 2.29 us
    pallas_call x0 -> x5, Pallas kernels: none -> 3.2 us  [call(): pl.pallas_call(kernel, out_shape=outs, in_specs=specs, out_specs=[VMEM] *...]
    dot_general x3 -> x0, matrix products: 1.73 us -> none  [the longest x1 0.75 us: body(): jnp.einsum('tdk,pdk->tdp', coef_used, basis_table, preferred_element_type...]
    ppermute x8, starting transfers between devices: 14.5 us -> 13.1 us  [swap(): return lax.ppermute(x, 'trade', [(i, i ^ (bit | 1)) for i in range(count)])]
    reduce_sum x2 -> x1, other arithmetic: 0.93 us -> 0.1 us  [body(): shortfall = jnp.sum(jnp.maximum(netted - collateral, 0.0), axis=(1, 3))]
    ppermute x8, waiting for transfers between devices: 7.1 us -> 6.31 us  [swap(): return lax.ppermute(x, 'trade', [(i, i ^ (bit | 1)) for i in range(count)])]
    lt x2 -> x0, other arithmetic: 0.74 us -> none  [the longest x1 0.74 us: body(): keep_mask = basis_index[None, :] < basis_size[:, None]]
    select_n x4, other arithmetic: 0.71 us -> 0.1 us  [the longest x1 0.07 us: body(): start = jnp.where(upper, flipped, margin_start)]
    unnamed x9 -> x16, local copies, waits for them, and re-layouts: 1.5 us -> 1.92 us
  transfers between devices with their start and end apart: 8 -> 8, of which waited for: 7 -> 7; matrix products, arithmetic and copies ran while one was open for 11% -> 1% of each run, Pallas kernels for 0% -> 8%
where the time goes in v3:
time: 26.8 us; the launch traced here: 26.6 us
  starting transfers between devices  13.1 us (49%)
  waiting for transfers between devices  6.31 us (24%)
  Pallas kernels  3.2 us (12%)
  local copies, waits for them, and re-layouts  2.29 us (9%)
  other arithmetic  0.89 us (3%)
  between operations  0.77 us (3%)
    ppermute x8, starting transfers between devices, swap(): return lax.ppermute(x, 'trade', [(i, i ^ (bit | 1)) for i in range(count)])  13.1 us
    ppermute x8, waiting for transfers between devices, swap(): return lax.ppermute(x, 'trade', [(i, i ^ (bit | 1)) for i in range(count)])  6.31 us
    pallas_call x5, Pallas kernels, call(): pl.pallas_call(kernel, out_shape=outs, in_specs=specs, out_specs=[VMEM] *...  3.2 us
    unnamed x16, local copies, waits for them, and re-layouts  1.92 us
    div x1, other arithmetic, body(): return shortfall / (2 * side_total)  0.57 us
  transfers between devices with their start and end apart: 8, of which 7 were waited for; matrix products, arithmetic and copies ran while one was open for 1% of the time, Pallas kernels for 8%

profile of v3, /device:TPU:0, one launch (start us, length us, event | category | flops | bytes accessed | tf_op | source)
XLA Modules:
  0.0 26.6 jit_solution(6103160056973525176)
XLA Ops:
  0.0 0.5 %collective-permute-start = (bf16[4,128]{1,0:T(4,128)(2,1)}, bf16[4,128]{1,0:T(4,128)(2,1)S(1)}, u32[]{:S(2)}, u32[]{:S(2)}) collective-permute-start(bf16[4,128]{1,0:T(4,128)(2,1)} %factors_ref.1), channel_id=1, source_target_pairs={{0,1},{1,0},{2,3},{3,2},{4,5},{5,4},{6,7},{7,6},{8,9},{9,8},{10,11... | collective-permute-start | bytes 3080 | tf_op jit(solution)/shard_map/ppermute | solution.py:32
  1.2 0.3 %collective-permute-done = bf16[4,128]{1,0:T(4,128)(2,1)S(1)} collective-permute-done((bf16[4,128]{1,0:T(4,128)(2,1)}, bf16[4,128]{1,0:T(4,128)(2,1)S(1)}, u32[]{:S(2)}, u32[]{:S(2)}) %collective-permute-start) | collective-permute-done | bytes 1056 | tf_op jit(solution)/shard_map/ppermute | solution.py:32
  1.5 2.7 %collective-permute-start.1 = (bf16[8,128]{1,0:T(8,128)(2,1)S(1)}, bf16[8,128]{1,0:T(8,128)(2,1)S(1)}, u32[]{:S(2)}, u32[]{:S(2)}) collective-permute-start(bf16[8,128]{1,0:T(8,128)(2,1)S(1)} %pad_maximum_fusion.3), channel_id=1, source_target_pairs={{0,3},{1,2},{2,1},{3,0},{4,7},{5,6},{6,5},{7,4},{8,11},{9,10},{10,... | collective-permute-start | bytes 6152 | tf_op jit(solution)/shard_map/ppermute | solution.py:32
  4.2 1.2 %copy-done = bf16[2048,256]{1,0:T(8,128)(2,1)S(1)} copy-done((bf16[2048,256]{1,0:T(8,128)(2,1)S(1)}, bf16[2048,256]{1,0:T(8,128)(2,1)}, u32[]{:S(2)}) %copy-start) | copy-done | bytes 1048600
  5.4 0.5 %shard_map.93.used_ref = bf16[2048,256]{1,0:T(8,128)(2,1)S(1)} custom-call(bf16[2048,256]{1,0:T(8,128)(2,1)S(1)} %copy-done, s32[16,128]{1,0:T(8,128)S(1)} %bitcast.5), custom_call_target="tpu_custom_call" | custom-call | flops 100000000 | bytes 2105344 | tf_op jit(solution)/shard_map/pallas_call | solution.py:21
  6.0 1.6 %collective-permute-start.2 = (bf16[16,128]{1,0:T(8,128)(2,1)S(1)}, bf16[16,128]{1,0:T(8,128)(2,1)S(1)}, u32[]{:S(2)}, u32[]{:S(2)}) collective-permute-start(bf16[16,128]{1,0:T(8,128)(2,1)S(1)} %pad_maximum_fusion.1), channel_id=1, source_target_pairs={{0,5},{1,4},{2,7},{3,6},{4,1},{5,0},{6,3},{7,2},{8,13},{9,12},{10,... | collective-permute-start | bytes 12296 | tf_op jit(solution)/shard_map/ppermute | solution.py:32
  7.5 0.6 %copy-done.5 = f32[2]{0:T(128)S(1)} copy-done((f32[2]{0:T(128)S(1)}, f32[2]{0:T(128)}, u32[]{:S(2)}) %copy-start.5) | copy-done | bytes 32
  8.2 0.8 %shard_map.92 = (f32[2,128]{1,0:T(2,128)S(1)}, bf16[3,256,128]{2,1,0:T(8,128)(2,1)S(1)}, bf16[32,2048]{1,0:T(8,128)(2,1)S(1)}) custom-call(s32[1]{0:T(128)} %bitcast.2.refs_0_, s32[1]{0:T(128)S(6)} %copy.10.refs_1_, f32[2]{0:T(128)S(1)} %copy-done.5, f32[16,32]{1,0:T(8,128)S(1)} %bitcast.6, s32[16,128]{1,0:T(8,128)S(1)} %bitcast.7, s32[1,32]{1,0:T(1,128)S(1)} %bitcast.8), custom_call_target="tpu_custom_call" | custom-call | flops 100000000 | bytes 339088 | tf_op jit(solution)/shard_map/pallas_call | solution.py:21
  9.1 2.6 %collective-permute-start.3 = (bf16[32,128]{1,0:T(8,128)(2,1)S(1)}, bf16[32,128]{1,0:T(8,128)(2,1)S(1)}, u32[]{:S(2)}, u32[]{:S(2)}) collective-permute-start(bf16[32,128]{1,0:T(8,128)(2,1)S(1)} %pad_maximum_fusion.paths_ref), channel_id=1, source_target_pairs={{0,9},{1,8},{2,11},{3,10},{4,13},{5,12},{6,15},{7,14},{8,1},{9,0},... | collective-permute-start | bytes 24584 | tf_op jit(solution)/shard_map/ppermute | solution.py:32
  11.6 1.0 %shard_map.94.near_ref = f32[32,256]{1,0:T(8,128)S(1)} custom-call(bf16[32,128]{1,0:T(8,128)(2,1)S(1)} %pad_maximum_fusion.paths_ref, bf16[3,256,128]{2,1,0:T(8,128)(2,1)S(1)} %get-tuple-element.17.split_ref, bf16[2048,256]{1,0:T(8,128)(2,1)S(1)} %shard_map.93.used_ref, bf16[32,2048]{1,0:T(8,128)(2,1)S(1)} %get-tuple-element.19.onehot_ref), custom_call_target="tpu_custom_call" | custom-call | flops 301989888 | bytes 1417216 | tf_op jit(solution)/shard_map/pallas_call | solution.py:21
  12.6 0.5 %collective-permute-done.3.paths_ref = bf16[32,128]{1,0:T(8,128)(2,1)S(1)} collective-permute-done((bf16[32,128]{1,0:T(8,128)(2,1)S(1)}, bf16[32,128]{1,0:T(8,128)(2,1)S(1)}, u32[]{:S(2)}, u32[]{:S(2)}) %collective-permute-start.3) | collective-permute-done | bytes 8224 | tf_op jit(solution)/shard_map/ppermute | solution.py:32
  13.1 1.0 %shard_map.95 = (f32[16,512]{1,0:T(8,128)S(1)}, f32[16,512]{1,0:T(8,128)S(1)}) custom-call(bf16[32,128]{1,0:T(8,128)(2,1)S(1)} %collective-permute-done.3.paths_ref, bf16[3,256,128]{2,1,0:T(8,128)(2,1)S(1)} %get-tuple-element.17.split_ref, bf16[2048,256]{1,0:T(8,128)(2,1)S(1)} %shard_map.93.used_ref, bf16[32,2048]{1,0:T(8,128)(2,1)S(1)} %get-tuple-element.19.onehot_ref, ...), custom_call_target="tpu_custom_call" | custom-call | flops 301989888 | bytes 1482752 | tf_op jit(solution)/shard_map/pallas_call | solution.py:21
  14.1 0.4 %collective-permute-start.4 = (f32[16,512]{1,0:T(8,128)S(1)}, f32[16,512]{1,0:T(8,128)S(1)}, u32[]{:S(2)}, u32[]{:S(2)}) collective-permute-start(f32[16,512]{1,0:T(8,128)S(1)} %get-tuple-element.21), channel_id=1, source_target_pairs={{0,1},{1,0},{2,3},{3,2},{4,5},{5,4},{6,7},{7,6},{8,9},{9,8},{10,11... | collective-permute-start | bytes 98312 | tf_op jit(solution)/shard_map/ppermute | solution.py:32
  14.4 0.9 %collective-permute-done.4 = f32[16,512]{1,0:T(8,128)S(1)} collective-permute-done((f32[16,512]{1,0:T(8,128)S(1)}, f32[16,512]{1,0:T(8,128)S(1)}, u32[]{:S(2)}, u32[]{:S(2)}) %collective-permute-start.4) | collective-permute-done | bytes 32800 | tf_op jit(solution)/shard_map/ppermute | solution.py:32
  15.3 1.3 %collective-permute-start.5 = (f32[8,512]{1,0:T(8,128)S(1)}, f32[8,512]{1,0:T(8,128)S(1)}, u32[]{:S(2)}, u32[]{:S(2)}) collective-permute-start(f32[8,512]{1,0:T(8,128)S(1)} %slice.48), channel_id=1, source_target_pairs={{0,3},{1,2},{2,1},{3,0},{4,7},{5,6},{6,5},{7,4},{8,11},{9,10},{10,... | collective-permute-start | bytes 49160 | tf_op jit(solution)/shard_map/ppermute | solution.py:32
  16.7 1.8 %collective-permute-done.5 = f32[8,512]{1,0:T(8,128)S(1)} collective-permute-done((f32[8,512]{1,0:T(8,128)S(1)}, f32[8,512]{1,0:T(8,128)S(1)}, u32[]{:S(2)}, u32[]{:S(2)}) %collective-permute-start.5) | collective-permute-done | bytes 16416 | tf_op jit(solution)/shard_map/ppermute | solution.py:32
  18.6 1.6 %collective-permute-start.6 = (f32[4,512]{1,0:T(4,128)S(1)}, f32[4,512]{1,0:T(4,128)S(1)}, u32[]{:S(2)}, u32[]{:S(2)}) collective-permute-start(f32[4,512]{1,0:T(4,128)S(1)} %slice.50), channel_id=1, source_target_pairs={{0,5},{1,4},{2,7},{3,6},{4,1},{5,0},{6,3},{7,2},{8,13},{9,12},{10,... | collective-permute-start | bytes 24584 | tf_op jit(solution)/shard_map/ppermute | solution.py:32
  20.2 0.1 broadcast_in_dim.8
  20.3 1.4 %collective-permute-done.6 = f32[4,512]{1,0:T(4,128)S(1)} collective-permute-done((f32[4,512]{1,0:T(4,128)S(1)}, f32[4,512]{1,0:T(4,128)S(1)}, u32[]{:S(2)}, u32[]{:S(2)}) %collective-permute-start.6) | collective-permute-done | bytes 8224 | tf_op jit(solution)/shard_map/ppermute | solution.py:32
  21.7 2.6 %collective-permute-start.7 = (f32[2,512]{1,0:T(2,128)S(1)}, f32[2,512]{1,0:T(2,128)S(1)}, u32[]{:S(2)}, u32[]{:S(2)}) collective-permute-start(f32[2,512]{1,0:T(2,128)S(1)} %pad_maximum_fusion.2), channel_id=1, source_target_pairs={{0,9},{1,8},{2,11},{3,10},{4,13},{5,12},{6,15},{7,14},{8,1},{9,0},... | collective-permute-start | bytes 12296 | tf_op jit(solution)/shard_map/ppermute | solution.py:32
  24.3 0.1 slice_reduce_fusion
  24.4 1.3 %collective-permute-done.7 = f32[2,512]{1,0:T(2,128)S(1)} collective-permute-done((f32[2,512]{1,0:T(2,128)S(1)}, f32[2,512]{1,0:T(2,128)S(1)}, u32[]{:S(2)}, u32[]{:S(2)}) %collective-permute-start.7) | collective-permute-done | bytes 4128 | tf_op jit(solution)/shard_map/ppermute | solution.py:32
  25.9 0.1 fusion.2
  26.0 0.6 %broadcast_multiply_fusion = f32[2,8]{1,0:T(2,128)} fusion(f32[2,8]{1,0:T(2,128)S(1)} %fusion.2), kind=kLoop, calls=%fused_computation.20 | loop fusion | flops 16 | bytes 128 | tf_op jit(solution)/shard_map/div | solution.py:211
  (36 shorter events, 0.5 us)
Async XLA Ops:
  0.0 1.5 %collective-permute-start = (bf16[4,128]{1,0:T(4,128)(2,1)}, bf16[4,128]{1,0:T(4,128)(2,1)S(1)}, u32[]{:S(2)}, u32[]{:S(2)}) collective-permute-start(bf16[4,128]{1,0:T(4,128)(2,1)} %factors_ref.1), channel_id=1, source_target_pairs={{0,1},{1,0},{2,3},{3,2},{4,5},{5,4},{6,7},{7,6},{8,9},{9,8},{10,11... | collective-permute-start | bytes 3080 | tf_op jit(solution)/shard_map/ppermute | solution.py:32
  0.5 0.7 %copy-start.4 = (bf16[4,128]{1,0:T(4,128)(2,1)S(1)}, bf16[4,128]{1,0:T(4,128)(2,1)}, u32[]{:S(2)}) copy-start(bf16[4,128]{1,0:T(4,128)(2,1)} %factors_ref.1) | copy-start | bytes 3076
  1.1 3.1 %copy-start.1 = (s32[2048]{0:T(1024)S(1)}, s32[2048]{0:T(1024)}, u32[]{:S(2)}) copy-start(s32[2048]{0:T(1024)} %param.12) | copy-start | bytes 24580
  1.5 4.4 %collective-permute-start.1 = (bf16[8,128]{1,0:T(8,128)(2,1)S(1)}, bf16[8,128]{1,0:T(8,128)(2,1)S(1)}, u32[]{:S(2)}, u32[]{:S(2)}) collective-permute-start(bf16[8,128]{1,0:T(8,128)(2,1)S(1)} %pad_maximum_fusion.3), channel_id=1, source_target_pairs={{0,3},{1,2},{2,1},{3,0},{4,7},{5,6},{6,5},{7,4},{8,11},{9,10},{10,... | collective-permute-start | bytes 6152 | tf_op jit(solution)/shard_map/ppermute | solution.py:32
  4.2 1.2 %copy-start = (bf16[2048,256]{1,0:T(8,128)(2,1)S(1)}, bf16[2048,256]{1,0:T(8,128)(2,1)}, u32[]{:S(2)}) copy-start(bf16[2048,256]{1,0:T(8,128)(2,1)} %coef_ref.1) | copy-start | bytes 3145732
  5.4 2.1 %copy-start.3 = (s32[2048]{0:T(1024)S(1)}, s32[2048]{0:T(1024)}, u32[]{:S(2)}) copy-start(s32[2048]{0:T(1024)} %param.13) | copy-start | bytes 24580
  5.9 1.6 %copy-start.2 = (f32[32,16]{0,1:T(8,128)S(1)}, f32[32,16]{0,1:T(8,128)}, u32[]{:S(2)}) copy-start(f32[32,16]{0,1:T(8,128)} %param.10) | copy-start | bytes 6148
  6.0 3.1 %collective-permute-start.2 = (bf16[16,128]{1,0:T(8,128)(2,1)S(1)}, bf16[16,128]{1,0:T(8,128)(2,1)S(1)}, u32[]{:S(2)}, u32[]{:S(2)}) collective-permute-start(bf16[16,128]{1,0:T(8,128)(2,1)S(1)} %pad_maximum_fusion.1), channel_id=1, source_target_pairs={{0,5},{1,4},{2,7},{3,6},{4,1},{5,0},{6,3},{7,2},{8,13},{9,12},{10,... | collective-permute-start | bytes 12296 | tf_op jit(solution)/shard_map/ppermute | solution.py:32
  7.5 0.7 %copy-start.5 = (f32[2]{0:T(128)S(1)}, f32[2]{0:T(128)}, u32[]{:S(2)}) copy-start(f32[2]{0:T(128)} %refs_2_.1) | copy-start | bytes 28
  7.5 0.7 %copy-start.6 = (s32[32]{0:T(128)S(1)}, s32[32]{0:T(128)}, u32[]{:S(2)}) copy-start(s32[32]{0:T(128)} %param.15) | copy-start | bytes 388
  9.1 4.0 %collective-permute-start.3 = (bf16[32,128]{1,0:T(8,128)(2,1)S(1)}, bf16[32,128]{1,0:T(8,128)(2,1)S(1)}, u32[]{:S(2)}, u32[]{:S(2)}) collective-permute-start(bf16[32,128]{1,0:T(8,128)(2,1)S(1)} %pad_maximum_fusion.paths_ref), channel_id=1, source_target_pairs={{0,9},{1,8},{2,11},{3,10},{4,13},{5,12},{6,15},{7,14},{8,1},{9,0},... | collective-permute-start | bytes 24584 | tf_op jit(solution)/shard_map/ppermute | solution.py:32
  14.1 1.3 %collective-permute-start.4 = (f32[16,512]{1,0:T(8,128)S(1)}, f32[16,512]{1,0:T(8,128)S(1)}, u32[]{:S(2)}, u32[]{:S(2)}) collective-permute-start(f32[16,512]{1,0:T(8,128)S(1)} %get-tuple-element.21), channel_id=1, source_target_pairs={{0,1},{1,0},{2,3},{3,2},{4,5},{5,4},{6,7},{7,6},{8,9},{9,8},{10,11... | collective-permute-start | bytes 98312 | tf_op jit(solution)/shard_map/ppermute | solution.py:32
  15.3 1.3 %copy-start.7 = (f32[2,64]{1,0:T(2,128)S(1)}, f32[2,64]{1,0:T(2,128)}, u32[]{:S(2)}) copy-start(f32[2,64]{1,0:T(2,128)} %param.17) | copy-start | bytes 1540
  15.3 3.2 %collective-permute-start.5 = (f32[8,512]{1,0:T(8,128)S(1)}, f32[8,512]{1,0:T(8,128)S(1)}, u32[]{:S(2)}, u32[]{:S(2)}) collective-permute-start(f32[8,512]{1,0:T(8,128)S(1)} %slice.48), channel_id=1, source_target_pairs={{0,3},{1,2},{2,1},{3,0},{4,7},{5,6},{6,5},{7,4},{8,11},{9,10},{10,... | collective-permute-start | bytes 49160 | tf_op jit(solution)/shard_map/ppermute | solution.py:32
  18.6 3.1 %collective-permute-start.6 = (f32[4,512]{1,0:T(4,128)S(1)}, f32[4,512]{1,0:T(4,128)S(1)}, u32[]{:S(2)}, u32[]{:S(2)}) collective-permute-start(f32[4,512]{1,0:T(4,128)S(1)} %slice.50), channel_id=1, source_target_pairs={{0,5},{1,4},{2,7},{3,6},{4,1},{5,0},{6,3},{7,2},{8,13},{9,12},{10,... | collective-permute-start | bytes 24584 | tf_op jit(solution)/shard_map/ppermute | solution.py:32
  21.7 4.0 %collective-permute-start.7 = (f32[2,512]{1,0:T(2,128)S(1)}, f32[2,512]{1,0:T(2,128)S(1)}, u32[]{:S(2)}, u32[]{:S(2)}) collective-permute-start(f32[2,512]{1,0:T(2,128)S(1)} %pad_maximum_fusion.2), channel_id=1, source_target_pairs={{0,9},{1,8},{2,11},{3,10},{4,13},{5,12},{6,15},{7,14},{8,1},{9,0},... | collective-permute-start | bytes 12296 | tf_op jit(solution)/shard_map/ppermute | solution.py:32

commit v4 on v3

--- a/solution.py
+++ b/solution.py
@@ -11,21 +11,28 @@
 LAG = 2
 LANES = 128
 PATH_BLOCK = 32
-SLOT_BLOCK = 1024
+SLOT_BLOCK = 512
 VMEM = pl.BlockSpec(memory_space=pltpu.VMEM)
 SMEM = pl.BlockSpec(memory_space=pltpu.SMEM)
-
-
-def call(kernel, outs, specs, flops, args):
+HBM = pl.BlockSpec(memory_space=pltpu.HBM)
+PARTS = 4
+
+
+def call(kernel, outs, specs, flops, args, scratch=()):
     sizes = [a.size * a.dtype.itemsize for a in (*args, *outs)]
     return pl.pallas_call(
         kernel,
         out_shape=outs,
         in_specs=specs,
         out_specs=[VMEM] * len(outs),
+        scratch_shapes=scratch,
         compiler_params=pltpu.CompilerParams(vmem_limit_bytes=24 * 2**20),
         cost_estimate=pl.CostEstimate(flops=flops, bytes_accessed=sum(sizes), transcendentals=0),
     )(*args)
+
+
+def in_hbm(x):
+    return pltpu.with_memory_space_constraint(x, pltpu.HBM)
 
 
 def swap(x, bit, count):
@@ -64,8 +71,37 @@
 
 
 def rows_kernel(
-    count, me_ref, live_ref, limit_ref, loadings_ref, ids_ref, owner_ref, limits_ref, split_ref, onehot_ref
+    count,
+    me_ref,
+    live_ref,
+    limit_hbm,
+    loadings_hbm,
+    ids_hbm,
+    owner_hbm,
+    limits_ref,
+    split_ref,
+    onehot_ref,
+    limit_ref,
+    loadings_ref,
+    ids_ref,
+    owner_ref,
+    sems,
 ):
+    copies = [
+        pltpu.make_async_copy(source, target, sems.at[i])
+        for i, (source, target) in enumerate(
+            (
+                (limit_hbm, limit_ref),
+                (loadings_hbm, loadings_ref),
+                (ids_hbm, ids_ref),
+                (owner_hbm, owner_ref),
+            )
+        )
+    ]
+    for copy in copies:
+        copy.start()
+    for copy in copies:
+        copy.wait()
     own_rows = limits_ref.shape[0]
     for r in range(own_rows):
         limits_ref[r : r + 1, :] = jnp.full((1, LANES), limit_ref[r])
@@ -81,10 +117,10 @@
         ids = jnp.where(lane + c * LANES < live, ids_ref[c : c + 1, :], -1)
         hit = jnp.where(ids == set_at, 1.0, 0.0)
         onehot_ref[:, c * LANES : (c + 1) * LANES] = hit.astype(jnp.bfloat16)
-    tall = jnp.concatenate([loadings_ref[...].T] * DATES, axis=0)
+    tall = jnp.concatenate([loadings_ref[...]] * DATES, axis=0)
     wide = jnp.concatenate([tall] * DATES, axis=1)
-    row = lax.broadcasted_iota(jnp.int32, wide.shape, 0) // K
-    column = lax.broadcasted_iota(jnp.int32, wide.shape, 1) // F
+    row = lax.broadcasted_iota(jnp.int32, wide.shape, 0) // F
+    column = lax.broadcasted_iota(jnp.int32, wide.shape, 1) // K
     rest = jnp.where(row == column, wide, 0.0)
     for i in range(3):
         part = rest.astype(jnp.bfloat16)
@@ -92,31 +128,42 @@
         rest = rest - part.astype(jnp.float32)
 
 
-def coef_kernel(coef_ref, size_ref, used_ref):
+def coef_kernel(coef_hbm, size_hbm, used_ref, coef_ref, size_ref, sems):
+    parts = sems.shape[0] - 1
+    step = coef_ref.shape[0] // parts
+    sizes_in = pltpu.make_async_copy(size_hbm, size_ref, sems.at[parts])
+    sizes_in.start()
+    coef_in = []
+    for i in range(parts):
+        rows = pl.ds(i * step, step)
+        coef_in.append(pltpu.make_async_copy(coef_hbm.at[rows, :], coef_ref.at[rows, :], sems.at[i]))
+        coef_in[i].start()
+    sizes_in.wait()
     sizes = size_ref[...].astype(jnp.float32).T
     width = coef_ref.shape[1]
     basis = (lax.broadcasted_iota(jnp.int32, (1, width), 1) & (K - 1)).astype(jnp.float32)
-    for c in range(size_ref.shape[0]):
-        rows = slice(c * LANES, (c + 1) * LANES)
-        coef = coef_ref[rows, :].astype(jnp.float32)
-        used_ref[rows, :] = jnp.where(basis < sizes[:, c : c + 1], coef, 0.0).astype(jnp.bfloat16)
+    for i in range(parts):
+        coef_in[i].wait()
+        for c in range(i * step // LANES, (i + 1) * step // LANES):
+            rows = slice(c * LANES, (c + 1) * LANES)
+            coef = coef_ref[rows, :].astype(jnp.float32)
+            used_ref[rows, :] = jnp.where(basis < sizes[:, c : c + 1], coef, 0.0).astype(jnp.bfloat16)
 
 
 def net_block(paths, split_ref, used_ref, onehot_ref):
     total = paths.shape[0]
-    tiled = jnp.concatenate([paths] * DATES, axis=0)
-    contract = (((1,), (1,)), ((), ()))
-    loaded = sum(
-        lax.dot_general(split_ref[i], tiled, contract, preferred_element_type=jnp.float32) for i in (2, 1, 0)
-    )
-    row = lax.broadcasted_iota(jnp.int32, loaded.shape, 0) // K
-    column = lax.broadcasted_iota(jnp.int32, loaded.shape, 1) // total
-    table = jnp.where(row == column, jnp.tanh(loaded), 0.0).astype(jnp.bfloat16)
+    loaded = sum(jnp.dot(paths, split_ref[i], preferred_element_type=jnp.float32) for i in (2, 1, 0))
+    tiled = jnp.concatenate([jnp.tanh(loaded)] * DATES, axis=0)
+    row = lax.broadcasted_iota(jnp.int32, tiled.shape, 0) // total
+    column = lax.broadcasted_iota(jnp.int32, tiled.shape, 1) // K
+    table = jnp.where(row == column, tiled, 0.0).astype(jnp.bfloat16)
     slots = used_ref.shape[0]
     step = min(SLOT_BLOCK, slots)
     result = jnp.zeros((onehot_ref.shape[0], DATES * total), jnp.float32)
     for at in range(0, slots, step):
-        values = jnp.dot(used_ref[at : at + step, :], table, preferred_element_type=jnp.float32)
+        values = lax.dot_general(
+            used_ref[at : at + step, :], table, (((1,), (1,)), ((), ())), preferred_element_type=jnp.float32
+        )
         values = values.astype(jnp.bfloat16)
         result = result + jnp.dot(onehot_ref[:, at : at + step], values, preferred_element_type=jnp.float32)
     return result
@@ -166,16 +213,32 @@
     near = join(own, swap(factors, 1, count), 1)
     sizes = basis_size.reshape(-1, LANES)
     sizes, near = lax.optimization_barrier((sizes, near))
-    (used,) = call(coef_kernel, [shape(trade_coef.shape, bf16)], [VMEM, VMEM], 10**8, (trade_coef, sizes))
+    (used,) = call(
+        coef_kernel,
+        [shape(trade_coef.shape, bf16)],
+        [HBM, HBM],
+        10**8,
+        (in_hbm(trade_coef), in_hbm(sizes)),
+        [pltpu.VMEM(trade_coef.shape, bf16), pltpu.VMEM(sizes.shape, jnp.int32), pltpu.SemaphoreType.DMA((PARTS + 1,))],
+    )
     near = join(near, swap(near, 2, count), 2)
     ids = set_ids.reshape(-1, LANES)
+    owner = netting_row.reshape(1, -1)
+    turned = loadings.T
     ids, near = lax.optimization_barrier((ids, near))
     limits, split, onehot = call(
         lambda *refs: rows_kernel(count, *refs),
-        [shape((own_rows, LANES), f32), shape((3, DATES * K, DATES * F), bf16), shape((set_total, slot_total), bf16)],
-        [SMEM, SMEM, SMEM, VMEM, VMEM, VMEM],
+        [shape((own_rows, LANES), f32), shape((3, DATES * F, DATES * K), bf16), shape((set_total, slot_total), bf16)],
+        [SMEM] * 2 + [HBM] * 4,
         10**8,
-        (me.astype(jnp.int32).reshape(1), live_count, threshold, loadings.T, ids, netting_row.reshape(1, -1)),
+        (me.astype(jnp.int32).reshape(1), live_count, *map(in_hbm, (threshold, turned, ids, owner))),
+        [
+            pltpu.SMEM(threshold.shape, f32),
+            pltpu.VMEM(turned.shape, f32),
+            pltpu.VMEM(ids.shape, jnp.int32),
+            pltpu.VMEM(owner.shape, jnp.int32),
+            pltpu.SemaphoreType.DMA((4,)),
+        ],
     )
     bit = 4
     while bit < count // 2:

time: 26.8 us -> 26.5 us (0.989)
  local copies, waits for them, and re-layouts: 2.29 us -> 0.39 us
  Pallas kernels: 3.2 us -> 4.2 us
  waiting for transfers between devices: 6.31 us -> 6.84 us
    unnamed x16 -> x4, local copies, waits for them, and re-layouts: 1.92 us -> 0.02 us
    pallas_call x5, Pallas kernels: 3.2 us -> 4.2 us  [call(): pl.pallas_call(kernel, out_shape=outs, in_specs=specs, out_specs=[VMEM] *...]
    ppermute x8, waiting for transfers between devices: 6.31 us -> 6.84 us  [swap(): return lax.ppermute(x, 'trade', [(i, i ^ (bit | 1)) for i in range(count)])]
  transfers between devices with their start and end apart: 8 -> 8, of which waited for: 7 -> 7; matrix products, arithmetic and copies ran while one was open for 1% -> 1% of each run, Pallas kernels for 8% -> 13%
where the time goes in v4:
time: 26.5 us; the launch traced here: 26.3 us
  starting transfers between devices  13.2 us (50%)
  waiting for transfers between devices  6.84 us (26%)
  Pallas kernels  4.2 us (16%)
  other arithmetic  0.89 us (3%)
  between operations  0.75 us (3%)
  local copies, waits for them, and re-layouts  0.39 us (1%)
    ppermute x8, starting transfers between devices, swap(): return lax.ppermute(x, 'trade', [(i, i ^ (bit | 1)) for i in range(count)])  13.2 us
    ppermute x8, waiting for transfers between devices, swap(): return lax.ppermute(x, 'trade', [(i, i ^ (bit | 1)) for i in range(count)])  6.84 us
    pallas_call x5, Pallas kernels, call(): pl.pallas_call(kernel, out_shape=outs, in_specs=specs, out_specs=[VMEM] *...  4.2 us
    div x1, other arithmetic, body(): return shortfall / (2 * side_total)  0.57 us
  transfers between devices with their start and end apart: 8, of which 7 were waited for; matrix products, arithmetic and copies ran while one was open for 1% of the time, Pallas kernels for 13%

profile of v4, /device:TPU:0, one launch (start us, length us, event | category | flops | bytes accessed | tf_op | source)
XLA Modules:
  0.0 26.3 jit_solution(7716729377422936522)
XLA Ops:
  0.0 0.5 %collective-permute-start = (bf16[4,128]{1,0:T(4,128)(2,1)}, bf16[4,128]{1,0:T(4,128)(2,1)S(1)}, u32[]{:S(2)}, u32[]{:S(2)}) collective-permute-start(bf16[4,128]{1,0:T(4,128)(2,1)} %factors_ref.1), channel_id=1, source_target_pairs={{0,1},{1,0},{2,3},{3,2},{4,5},{5,4},{6,7},{7,6},{8,9},{9,8},{10,11... | collective-permute-start | bytes 3080 | tf_op jit(solution)/shard_map/ppermute | solution.py:39
  1.1 0.3 %collective-permute-done = bf16[4,128]{1,0:T(4,128)(2,1)S(1)} collective-permute-done((bf16[4,128]{1,0:T(4,128)(2,1)}, bf16[4,128]{1,0:T(4,128)(2,1)S(1)}, u32[]{:S(2)}, u32[]{:S(2)}) %collective-permute-start) | collective-permute-done | bytes 1056 | tf_op jit(solution)/shard_map/ppermute | solution.py:39
  1.5 2.7 %collective-permute-start.1 = (bf16[8,128]{1,0:T(8,128)(2,1)S(1)}, bf16[8,128]{1,0:T(8,128)(2,1)S(1)}, u32[]{:S(2)}, u32[]{:S(2)}) collective-permute-start(bf16[8,128]{1,0:T(8,128)(2,1)S(1)} %pad_maximum_fusion.3), channel_id=1, source_target_pairs={{0,3},{1,2},{2,1},{3,0},{4,7},{5,6},{6,5},{7,4},{8,11},{9,10},{10,... | collective-permute-start | bytes 6152 | tf_op jit(solution)/shard_map/ppermute | solution.py:39
  4.2 1.6 %shard_map.93.used_ref = bf16[2048,256]{1,0:T(8,128)(2,1)S(1)} custom-call(bf16[2048,256]{1,0:T(8,128)(2,1)} %coef_hbm.1, s32[16,128]{1,0:T(8,128)} %bitcast.5), custom_call_target="tpu_custom_call" | custom-call | flops 100000000 | bytes 2105344 | tf_op jit(solution)/shard_map/pallas_call | solution.py:23
  5.8 1.6 %collective-permute-start.2 = (bf16[16,128]{1,0:T(8,128)(2,1)S(1)}, bf16[16,128]{1,0:T(8,128)(2,1)S(1)}, u32[]{:S(2)}, u32[]{:S(2)}) collective-permute-start(bf16[16,128]{1,0:T(8,128)(2,1)S(1)} %pad_maximum_fusion.1), channel_id=1, source_target_pairs={{0,5},{1,4},{2,7},{3,6},{4,1},{5,0},{6,3},{7,2},{8,13},{9,12},{10,... | collective-permute-start | bytes 12296 | tf_op jit(solution)/shard_map/ppermute | solution.py:39
  7.4 0.9 %shard_map.92 = (f32[2,128]{1,0:T(2,128)S(1)}, bf16[3,128,256]{2,1,0:T(8,128)(2,1)S(1)}, bf16[32,2048]{1,0:T(8,128)(2,1)S(1)}) custom-call(s32[1]{0:T(128)} %bitcast.2.refs_0_, s32[1]{0:T(128)S(6)} %copy.10.refs_1_, f32[2]{0:T(128)} %refs_2_.1, f32[16,32]{1,0:T(8,128)} %bitcast.6, s32[16,128]{1,0:T(8,128)} %bitcast.7, s32[1,32]{1,0:T(1,128)} %bitcast.8), custom_call_target="tpu_custom_call" | custom-call | flops 100000000 | bytes 339088 | tf_op jit(solution)/shard_map/pallas_call | solution.py:23
  8.3 0.6 %collective-permute-done.2 = bf16[16,128]{1,0:T(8,128)(2,1)S(1)} collective-permute-done((bf16[16,128]{1,0:T(8,128)(2,1)S(1)}, bf16[16,128]{1,0:T(8,128)(2,1)S(1)}, u32[]{:S(2)}, u32[]{:S(2)}) %collective-permute-start.2) | collective-permute-done | bytes 4128 | tf_op jit(solution)/shard_map/ppermute | solution.py:39
  8.9 2.6 %collective-permute-start.3 = (bf16[32,128]{1,0:T(8,128)(2,1)S(1)}, bf16[32,128]{1,0:T(8,128)(2,1)S(1)}, u32[]{:S(2)}, u32[]{:S(2)}) collective-permute-start(bf16[32,128]{1,0:T(8,128)(2,1)S(1)} %pad_maximum_fusion.paths_ref), channel_id=1, source_target_pairs={{0,9},{1,8},{2,11},{3,10},{4,13},{5,12},{6,15},{7,14},{8,1},{9,0},... | collective-permute-start | bytes 24584 | tf_op jit(solution)/shard_map/ppermute | solution.py:39
  11.5 0.9 %shard_map.94.near_ref = f32[32,256]{1,0:T(8,128)S(1)} custom-call(bf16[32,128]{1,0:T(8,128)(2,1)S(1)} %pad_maximum_fusion.paths_ref, bf16[3,128,256]{2,1,0:T(8,128)(2,1)S(1)} %get-tuple-element.17.split_ref, bf16[2048,256]{1,0:T(8,128)(2,1)S(1)} %shard_map.93.used_ref, bf16[32,2048]{1,0:T(8,128)(2,1)S(1)} %get-tuple-element.19.onehot_ref), custom_call_target="tpu_custom_call" | custom-call | flops 301989888 | bytes 1417216 | tf_op jit(solution)/shard_map/pallas_call | solution.py:23
  12.4 0.6 %collective-permute-done.3.paths_ref = bf16[32,128]{1,0:T(8,128)(2,1)S(1)} collective-permute-done((bf16[32,128]{1,0:T(8,128)(2,1)S(1)}, bf16[32,128]{1,0:T(8,128)(2,1)S(1)}, u32[]{:S(2)}, u32[]{:S(2)}) %collective-permute-start.3) | collective-permute-done | bytes 8224 | tf_op jit(solution)/shard_map/ppermute | solution.py:39
  13.0 0.9 %shard_map.95 = (f32[16,512]{1,0:T(8,128)S(1)}, f32[16,512]{1,0:T(8,128)S(1)}) custom-call(bf16[32,128]{1,0:T(8,128)(2,1)S(1)} %collective-permute-done.3.paths_ref, bf16[3,128,256]{2,1,0:T(8,128)(2,1)S(1)} %get-tuple-element.17.split_ref, bf16[2048,256]{1,0:T(8,128)(2,1)S(1)} %shard_map.93.used_ref, bf16[32,2048]{1,0:T(8,128)(2,1)S(1)} %get-tuple-element.19.onehot_ref, ...), custom_call_target="tpu_custom_call" | custom-call | flops 301989888 | bytes 1482752 | tf_op jit(solution)/shard_map/pallas_call | solution.py:23
  13.8 0.3 %collective-permute-start.4 = (f32[16,512]{1,0:T(8,128)S(1)}, f32[16,512]{1,0:T(8,128)S(1)}, u32[]{:S(2)}, u32[]{:S(2)}) collective-permute-start(f32[16,512]{1,0:T(8,128)S(1)} %get-tuple-element.21), channel_id=1, source_target_pairs={{0,1},{1,0},{2,3},{3,2},{4,5},{5,4},{6,7},{7,6},{8,9},{9,8},{10,11... | collective-permute-start | bytes 98312 | tf_op jit(solution)/shard_map/ppermute | solution.py:39
  14.2 0.9 %collective-permute-done.4 = f32[16,512]{1,0:T(8,128)S(1)} collective-permute-done((f32[16,512]{1,0:T(8,128)S(1)}, f32[16,512]{1,0:T(8,128)S(1)}, u32[]{:S(2)}, u32[]{:S(2)}) %collective-permute-start.4) | collective-permute-done | bytes 32800 | tf_op jit(solution)/shard_map/ppermute | solution.py:39
  15.1 1.5 %collective-permute-start.5 = (f32[8,512]{1,0:T(8,128)S(1)}, f32[8,512]{1,0:T(8,128)S(1)}, u32[]{:S(2)}, u32[]{:S(2)}) collective-permute-start(f32[8,512]{1,0:T(8,128)S(1)} %slice.48), channel_id=1, source_target_pairs={{0,3},{1,2},{2,1},{3,0},{4,7},{5,6},{6,5},{7,4},{8,11},{9,10},{10,... | collective-permute-start | bytes 49160 | tf_op jit(solution)/shard_map/ppermute | solution.py:39
  16.6 1.7 %collective-permute-done.5 = f32[8,512]{1,0:T(8,128)S(1)} collective-permute-done((f32[8,512]{1,0:T(8,128)S(1)}, f32[8,512]{1,0:T(8,128)S(1)}, u32[]{:S(2)}, u32[]{:S(2)}) %collective-permute-start.5) | collective-permute-done | bytes 16416 | tf_op jit(solution)/shard_map/ppermute | solution.py:39
  18.3 1.6 %collective-permute-start.6 = (f32[4,512]{1,0:T(4,128)S(1)}, f32[4,512]{1,0:T(4,128)S(1)}, u32[]{:S(2)}, u32[]{:S(2)}) collective-permute-start(f32[4,512]{1,0:T(4,128)S(1)} %slice.50), channel_id=1, source_target_pairs={{0,5},{1,4},{2,7},{3,6},{4,1},{5,0},{6,3},{7,2},{8,13},{9,12},{10,... | collective-permute-start | bytes 24584 | tf_op jit(solution)/shard_map/ppermute | solution.py:39
  19.9 0.1 broadcast_in_dim.8
  20.0 1.4 %collective-permute-done.6 = f32[4,512]{1,0:T(4,128)S(1)} collective-permute-done((f32[4,512]{1,0:T(4,128)S(1)}, f32[4,512]{1,0:T(4,128)S(1)}, u32[]{:S(2)}, u32[]{:S(2)}) %collective-permute-start.6) | collective-permute-done | bytes 8224 | tf_op jit(solution)/shard_map/ppermute | solution.py:39
  21.5 2.6 %collective-permute-start.7 = (f32[2,512]{1,0:T(2,128)S(1)}, f32[2,512]{1,0:T(2,128)S(1)}, u32[]{:S(2)}, u32[]{:S(2)}) collective-permute-start(f32[2,512]{1,0:T(2,128)S(1)} %pad_maximum_fusion.2), channel_id=1, source_target_pairs={{0,9},{1,8},{2,11},{3,10},{4,13},{5,12},{6,15},{7,14},{8,1},{9,0},... | collective-permute-start | bytes 12296 | tf_op jit(solution)/shard_map/ppermute | solution.py:39
  24.1 0.1 slice_reduce_fusion
  24.2 1.3 %collective-permute-done.7 = f32[2,512]{1,0:T(2,128)S(1)} collective-permute-done((f32[2,512]{1,0:T(2,128)S(1)}, f32[2,512]{1,0:T(2,128)S(1)}, u32[]{:S(2)}, u32[]{:S(2)}) %collective-permute-start.7) | collective-permute-done | bytes 4128 | tf_op jit(solution)/shard_map/ppermute | solution.py:39
  25.5 0.1 reshape.22
  25.6 0.1 fusion.2
  25.7 0.6 %broadcast_multiply_fusion = f32[2,8]{1,0:T(2,128)} fusion(f32[2,8]{1,0:T(2,128)S(1)} %fusion.2), kind=kLoop, calls=%fused_computation.20 | loop fusion | flops 16 | bytes 128 | tf_op jit(solution)/shard_map/div | solution.py:274
  (24 shorter events, 0.3 us)
Async XLA Ops:
  0.0 1.5 %collective-permute-start = (bf16[4,128]{1,0:T(4,128)(2,1)}, bf16[4,128]{1,0:T(4,128)(2,1)S(1)}, u32[]{:S(2)}, u32[]{:S(2)}) collective-permute-start(bf16[4,128]{1,0:T(4,128)(2,1)} %factors_ref.1), channel_id=1, source_target_pairs={{0,1},{1,0},{2,3},{3,2},{4,5},{5,4},{6,7},{7,6},{8,9},{9,8},{10,11... | collective-permute-start | bytes 3080 | tf_op jit(solution)/shard_map/ppermute | solution.py:39
  0.5 0.7 %copy-start = (bf16[4,128]{1,0:T(4,128)(2,1)S(1)}, bf16[4,128]{1,0:T(4,128)(2,1)}, u32[]{:S(2)}) copy-start(bf16[4,128]{1,0:T(4,128)(2,1)} %factors_ref.1) | copy-start | bytes 3076
  1.5 4.3 %collective-permute-start.1 = (bf16[8,128]{1,0:T(8,128)(2,1)S(1)}, bf16[8,128]{1,0:T(8,128)(2,1)S(1)}, u32[]{:S(2)}, u32[]{:S(2)}) collective-permute-start(bf16[8,128]{1,0:T(8,128)(2,1)S(1)} %pad_maximum_fusion.3), channel_id=1, source_target_pairs={{0,3},{1,2},{2,1},{3,0},{4,7},{5,6},{6,5},{7,4},{8,11},{9,10},{10,... | collective-permute-start | bytes 6152 | tf_op jit(solution)/shard_map/ppermute | solution.py:39
  5.8 3.1 %collective-permute-start.2 = (bf16[16,128]{1,0:T(8,128)(2,1)S(1)}, bf16[16,128]{1,0:T(8,128)(2,1)S(1)}, u32[]{:S(2)}, u32[]{:S(2)}) collective-permute-start(bf16[16,128]{1,0:T(8,128)(2,1)S(1)} %pad_maximum_fusion.1), channel_id=1, source_target_pairs={{0,5},{1,4},{2,7},{3,6},{4,1},{5,0},{6,3},{7,2},{8,13},{9,12},{10,... | collective-permute-start | bytes 12296 | tf_op jit(solution)/shard_map/ppermute | solution.py:39
  8.9 4.0 %collective-permute-start.3 = (bf16[32,128]{1,0:T(8,128)(2,1)S(1)}, bf16[32,128]{1,0:T(8,128)(2,1)S(1)}, u32[]{:S(2)}, u32[]{:S(2)}) collective-permute-start(bf16[32,128]{1,0:T(8,128)(2,1)S(1)} %pad_maximum_fusion.paths_ref), channel_id=1, source_target_pairs={{0,9},{1,8},{2,11},{3,10},{4,13},{5,12},{6,15},{7,14},{8,1},{9,0},... | collective-permute-start | bytes 24584 | tf_op jit(solution)/shard_map/ppermute | solution.py:39
  13.8 1.2 %collective-permute-start.4 = (f32[16,512]{1,0:T(8,128)S(1)}, f32[16,512]{1,0:T(8,128)S(1)}, u32[]{:S(2)}, u32[]{:S(2)}) collective-permute-start(f32[16,512]{1,0:T(8,128)S(1)} %get-tuple-element.21), channel_id=1, source_target_pairs={{0,1},{1,0},{2,3},{3,2},{4,5},{5,4},{6,7},{7,6},{8,9},{9,8},{10,11... | collective-permute-start | bytes 98312 | tf_op jit(solution)/shard_map/ppermute | solution.py:39
  15.0 1.5 %copy-start.1 = (f32[2,64]{1,0:T(2,128)S(1)}, f32[2,64]{1,0:T(2,128)}, u32[]{:S(2)}) copy-start(f32[2,64]{1,0:T(2,128)} %param.17) | copy-start | bytes 1540
  15.1 3.2 %collective-permute-start.5 = (f32[8,512]{1,0:T(8,128)S(1)}, f32[8,512]{1,0:T(8,128)S(1)}, u32[]{:S(2)}, u32[]{:S(2)}) collective-permute-start(f32[8,512]{1,0:T(8,128)S(1)} %slice.48), channel_id=1, source_target_pairs={{0,3},{1,2},{2,1},{3,0},{4,7},{5,6},{6,5},{7,4},{8,11},{9,10},{10,... | collective-permute-start | bytes 49160 | tf_op jit(solution)/shard_map/ppermute | solution.py:39
  18.3 3.1 %collective-permute-start.6 = (f32[4,512]{1,0:T(4,128)S(1)}, f32[4,512]{1,0:T(4,128)S(1)}, u32[]{:S(2)}, u32[]{:S(2)}) collective-permute-start(f32[4,512]{1,0:T(4,128)S(1)} %slice.50), channel_id=1, source_target_pairs={{0,5},{1,4},{2,7},{3,6},{4,1},{5,0},{6,3},{7,2},{8,13},{9,12},{10,... | collective-permute-start | bytes 24584 | tf_op jit(solution)/shard_map/ppermute | solution.py:39
  21.5 4.0 %collective-permute-start.7 = (f32[2,512]{1,0:T(2,128)S(1)}, f32[2,512]{1,0:T(2,128)S(1)}, u32[]{:S(2)}, u32[]{:S(2)}) collective-permute-start(f32[2,512]{1,0:T(2,128)S(1)} %pad_maximum_fusion.2), channel_id=1, source_target_pairs={{0,9},{1,8},{2,11},{3,10},{4,13},{5,12},{6,15},{7,14},{8,1},{9,0},... | collective-permute-start | bytes 12296 | tf_op jit(solution)/shard_map/ppermute | solution.py:39

commit v5 on v4

v5 whole, which is shorter than its diff:
```python
import jax
import jax.numpy as jnp
from jax import lax
from jax.experimental import pallas as pl
from jax.experimental.pallas import tpu as pltpu
from jax.sharding import PartitionSpec as P

F = 16
K = 32
DATES = 8
LAG = 2
LANES = 128
PATH_BLOCK = 32
VMEM = pl.BlockSpec(memory_space=pltpu.VMEM)
SMEM = pl.BlockSpec(memory_space=pltpu.SMEM)
HBM = pl.BlockSpec(memory_space=pltpu.HBM)
PARTS = 4


def call(kernel, outs, specs, flops, args, scratch=()):
    sizes = [a.size * a.dtype.itemsize for a in (*args, *outs)]
    return pl.pallas_call(
        kernel,
        out_shape=outs,
        in_specs=specs,
        out_specs=[VMEM] * len(outs),
        scratch_shapes=scratch,
        compiler_params=pltpu.CompilerParams(vmem_limit_bytes=24 * 2**20),
        cost_estimate=pl.CostEstimate(flops=flops, bytes_accessed=sum(sizes) if flops else 0, transcendentals=0),
    )(*args)


def in_hbm(x):
    return pltpu.with_memory_space_constraint(x, pltpu.HBM)


def swap(x, bit, count):
    return lax.ppermute(x, "trade", [(i, i ^ (bit | 1)) for i in range(count)])


def join(own, other, bit):
    upper = (lax.axis_index("trade") & bit) != 0
    return jnp.concatenate([jnp.where(upper, other, own), jnp.where(upper, own, other)], axis=0)


def rounds(count):
    bits = []
    bit = 2
    while bit < count:
        bits.append(bit)
        bit *= 2
    return bits + [1]


def offsets(index, count):
    result = jnp.zeros_like(index)
    top = count // 2
    for bit in rounds(count):
        result = result ^ jnp.where((index & top) != 0, bit | 1, 0)
        top //= 2
    return result


def parity(index, count):
    result = index & 1
    bit = 2
    while bit < count:
        result = result ^ jnp.where((index & bit) != 0, 1, 0)
        bit *= 2
    return result


def scatter_sums(kept, sent, count):
    near = kept.shape[1] // 2
    for bit in rounds(count)[:-1]:
        if bit == count // 2:
            sent = jnp.concatenate([sent[:, near:], sent[:, :near]], axis=1)
        x = kept + swap(sent, bit, count)
        half = x.shape[0] // 2
        kept, sent = x[:half], x[half:]
    return kept, swap(sent, 1, count)


def fetch_kernel(
    factors_hbm,
    coef_hbm,
    size_hbm,
    ids_hbm,
    owner_hbm,
    margin_hbm,
    limit_hbm,
    loadings_hbm,
    own_ref,
    used_ref,
    ids_ref,
    owner_ref,
    margin_ref,
    limits_ref,
    split_ref,
    coef_ref,
    size_ref,
    limit_ref,
    loadings_ref,
    sems,
):
    slots, width = coef_ref.shape
    step = slots // PARTS
    pairs = (
        (size_hbm, size_ref),
        (limit_hbm, limit_ref),
        (loadings_hbm, loadings_ref),
        (factors_hbm, own_ref),
        (ids_hbm, ids_ref),
        (owner_hbm, owner_ref),
        (margin_hbm, margin_ref),
    )
    small = [pltpu.make_async_copy(source, target, sems.at[PARTS + i]) for i, (source, target) in enumerate(pairs)]
    large = [
        pltpu.make_async_copy(
            coef_hbm.at[pl.ds(i * step, step), :], coef_ref.at[pl.ds(i * step, step), :], sems.at[i]
        )
        for i in range(PARTS)
    ]
    for copy in small[:3] + large + small[3:]:
        copy.start()
    for copy in small[:3]:
        copy.wait()
    for r in range(limits_ref.shape[0]):
        limits_ref[r : r + 1, :] = jnp.full((1, LANES), limit_ref[r])
    tall = jnp.concatenate([loadings_ref[...]] * DATES, axis=0)
    wide = jnp.concatenate([tall] * DATES, axis=1)
    row = lax.broadcasted_iota(jnp.int32, wide.shape, 0) // F
    column = lax.broadcasted_iota(jnp.int32, wide.shape, 1) // K
    rest = jnp.where(row == column, wide, 0.0)
    for i in range(3):
        part = rest.astype(jnp.bfloat16)
        split_ref[i] = part
        rest = rest - part.astype(jnp.float32)
    sizes = size_ref[...].astype(jnp.float32).T
    basis = (lax.broadcasted_iota(jnp.int32, (1, width), 1) & (K - 1)).astype(jnp.float32)
    for i in range(PARTS):
        large[i].wait()
        for c in range(i * step // LANES, (i + 1) * step // LANES):
            rows = slice(c * LANES, (c + 1) * LANES)
            coef = coef_ref[rows, :].astype(jnp.float32)
            used_ref[rows, :] = jnp.where(basis < sizes[:, c : c + 1], coef, 0.0).astype(jnp.bfloat16)
    for copy in small[3:]:
        copy.wait()


def write_onehot(code, set_at, hot_ref):
    for c in range(code.shape[0]):
        hit = jnp.where(code[c : c + 1, :] == set_at, 1.0, 0.0)
        hot_ref[:, c * LANES : (c + 1) * LANES] = hit.astype(jnp.bfloat16)


def rows_kernel(count, own_rows, me_ref, live_ref, ids_ref, owner_ref, set_ref, hot_ref, code_ref):
    set_total = owner_ref.shape[1]
    place = lax.broadcasted_iota(jnp.int32, (set_total, 1), 0)
    block = lax.shift_right_logical(place, own_rows.bit_length() - 1)
    row_at = (offsets(block, count) ^ me_ref[0]) * own_rows + (place & (own_rows - 1))
    sets = lax.broadcasted_iota(jnp.int32, (set_total, set_total), 1)
    set_at = jnp.sum(jnp.where(row_at == owner_ref[...], sets, 0), axis=1, keepdims=True)
    set_ref[...] = jnp.broadcast_to(set_at, set_ref.shape)
    shape = ids_ref.shape
    slot = lax.broadcasted_iota(jnp.int32, shape, 0) * LANES + lax.broadcasted_iota(jnp.int32, shape, 1)
    code = jnp.where(slot < live_ref[0], ids_ref[...], -1)
    code_ref[...] = code
    write_onehot(code, set_at, hot_ref)


def other_rows_kernel(set_ref, code_ref, hot_ref):
    write_onehot(code_ref[...], set_ref[:, :1], hot_ref)


def net_block(paths, split_ref, trades):
    total = paths.shape[0]
    loaded = sum(jnp.dot(paths, split_ref[i], preferred_element_type=jnp.float32) for i in (2, 1, 0))
    tiled = jnp.concatenate([jnp.tanh(loaded)] * DATES, axis=0)
    row = lax.broadcasted_iota(jnp.int32, tiled.shape, 0) // total
    column = lax.broadcasted_iota(jnp.int32, tiled.shape, 1) // K
    table = jnp.where(row == column, tiled, 0.0).astype(jnp.bfloat16)
    result = 0.0
    for used_ref, onehot_ref in trades:
        values = lax.dot_general(
            used_ref[...],
            table,
            (((1,), (1,)), ((), ())),
            preferred_element_type=jnp.float32,
        )
        values = values.astype(jnp.bfloat16)
        result = result + jnp.dot(onehot_ref[...], values, preferred_element_type=jnp.float32)
    return result


def near_kernel(paths_ref, split_ref, used_ref, other_ref, onehot_ref, other_hot_ref, net_ref):
    trades = ((used_ref, onehot_ref), (other_ref, other_hot_ref))
    block = min(PATH_BLOCK, paths_ref.shape[0])
    for b in range(paths_ref.shape[0] // block):
        net = net_block(paths_ref[b * block : (b + 1) * block, :], split_ref, trades)
        net_ref[:, b * DATES * block : (b + 1) * DATES * block] = net


def far_kernel(
    paths_ref, split_ref, used_ref, other_ref, onehot_ref, other_hot_ref, near_ref, kept_ref, sent_ref
):
    half = kept_ref.shape[0]
    width = near_ref.shape[1]
    kept_ref[:, :width] = near_ref[:half, :]
    sent_ref[:, :width] = near_ref[half:, :]
    trades = ((used_ref, onehot_ref), (other_ref, other_hot_ref))
    block = min(PATH_BLOCK, paths_ref.shape[0])
    for b in range(paths_ref.shape[0] // block):
        net = net_block(paths_ref[b * block : (b + 1) * block, :], split_ref, trades)
        at = width + b * DATES * block
        kept_ref[:, at : at + DATES * block] = net[:half, :]
        sent_ref[:, at : at + DATES * block] = net[half:, :]


def body(
    factors,
    loadings,
    trade_coef,
    basis_size,
    set_ids,
    live_count,
    netting_row,
    threshold,
    margin_start,
    *,
    count,
):
    me = lax.axis_index("trade")
    own_rows = threshold.shape[0]
    set_total = netting_row.shape[0]
    slot_total, width = trade_coef.shape
    shape = jax.ShapeDtypeStruct
    f32, bf16 = jnp.float32, jnp.bfloat16

    sizes = basis_size.reshape(-1, LANES)
    ids = set_ids.reshape(-1, LANES)
    owner = netting_row.reshape(1, -1)
    turned = loadings.T
    own, used, ids, owner, margin, limits, split = call(
        fetch_kernel,
        [
            shape(factors.shape, bf16),
            shape(trade_coef.shape, bf16),
            shape(ids.shape, jnp.int32),
            shape(owner.shape, jnp.int32),
            shape(margin_start.shape, f32),
            shape((own_rows, LANES), f32),
            shape((3, DATES * F, DATES * K), bf16),
        ],
        [HBM] * 8,
        10**8,
        tuple(map(in_hbm, (factors, trade_coef, sizes, ids, owner, margin_start, threshold, turned))),
        [
            pltpu.VMEM(trade_coef.shape, bf16),
            pltpu.VMEM(sizes.shape, jnp.int32),
            pltpu.SMEM(threshold.shape, f32),
            pltpu.VMEM(turned.shape, f32),
            pltpu.SemaphoreType.DMA((PARTS + 7,)),
        ],
    )
    near = join(own, swap(factors, 2, count), 2)
    used, ids, live_count, near = lax.optimization_barrier((used, ids, live_count, near))
    other = swap(used, 1, count)
    set_at, onehot, code = call(
        lambda *refs: rows_kernel(count, own_rows, *refs),
        [
            shape((set_total, LANES), jnp.int32),
            shape((set_total, slot_total), bf16),
            shape(ids.shape, jnp.int32),
        ],
        [SMEM] * 2 + [VMEM] * 2,
        0,
        (me.astype(jnp.int32).reshape(1), live_count, ids, owner),
    )
    (other_hot,) = call(
        other_rows_kernel,
        [shape((set_total, slot_total), bf16)],
        [VMEM] * 2,
        10**8,
        (set_at, swap(code, 1, count)),
    )
    bit = 4
    while bit < count // 2:
        near = join(near, swap(near, bit, count), bit)
        bit *= 2
    far = swap(near, bit, count)
    side_total = near.shape[0]
    columns = DATES * side_total
    work = 4 * columns * slot_total * (width + set_total)
    (near_net,) = call(
        near_kernel,
        [shape((set_total, columns), f32)],
        [VMEM] * 6,
        work,
        (near, split, used, other, onehot, other_hot),
    )
    kept, sent = call(
        far_kernel,
        [shape((set_total // 2, 2 * columns), f32)] * 2,
        [VMEM] * 7,
        work,
        (far, split, used, other, onehot, other_hot, near_net),
    )
    margin, limits, me, kept = lax.optimization_barrier((margin, limits, me, kept))
    sums = scatter_sums(kept, sent, count)

    pairs = margin.reshape(own_rows, count // 2, 2, -1)
    odd = parity(2 * jnp.arange(count // 2, dtype=jnp.int32) ^ me, count)[:, None] != 0
    first, second = pairs[:, :, 0], pairs[:, :, 1]
    upper = (me & (count // 2)) != 0
    block = min(PATH_BLOCK, side_total)
    total = 0.0
    for netted, start in zip(sums, (jnp.where(odd, second, first), jnp.where(odd, first, second))):
        start = start.reshape(own_rows, 2, -1)
        start = jnp.where(upper, start[:, ::-1], start).reshape(own_rows, -1, 1, block)
        netted = netted.reshape(own_rows, -1, DATES, block)
        excess = jnp.maximum(netted[:, :, : DATES - LAG] - limits[:, :1, None, None], 0.0)
        held = jnp.broadcast_to(start, (own_rows, start.shape[1], LAG, block))
        collateral = jnp.concatenate([held, excess], axis=2)
        total = total + jnp.sum(jnp.maximum(netted - collateral, 0.0), axis=(1, 3))
    return total / (4 * side_total)


def solution(mesh):
    count = mesh.shape["trade"]

    def local(*args):
        return body(*args, count=count)

    return jax.shard_map(
        local,
        mesh=mesh,
        in_specs=(
            P(("group", "trade"), None),
            P(),
            P(("group", "trade"), None),
            P(("group", "trade")),
            P(("group", "trade")),
            P(("group", "trade")),
            P("group"),
            P(("group", "trade")),
            P(("group", "trade"), None),
        ),
        out_specs=P(("group", "trade"), None),
        check_vma=False,
    )
```

time: 26.5 us -> 25.9 us (0.977)
  waiting for transfers between devices: 6.84 us -> 5.86 us
  local copies, waits for them, and re-layouts: 0.39 us -> 0.82 us
  starting transfers between devices: 13.2 us -> 13.5 us
    ppermute x8 -> x9, waiting for transfers between devices: 6.84 us -> 5.86 us  [swap(): return lax.ppermute(x, 'trade', [(i, i ^ (bit | 1)) for i in range(count)])]
    ppermute x8 -> x9, starting transfers between devices: 13.2 us -> 13.5 us  [swap(): return lax.ppermute(x, 'trade', [(i, i ^ (bit | 1)) for i in range(count)])]
  transfers between devices with their start and end apart: 8 -> 9, of which waited for: 7 -> 6; matrix products, arithmetic and copies ran while one was open for 1% -> 1% of each run, Pallas kernels for 13% -> 11%
where the time goes in v5:
time: 25.9 us; the launch traced here: 25.7 us
  starting transfers between devices  13.5 us (52%)
  waiting for transfers between devices  5.86 us (23%)
  Pallas kernels  4 us (15%)
  other arithmetic  0.82 us (3%)
  local copies, waits for them, and re-layouts  0.82 us (3%)
  between operations  0.77 us (3%)
    ppermute x9, starting transfers between devices, swap(): return lax.ppermute(x, 'trade', [(i, i ^ (bit | 1)) for i in range(count)])  13.5 us
    ppermute x9, waiting for transfers between devices, swap(): return lax.ppermute(x, 'trade', [(i, i ^ (bit | 1)) for i in range(count)])  5.86 us
    pallas_call x5, Pallas kernels, call(): pl.pallas_call(kernel, out_shape=outs, in_specs=specs, out_specs=[VMEM] *...  4 us
    div x1, other arithmetic, body(): return total / (4 * side_total)  0.57 us
  transfers between devices with their start and end apart: 9, of which 6 were waited for; matrix products, arithmetic and copies ran while one was open for 1% of the time, Pallas kernels for 11%

profile of v5, /device:TPU:0, one launch (start us, length us, event | category | flops | bytes accessed | tf_op | source)
XLA Modules:
  0.0 25.7 jit_solution(2700118146167042771)
XLA Ops:
  0.0 2.4 %collective-permute-start = (bf16[4,128]{1,0:T(4,128)(2,1)}, bf16[4,128]{1,0:T(4,128)(2,1)S(1)}, u32[]{:S(2)}, u32[]{:S(2)}) collective-permute-start(bf16[4,128]{1,0:T(4,128)(2,1)} %factors_hbm.1), channel_id=1, source_target_pairs={{0,3},{1,2},{2,1},{3,0},{4,7},{5,6},{6,5},{7,4},{8,11},{9,10},{10,... | collective-permute-start | bytes 3080 | tf_op jit(solution)/shard_map/ppermute | solution.py:38
  2.4 1.6 %shard_map.91 = (bf16[4,128]{1,0:T(4,128)(2,1)S(1)}, bf16[2048,256]{1,0:T(8,128)(2,1)S(1)}, s32[16,128]{1,0:T(8,128)S(1)}, s32[1,32]{1,0:T(1,128)S(1)}, f32[2,64...) custom-call(bf16[4,128]{1,0:T(4,128)(2,1)} %factors_hbm.1, bf16[2048,256]{1,0:T(8,128)(2,1)} %coef_hbm.1, ...), custom_call_target="tpu_custom_call" | custom-call | flops 100000000 | bytes 2324744 | tf_op jit(solution)/shard_map/pallas_call | solution.py:22
  4.1 0.7 %collective-permute-start.3 = (bf16[2048,256]{1,0:T(8,128)(2,1)S(1)}, bf16[2048,256]{1,0:T(8,128)(2,1)S(1)}, u32[]{:S(2)}, u32[]{:S(2)}) collective-permute-start(bf16[2048,256]{1,0:T(8,128)(2,1)S(1)} %get-tuple-element.32.used_ref), channel_id=1, source_target_pairs={{0,1},{1,0},{2,3},{3,2},{4,5},{5,4},{6,7},{7,6},{8,9},{9,8},{10,11... | collective-permute-start | bytes 3145736 | tf_op jit(solution)/shard_map/ppermute | solution.py:38
  4.9 1.6 %collective-permute-start.1 = (bf16[8,128]{1,0:T(8,128)(2,1)S(1)}, bf16[8,128]{1,0:T(8,128)(2,1)S(1)}, u32[]{:S(2)}, u32[]{:S(2)}) collective-permute-start(bf16[8,128]{1,0:T(8,128)(2,1)S(1)} %pad_maximum_fusion.2), channel_id=1, source_target_pairs={{0,5},{1,4},{2,7},{3,6},{4,1},{5,0},{6,3},{7,2},{8,13},{9,12},{10,... | collective-permute-start | bytes 6152 | tf_op jit(solution)/shard_map/ppermute | solution.py:38
  7.1 0.1 shard_map.92
  7.2 0.2 collective-permute-start.4
  7.4 0.4 %collective-permute-done.1 = bf16[8,128]{1,0:T(8,128)(2,1)S(1)} collective-permute-done((bf16[8,128]{1,0:T(8,128)(2,1)S(1)}, bf16[8,128]{1,0:T(8,128)(2,1)S(1)}, u32[]{:S(2)}, u32[]{:S(2)}) %collective-permute-start.1) | collective-permute-done | bytes 2080 | tf_op jit(solution)/shard_map/ppermute | solution.py:38
  7.9 2.7 %collective-permute-start.2 = (bf16[16,128]{1,0:T(8,128)(2,1)S(1)}, bf16[16,128]{1,0:T(8,128)(2,1)S(1)}, u32[]{:S(2)}, u32[]{:S(2)}) collective-permute-start(bf16[16,128]{1,0:T(8,128)(2,1)S(1)} %pad_maximum_fusion.paths_ref), channel_id=1, source_target_pairs={{0,9},{1,8},{2,11},{3,10},{4,13},{5,12},{6,15},{7,14},{8,1},{9,0},... | collective-permute-start | bytes 12296 | tf_op jit(solution)/shard_map/ppermute | solution.py:38
  10.5 0.1 shard_map.93.other_hot_ref
  10.6 1.1 %shard_map.94.near_ref = f32[32,128]{1,0:T(8,128)S(1)} custom-call(bf16[16,128]{1,0:T(8,128)(2,1)S(1)} %pad_maximum_fusion.paths_ref, bf16[3,128,256]{2,1,0:T(8,128)(2,1)S(1)} %get-tuple-element.31.split_ref, bf16[2048,256]{1,0:T(8,128)(2,1)S(1)} %get-tuple-element.32.used_ref, bf16[2048,256]{1,0:T(8,128)(2,1)S(1)} %collective-permute-done.3.other_ref, ...), custom_call_target="tpu_custom_call" | custom-call | flops 301989888 | bytes 2576384 | tf_op jit(solution)/shard_map/pallas_call | solution.py:22
  11.7 0.2 collective-permute-done.2.paths_ref
  11.9 1.1 %shard_map.95 = (f32[16,256]{1,0:T(8,128)S(1)}, f32[16,256]{1,0:T(8,128)S(1)}) custom-call(bf16[16,128]{1,0:T(8,128)(2,1)S(1)} %collective-permute-done.2.paths_ref, bf16[3,128,256]{2,1,0:T(8,128)(2,1)S(1)} %get-tuple-element.31.split_ref, bf16[2048,256]{1,0:T(8,128)(2,1)S(1)} %get-tuple-element.32.used_ref, ...), custom_call_target="tpu_custom_call" | custom-call | flops 301989888 | bytes 2609152 | tf_op jit(solution)/shard_map/pallas_call | solution.py:22
  13.1 0.1 reshape.47
  13.4 1.5 %collective-permute-start.5 = (f32[16,256]{1,0:T(8,128)S(1)}, f32[16,256]{1,0:T(8,128)S(1)}, u32[]{:S(2)}, u32[]{:S(2)}) collective-permute-start(f32[16,256]{1,0:T(8,128)S(1)} %get-tuple-element.41), channel_id=1, source_target_pairs={{0,3},{1,2},{2,1},{3,0},{4,7},{5,6},{6,5},{7,4},{8,11},{9,10},{10,... | collective-permute-start | bytes 49160 | tf_op jit(solution)/shard_map/ppermute | solution.py:38
  15.0 1.6 %collective-permute-done.5 = f32[16,256]{1,0:T(8,128)S(1)} collective-permute-done((f32[16,256]{1,0:T(8,128)S(1)}, f32[16,256]{1,0:T(8,128)S(1)}, u32[]{:S(2)}, u32[]{:S(2)}) %collective-permute-start.5) | collective-permute-done | bytes 16416 | tf_op jit(solution)/shard_map/ppermute | solution.py:38
  16.6 1.6 %collective-permute-start.6 = (f32[8,256]{1,0:T(8,128)S(1)}, f32[8,256]{1,0:T(8,128)S(1)}, u32[]{:S(2)}, u32[]{:S(2)}) collective-permute-start(f32[8,256]{1,0:T(8,128)S(1)} %slice.53), channel_id=1, source_target_pairs={{0,5},{1,4},{2,7},{3,6},{4,1},{5,0},{6,3},{7,2},{8,13},{9,12},{10,... | collective-permute-start | bytes 24584 | tf_op jit(solution)/shard_map/ppermute | solution.py:38
  18.2 1.5 %collective-permute-done.6 = f32[8,256]{1,0:T(8,128)S(1)} collective-permute-done((f32[8,256]{1,0:T(8,128)S(1)}, f32[8,256]{1,0:T(8,128)S(1)}, u32[]{:S(2)}, u32[]{:S(2)}) %collective-permute-start.6) | collective-permute-done | bytes 8224 | tf_op jit(solution)/shard_map/ppermute | solution.py:38
  19.7 2.6 %collective-permute-start.7 = (f32[4,256]{1,0:T(4,128)S(1)}, f32[4,256]{1,0:T(4,128)S(1)}, u32[]{:S(2)}, u32[]{:S(2)}) collective-permute-start(f32[4,256]{1,0:T(4,128)S(1)} %pad_maximum_fusion.1), channel_id=1, source_target_pairs={{0,9},{1,8},{2,11},{3,10},{4,13},{5,12},{6,15},{7,14},{8,1},{9,0},... | collective-permute-start | bytes 12296 | tf_op jit(solution)/shard_map/ppermute | solution.py:38
  22.4 1.3 %collective-permute-done.7 = f32[4,256]{1,0:T(4,128)S(1)} collective-permute-done((f32[4,256]{1,0:T(4,128)S(1)}, f32[4,256]{1,0:T(4,128)S(1)}, u32[]{:S(2)}, u32[]{:S(2)}) %collective-permute-start.7) | collective-permute-done | bytes 4128 | tf_op jit(solution)/shard_map/ppermute | solution.py:38
  23.7 0.1 collective-permute-start.8
  23.8 0.1 slice_reduce_fusion.2
  24.0 0.8 %collective-permute-done.8 = f32[2,256]{1,0:T(2,128)S(1)} collective-permute-done((f32[2,256]{1,0:T(2,128)S(1)}, f32[2,256]{1,0:T(2,128)S(1)}, u32[]{:S(2)}, u32[]{:S(2)}) %collective-permute-start.8) | collective-permute-done | bytes 2080 | tf_op jit(solution)/shard_map/ppermute | solution.py:38
  25.0 0.1 fusion.3
  25.1 0.6 %add_multiply_fusion = f32[2,8]{1,0:T(2,128)} fusion(f32[2,8]{1,0:T(2,128)S(1)} %get-tuple-element.59, f32[2,8]{1,0:T(2,128)S(1)} %get-tuple-element.60), kind=kLoop, calls=%fused_computation.29 | loop fusion | flops 32 | bytes 192 | tf_op jit(solution)/shard_map/div | solution.py:326
  (30 shorter events, 0.8 us)
Async XLA Ops:
  0.0 4.1 %collective-permute-start = (bf16[4,128]{1,0:T(4,128)(2,1)}, bf16[4,128]{1,0:T(4,128)(2,1)S(1)}, u32[]{:S(2)}, u32[]{:S(2)}) collective-permute-start(bf16[4,128]{1,0:T(4,128)(2,1)} %factors_hbm.1), channel_id=1, source_target_pairs={{0,3},{1,2},{2,1},{3,0},{4,7},{5,6},{6,5},{7,4},{8,11},{9,10},{10,... | collective-permute-start | bytes 3080 | tf_op jit(solution)/shard_map/ppermute | solution.py:38
  4.1 6.5 %collective-permute-start.3 = (bf16[2048,256]{1,0:T(8,128)(2,1)S(1)}, bf16[2048,256]{1,0:T(8,128)(2,1)S(1)}, u32[]{:S(2)}, u32[]{:S(2)}) collective-permute-start(bf16[2048,256]{1,0:T(8,128)(2,1)S(1)} %get-tuple-element.32.used_ref), channel_id=1, source_target_pairs={{0,1},{1,0},{2,3},{3,2},{4,5},{5,4},{6,7},{7,6},{8,9},{9,8},{10,11... | collective-permute-start | bytes 3145736 | tf_op jit(solution)/shard_map/ppermute | solution.py:38
  4.9 3.0 %collective-permute-start.1 = (bf16[8,128]{1,0:T(8,128)(2,1)S(1)}, bf16[8,128]{1,0:T(8,128)(2,1)S(1)}, u32[]{:S(2)}, u32[]{:S(2)}) collective-permute-start(bf16[8,128]{1,0:T(8,128)(2,1)S(1)} %pad_maximum_fusion.2), channel_id=1, source_target_pairs={{0,5},{1,4},{2,7},{3,6},{4,1},{5,0},{6,3},{7,2},{8,13},{9,12},{10,... | collective-permute-start | bytes 6152 | tf_op jit(solution)/shard_map/ppermute | solution.py:38
  7.2 3.3 %collective-permute-start.4 = (s32[16,128]{1,0:T(8,128)S(1)}, s32[16,128]{1,0:T(8,128)S(1)}, u32[]{:S(2)}, u32[]{:S(2)}) collective-permute-start(s32[16,128]{1,0:T(8,128)S(1)} %get-tuple-element.38), channel_id=1, source_target_pairs={{0,1},{1,0},{2,3},{3,2},{4,5},{5,4},{6,7},{7,6},{8,9},{9,8},{10,11... | collective-permute-start | bytes 24584 | tf_op jit(solution)/shard_map/ppermute | solution.py:38
  7.9 4.0 %collective-permute-start.2 = (bf16[16,128]{1,0:T(8,128)(2,1)S(1)}, bf16[16,128]{1,0:T(8,128)(2,1)S(1)}, u32[]{:S(2)}, u32[]{:S(2)}) collective-permute-start(bf16[16,128]{1,0:T(8,128)(2,1)S(1)} %pad_maximum_fusion.paths_ref), channel_id=1, source_target_pairs={{0,9},{1,8},{2,11},{3,10},{4,13},{5,12},{6,15},{7,14},{8,1},{9,0},... | collective-permute-start | bytes 12296 | tf_op jit(solution)/shard_map/ppermute | solution.py:38
  13.4 3.2 %collective-permute-start.5 = (f32[16,256]{1,0:T(8,128)S(1)}, f32[16,256]{1,0:T(8,128)S(1)}, u32[]{:S(2)}, u32[]{:S(2)}) collective-permute-start(f32[16,256]{1,0:T(8,128)S(1)} %get-tuple-element.41), channel_id=1, source_target_pairs={{0,3},{1,2},{2,1},{3,0},{4,7},{5,6},{6,5},{7,4},{8,11},{9,10},{10,... | collective-permute-start | bytes 49160 | tf_op jit(solution)/shard_map/ppermute | solution.py:38
  16.6 3.1 %collective-permute-start.6 = (f32[8,256]{1,0:T(8,128)S(1)}, f32[8,256]{1,0:T(8,128)S(1)}, u32[]{:S(2)}, u32[]{:S(2)}) collective-permute-start(f32[8,256]{1,0:T(8,128)S(1)} %slice.53), channel_id=1, source_target_pairs={{0,5},{1,4},{2,7},{3,6},{4,1},{5,0},{6,3},{7,2},{8,13},{9,12},{10,... | collective-permute-start | bytes 24584 | tf_op jit(solution)/shard_map/ppermute | solution.py:38
  19.7 4.0 %collective-permute-start.7 = (f32[4,256]{1,0:T(4,128)S(1)}, f32[4,256]{1,0:T(4,128)S(1)}, u32[]{:S(2)}, u32[]{:S(2)}) collective-permute-start(f32[4,256]{1,0:T(4,128)S(1)} %pad_maximum_fusion.1), channel_id=1, source_target_pairs={{0,9},{1,8},{2,11},{3,10},{4,13},{5,12},{6,15},{7,14},{8,1},{9,0},... | collective-permute-start | bytes 12296 | tf_op jit(solution)/shard_map/ppermute | solution.py:38
  23.7 1.2 %collective-permute-start.8 = (f32[2,256]{1,0:T(2,128)S(1)}, f32[2,256]{1,0:T(2,128)S(1)}, u32[]{:S(2)}, u32[]{:S(2)}) collective-permute-start(f32[2,256]{1,0:T(2,128)S(1)} %get-tuple-element.51), channel_id=1, source_target_pairs={{0,1},{1,0},{2,3},{3,2},{4,5},{5,4},{6,7},{7,6},{8,9},{9,8},{10,11... | collective-permute-start | bytes 6152 | tf_op jit(solution)/shard_map/ppermute | solution.py:38

commit v6 on v5

--- a/solution.py
+++ b/solution.py
@@ -154,7 +154,60 @@
         hot_ref[:, c * LANES : (c + 1) * LANES] = hit.astype(jnp.bfloat16)
 
 
-def rows_kernel(count, own_rows, me_ref, live_ref, ids_ref, owner_ref, set_ref, hot_ref, code_ref):
+def held_margin(count, me, margin, held_ref):
+    path_total = margin.shape[1]
+    own = path_total // count
+    side = path_total // 4
+    block = min(PATH_BLOCK, side)
+    columns = DATES * block
+    lane = lax.broadcasted_iota(jnp.int32, (1, columns), 1)
+    source = lax.broadcasted_iota(jnp.int32, (path_total, 1), 0)
+    mine = parity(me, count)
+    far_bit = jnp.where((me & (count // 2)) != 0, 1, 0)
+    inner = lane - (lane // block) * block
+    at = 0
+    for other in range(2):
+        for half in range(2):
+            for b in range(side // block):
+                place = b * block + inner
+                device = place // own
+                chip = (far_bit ^ half) * (count // 4) + device
+                core = parity(chip, count) ^ mine ^ other
+                wanted = (2 * chip + core) * own + (place - device * own)
+                pick = jnp.where(source == wanted, 1.0, 0.0)
+                held_ref[:, at : at + columns] = jnp.dot(
+                    margin, pick, precision=lax.Precision.HIGHEST, preferred_element_type=jnp.float32
+                )
+                at += columns
+
+
+def final_kernel(own_ref, other_ref, held_ref, limits_ref, out_ref):
+    rows, width = own_ref.shape
+    side = width // (2 * DATES)
+    block = min(PATH_BLOCK, side)
+    columns = DATES * block
+    limit = jnp.broadcast_to(limits_ref[:, :1], (rows, columns))
+    lane = lax.broadcasted_iota(jnp.int32, (rows, columns), 1)
+    total = jnp.zeros((rows, columns), jnp.float32)
+    at = 0
+    for net_ref in (own_ref, other_ref):
+        for b in range(width // columns):
+            netted = net_ref[:, b * columns : (b + 1) * columns]
+            before = pltpu.roll(netted, LAG * block, 1)
+            margin = jnp.maximum(before - limit, 0.0)
+            collateral = jnp.where(lane < LAG * block, held_ref[:, at : at + columns], margin)
+            total = total + jnp.maximum(netted - collateral, 0.0)
+            at += columns
+    date = lax.broadcasted_iota(jnp.int32, (columns, DATES), 0) // block
+    pick = jnp.where(date == lax.broadcasted_iota(jnp.int32, (columns, DATES), 1), 1.0, 0.0)
+    out = jnp.dot(total, pick, precision=lax.Precision.HIGHEST, preferred_element_type=jnp.float32)
+    out_ref[...] = out / (4 * side)
+
+
+def rows_kernel(
+    count, own_rows, me_ref, live_ref, ids_ref, owner_ref, margin_ref, set_ref, hot_ref, code_ref, held_ref
+):
+    held_margin(count, me_ref[0], margin_ref[...], held_ref)
     set_total = owner_ref.shape[1]
     place = lax.broadcasted_iota(jnp.int32, (set_total, 1), 0)
     block = lax.shift_right_logical(place, own_rows.bit_length() - 1)
@@ -266,16 +319,17 @@
     near = join(own, swap(factors, 2, count), 2)
     used, ids, live_count, near = lax.optimization_barrier((used, ids, live_count, near))
     other = swap(used, 1, count)
-    set_at, onehot, code = call(
+    set_at, onehot, code, held = call(
         lambda *refs: rows_kernel(count, own_rows, *refs),
         [
             shape((set_total, LANES), jnp.int32),
             shape((set_total, slot_total), bf16),
             shape(ids.shape, jnp.int32),
+            shape((own_rows, DATES * margin_start.shape[1]), f32),
         ],
-        [SMEM] * 2 + [VMEM] * 2,
+        [SMEM] * 2 + [VMEM] * 3,
         0,
-        (me.astype(jnp.int32).reshape(1), live_count, ids, owner),
+        (me.astype(jnp.int32).reshape(1), live_count, ids, owner, margin),
     )
     (other_hot,) = call(
         other_rows_kernel,
@@ -306,24 +360,15 @@
         work,
         (far, split, used, other, onehot, other_hot, near_net),
     )
-    margin, limits, me, kept = lax.optimization_barrier((margin, limits, me, kept))
-    sums = scatter_sums(kept, sent, count)
-
-    pairs = margin.reshape(own_rows, count // 2, 2, -1)
-    odd = parity(2 * jnp.arange(count // 2, dtype=jnp.int32) ^ me, count)[:, None] != 0
-    first, second = pairs[:, :, 0], pairs[:, :, 1]
-    upper = (me & (count // 2)) != 0
-    block = min(PATH_BLOCK, side_total)
-    total = 0.0
-    for netted, start in zip(sums, (jnp.where(odd, second, first), jnp.where(odd, first, second))):
-        start = start.reshape(own_rows, 2, -1)
-        start = jnp.where(upper, start[:, ::-1], start).reshape(own_rows, -1, 1, block)
-        netted = netted.reshape(own_rows, -1, DATES, block)
-        excess = jnp.maximum(netted[:, :, : DATES - LAG] - limits[:, :1, None, None], 0.0)
-        held = jnp.broadcast_to(start, (own_rows, start.shape[1], LAG, block))
-        collateral = jnp.concatenate([held, excess], axis=2)
-        total = total + jnp.sum(jnp.maximum(netted - collateral, 0.0), axis=(1, 3))
-    return total / (4 * side_total)
+    own_net, other_net = scatter_sums(kept, sent, count)
+    (expected,) = call(
+        final_kernel,
+        [shape((own_rows, DATES), f32)],
+        [VMEM] * 4,
+        10**6,
+        (own_net, other_net, held, limits),
+    )
+    return expected
 
 
 def solution(mesh):

time: 25.9 us -> 25.4 us (0.981)
  Pallas kernels: 4 us -> 4.91 us
  local copies, waits for them, and re-layouts: 0.82 us -> 0.02 us
  other arithmetic: 0.82 us -> 0.05 us
    pallas_call x5 -> x6, Pallas kernels: 4 us -> 4.91 us  [call(): pl.pallas_call(kernel, out_shape=outs, in_specs=specs, out_specs=[VMEM] *...]
    div x1 -> x0, other arithmetic: 0.57 us -> none  [body(): return total / (4 * side_total)]
  transfers between devices with their start and end apart: 9 -> 9, of which waited for: 6 -> 6; matrix products, arithmetic and copies ran while one was open for 1% -> 0% of each run, Pallas kernels for 11% -> 12%
where the time goes in v6:
time: 25.4 us; the launch traced here: 25.2 us
  starting transfers between devices  13.5 us (53%)
  waiting for transfers between devices  6.06 us (24%)
  Pallas kernels  4.91 us (19%)
  between operations  0.73 us (3%)
    ppermute x9, starting transfers between devices, swap(): return lax.ppermute(x, 'trade', [(i, i ^ (bit | 1)) for i in range(count)])  13.5 us
    ppermute x9, waiting for transfers between devices, swap(): return lax.ppermute(x, 'trade', [(i, i ^ (bit | 1)) for i in range(count)])  6.06 us
    pallas_call x6, Pallas kernels, call(): pl.pallas_call(kernel, out_shape=outs, in_specs=specs, out_specs=[VMEM] *...  4.91 us
  transfers between devices with their start and end apart: 9, of which 6 were waited for; matrix products, arithmetic and copies ran while one was open for 0% of the time, Pallas kernels for 12%

profile of v6, /device:TPU:0, one launch (start us, length us, event | category | flops | bytes accessed | tf_op | source)
XLA Modules:
  0.0 25.2 jit_solution(3427282426029453529)
XLA Ops:
  0.0 2.4 %collective-permute-start = (bf16[4,128]{1,0:T(4,128)(2,1)}, bf16[4,128]{1,0:T(4,128)(2,1)S(1)}, u32[]{:S(2)}, u32[]{:S(2)}) collective-permute-start(bf16[4,128]{1,0:T(4,128)(2,1)} %factors_hbm.1), channel_id=1, source_target_pairs={{0,3},{1,2},{2,1},{3,0},{4,7},{5,6},{6,5},{7,4},{8,11},{9,10},{10,... | collective-permute-start | bytes 3080 | tf_op jit(solution)/shard_map/ppermute | solution.py:38
  2.4 1.6 %shard_map.91 = (bf16[4,128]{1,0:T(4,128)(2,1)S(1)}, bf16[2048,256]{1,0:T(8,128)(2,1)S(1)}, s32[16,128]{1,0:T(8,128)S(1)}, s32[1,32]{1,0:T(1,128)S(1)}, f32[2,64...) custom-call(bf16[4,128]{1,0:T(4,128)(2,1)} %factors_hbm.1, bf16[2048,256]{1,0:T(8,128)(2,1)} %coef_hbm.1, ...), custom_call_target="tpu_custom_call" | custom-call | flops 100000000 | bytes 2324744 | tf_op jit(solution)/shard_map/pallas_call | solution.py:22
  4.1 0.0 collective-permute-done
  4.1 0.7 %collective-permute-start.3 = (bf16[2048,256]{1,0:T(8,128)(2,1)S(1)}, bf16[2048,256]{1,0:T(8,128)(2,1)S(1)}, u32[]{:S(2)}, u32[]{:S(2)}) collective-permute-start(bf16[2048,256]{1,0:T(8,128)(2,1)S(1)} %get-tuple-element.27.used_ref), channel_id=1, source_target_pairs={{0,1},{1,0},{2,3},{3,2},{4,5},{5,4},{6,7},{7,6},{8,9},{9,8},{10,11... | collective-permute-start | bytes 3145736 | tf_op jit(solution)/shard_map/ppermute | solution.py:38
  4.9 1.6 %collective-permute-start.1 = (bf16[8,128]{1,0:T(8,128)(2,1)S(1)}, bf16[8,128]{1,0:T(8,128)(2,1)S(1)}, u32[]{:S(2)}, u32[]{:S(2)}) collective-permute-start(bf16[8,128]{1,0:T(8,128)(2,1)S(1)} %pad_maximum_fusion.2), channel_id=1, source_target_pairs={{0,5},{1,4},{2,7},{3,6},{4,1},{5,0},{6,3},{7,2},{8,13},{9,12},{10,... | collective-permute-start | bytes 6152 | tf_op jit(solution)/shard_map/ppermute | solution.py:38
  7.1 0.2 shard_map.92
  7.3 0.2 collective-permute-start.4
  7.5 0.4 %collective-permute-done.1 = bf16[8,128]{1,0:T(8,128)(2,1)S(1)} collective-permute-done((bf16[8,128]{1,0:T(8,128)(2,1)S(1)}, bf16[8,128]{1,0:T(8,128)(2,1)S(1)}, u32[]{:S(2)}, u32[]{:S(2)}) %collective-permute-start.1) | collective-permute-done | bytes 2080 | tf_op jit(solution)/shard_map/ppermute | solution.py:38
  7.9 2.7 %collective-permute-start.2 = (bf16[16,128]{1,0:T(8,128)(2,1)S(1)}, bf16[16,128]{1,0:T(8,128)(2,1)S(1)}, u32[]{:S(2)}, u32[]{:S(2)}) collective-permute-start(bf16[16,128]{1,0:T(8,128)(2,1)S(1)} %pad_maximum_fusion.paths_ref), channel_id=1, source_target_pairs={{0,9},{1,8},{2,11},{3,10},{4,13},{5,12},{6,15},{7,14},{8,1},{9,0},... | collective-permute-start | bytes 12296 | tf_op jit(solution)/shard_map/ppermute | solution.py:38
  10.5 0.0 collective-permute-done.4.code_ref
  10.5 0.1 shard_map.93.other_hot_ref
  10.6 0.0 collective-permute-done.3.other_ref
  10.6 1.1 %shard_map.94.near_ref = f32[32,128]{1,0:T(8,128)S(1)} custom-call(bf16[16,128]{1,0:T(8,128)(2,1)S(1)} %pad_maximum_fusion.paths_ref, bf16[3,128,256]{2,1,0:T(8,128)(2,1)S(1)} %get-tuple-element.26.split_ref, bf16[2048,256]{1,0:T(8,128)(2,1)S(1)} %get-tuple-element.27.used_ref, bf16[2048,256]{1,0:T(8,128)(2,1)S(1)} %collective-permute-done.3.other_ref, ...), custom_call_target="tpu_custom_call" | custom-call | flops 301989888 | bytes 2576384 | tf_op jit(solution)/shard_map/pallas_call | solution.py:22
  11.7 0.2 collective-permute-done.2.paths_ref
  11.9 1.1 %shard_map.95 = (f32[16,256]{1,0:T(8,128)S(1)}, f32[16,256]{1,0:T(8,128)S(1)}) custom-call(bf16[16,128]{1,0:T(8,128)(2,1)S(1)} %collective-permute-done.2.paths_ref, bf16[3,128,256]{2,1,0:T(8,128)(2,1)S(1)} %get-tuple-element.26.split_ref, bf16[2048,256]{1,0:T(8,128)(2,1)S(1)} %get-tuple-element.27.used_ref, ...), custom_call_target="tpu_custom_call" | custom-call | flops 301989888 | bytes 2609152 | tf_op jit(solution)/shard_map/pallas_call | solution.py:22
  12.9 1.6 %collective-permute-start.5 = (f32[16,256]{1,0:T(8,128)S(1)}, f32[16,256]{1,0:T(8,128)S(1)}, u32[]{:S(2)}, u32[]{:S(2)}) collective-permute-start(f32[16,256]{1,0:T(8,128)S(1)} %get-tuple-element.36), channel_id=1, source_target_pairs={{0,3},{1,2},{2,1},{3,0},{4,7},{5,6},{6,5},{7,4},{8,11},{9,10},{10,... | collective-permute-start | bytes 49160 | tf_op jit(solution)/shard_map/ppermute | solution.py:38
  14.5 1.6 %collective-permute-done.5 = f32[16,256]{1,0:T(8,128)S(1)} collective-permute-done((f32[16,256]{1,0:T(8,128)S(1)}, f32[16,256]{1,0:T(8,128)S(1)}, u32[]{:S(2)}, u32[]{:S(2)}) %collective-permute-start.5) | collective-permute-done | bytes 16416 | tf_op jit(solution)/shard_map/ppermute | solution.py:38
  16.2 1.6 %collective-permute-start.6 = (f32[8,256]{1,0:T(8,128)S(1)}, f32[8,256]{1,0:T(8,128)S(1)}, u32[]{:S(2)}, u32[]{:S(2)}) collective-permute-start(f32[8,256]{1,0:T(8,128)S(1)} %slice.32), channel_id=1, source_target_pairs={{0,5},{1,4},{2,7},{3,6},{4,1},{5,0},{6,3},{7,2},{8,13},{9,12},{10,... | collective-permute-start | bytes 24584 | tf_op jit(solution)/shard_map/ppermute | solution.py:38
  17.8 1.5 %collective-permute-done.6 = f32[8,256]{1,0:T(8,128)S(1)} collective-permute-done((f32[8,256]{1,0:T(8,128)S(1)}, f32[8,256]{1,0:T(8,128)S(1)}, u32[]{:S(2)}, u32[]{:S(2)}) %collective-permute-start.6) | collective-permute-done | bytes 8224 | tf_op jit(solution)/shard_map/ppermute | solution.py:38
  19.3 2.6 %collective-permute-start.7 = (f32[4,256]{1,0:T(4,128)S(1)}, f32[4,256]{1,0:T(4,128)S(1)}, u32[]{:S(2)}, u32[]{:S(2)}) collective-permute-start(f32[4,256]{1,0:T(4,128)S(1)} %pad_maximum_fusion.1), channel_id=1, source_target_pairs={{0,9},{1,8},{2,11},{3,10},{4,13},{5,12},{6,15},{7,14},{8,1},{9,0},... | collective-permute-start | bytes 12296 | tf_op jit(solution)/shard_map/ppermute | solution.py:38
  21.9 1.3 %collective-permute-done.7 = f32[4,256]{1,0:T(4,128)S(1)} collective-permute-done((f32[4,256]{1,0:T(4,128)S(1)}, f32[4,256]{1,0:T(4,128)S(1)}, u32[]{:S(2)}, u32[]{:S(2)}) %collective-permute-start.7) | collective-permute-done | bytes 4128 | tf_op jit(solution)/shard_map/ppermute | solution.py:38
  23.3 0.1 collective-permute-start.8
  23.4 1.0 %collective-permute-done.8.other_ref = f32[2,256]{1,0:T(2,128)S(1)} collective-permute-done((f32[2,256]{1,0:T(2,128)S(1)}, f32[2,256]{1,0:T(2,128)S(1)}, u32[]{:S(2)}, u32[]{:S(2)}) %collective-permute-start.8) | collective-permute-done | bytes 2080 | tf_op jit(solution)/shard_map/ppermute | solution.py:38
  24.4 0.8 %shard_map.96 = f32[2,8]{1,0:T(2,128)} custom-call(f32[2,256]{1,0:T(2,128)S(1)} %get-tuple-element.42.own_ref, f32[2,256]{1,0:T(2,128)S(1)} %collective-permute-done.8.other_ref, f32[2,512]{1,0:T(2,128)S(1)} %get-tuple-element.37.held_ref, f32[2,128]{1,0:T(2,128)S(1)} %get-tuple-element.38.limits_ref), custom_call_target="tpu_custom_call" | custom-call | flops 1000000 | bytes 9280 | tf_op jit(solution)/shard_map/pallas_call | solution.py:22
  (11 shorter events, 0.1 us)
Async XLA Ops:
  0.0 4.1 %collective-permute-start = (bf16[4,128]{1,0:T(4,128)(2,1)}, bf16[4,128]{1,0:T(4,128)(2,1)S(1)}, u32[]{:S(2)}, u32[]{:S(2)}) collective-permute-start(bf16[4,128]{1,0:T(4,128)(2,1)} %factors_hbm.1), channel_id=1, source_target_pairs={{0,3},{1,2},{2,1},{3,0},{4,7},{5,6},{6,5},{7,4},{8,11},{9,10},{10,... | collective-permute-start | bytes 3080 | tf_op jit(solution)/shard_map/ppermute | solution.py:38
  4.1 6.5 %collective-permute-start.3 = (bf16[2048,256]{1,0:T(8,128)(2,1)S(1)}, bf16[2048,256]{1,0:T(8,128)(2,1)S(1)}, u32[]{:S(2)}, u32[]{:S(2)}) collective-permute-start(bf16[2048,256]{1,0:T(8,128)(2,1)S(1)} %get-tuple-element.27.used_ref), channel_id=1, source_target_pairs={{0,1},{1,0},{2,3},{3,2},{4,5},{5,4},{6,7},{7,6},{8,9},{9,8},{10,11... | collective-permute-start | bytes 3145736 | tf_op jit(solution)/shard_map/ppermute | solution.py:38
  4.9 3.0 %collective-permute-start.1 = (bf16[8,128]{1,0:T(8,128)(2,1)S(1)}, bf16[8,128]{1,0:T(8,128)(2,1)S(1)}, u32[]{:S(2)}, u32[]{:S(2)}) collective-permute-start(bf16[8,128]{1,0:T(8,128)(2,1)S(1)} %pad_maximum_fusion.2), channel_id=1, source_target_pairs={{0,5},{1,4},{2,7},{3,6},{4,1},{5,0},{6,3},{7,2},{8,13},{9,12},{10,... | collective-permute-start | bytes 6152 | tf_op jit(solution)/shard_map/ppermute | solution.py:38
  7.3 3.2 %collective-permute-start.4 = (s32[16,128]{1,0:T(8,128)S(1)}, s32[16,128]{1,0:T(8,128)S(1)}, u32[]{:S(2)}, u32[]{:S(2)}) collective-permute-start(s32[16,128]{1,0:T(8,128)S(1)} %get-tuple-element.34), channel_id=1, source_target_pairs={{0,1},{1,0},{2,3},{3,2},{4,5},{5,4},{6,7},{7,6},{8,9},{9,8},{10,11... | collective-permute-start | bytes 24584 | tf_op jit(solution)/shard_map/ppermute | solution.py:38
  7.9 4.0 %collective-permute-start.2 = (bf16[16,128]{1,0:T(8,128)(2,1)S(1)}, bf16[16,128]{1,0:T(8,128)(2,1)S(1)}, u32[]{:S(2)}, u32[]{:S(2)}) collective-permute-start(bf16[16,128]{1,0:T(8,128)(2,1)S(1)} %pad_maximum_fusion.paths_ref), channel_id=1, source_target_pairs={{0,9},{1,8},{2,11},{3,10},{4,13},{5,12},{6,15},{7,14},{8,1},{9,0},... | collective-permute-start | bytes 12296 | tf_op jit(solution)/shard_map/ppermute | solution.py:38
  12.9 3.2 %collective-permute-start.5 = (f32[16,256]{1,0:T(8,128)S(1)}, f32[16,256]{1,0:T(8,128)S(1)}, u32[]{:S(2)}, u32[]{:S(2)}) collective-permute-start(f32[16,256]{1,0:T(8,128)S(1)} %get-tuple-element.36), channel_id=1, source_target_pairs={{0,3},{1,2},{2,1},{3,0},{4,7},{5,6},{6,5},{7,4},{8,11},{9,10},{10,... | collective-permute-start | bytes 49160 | tf_op jit(solution)/shard_map/ppermute | solution.py:38
  16.2 3.1 %collective-permute-start.6 = (f32[8,256]{1,0:T(8,128)S(1)}, f32[8,256]{1,0:T(8,128)S(1)}, u32[]{:S(2)}, u32[]{:S(2)}) collective-permute-start(f32[8,256]{1,0:T(8,128)S(1)} %slice.32), channel_id=1, source_target_pairs={{0,5},{1,4},{2,7},{3,6},{4,1},{5,0},{6,3},{7,2},{8,13},{9,12},{10,... | collective-permute-start | bytes 24584 | tf_op jit(solution)/shard_map/ppermute | solution.py:38
  19.3 4.0 %collective-permute-start.7 = (f32[4,256]{1,0:T(4,128)S(1)}, f32[4,256]{1,0:T(4,128)S(1)}, u32[]{:S(2)}, u32[]{:S(2)}) collective-permute-start(f32[4,256]{1,0:T(4,128)S(1)} %pad_maximum_fusion.1), channel_id=1, source_target_pairs={{0,9},{1,8},{2,11},{3,10},{4,13},{5,12},{6,15},{7,14},{8,1},{9,0},... | collective-permute-start | bytes 12296 | tf_op jit(solution)/shard_map/ppermute | solution.py:38
  23.3 1.2 %collective-permute-start.8 = (f32[2,256]{1,0:T(2,128)S(1)}, f32[2,256]{1,0:T(2,128)S(1)}, u32[]{:S(2)}, u32[]{:S(2)}) collective-permute-start(f32[2,256]{1,0:T(2,128)S(1)} %get-tuple-element.41), channel_id=1, source_target_pairs={{0,1},{1,0},{2,3},{3,2},{4,5},{5,4},{6,7},{7,6},{8,9},{9,8},{10,11... | collective-permute-start | bytes 6152 | tf_op jit(solution)/shard_map/ppermute | solution.py:38

commit v7 on v6

--- a/solution.py
+++ b/solution.py
@@ -14,7 +14,7 @@
 VMEM = pl.BlockSpec(memory_space=pltpu.VMEM)
 SMEM = pl.BlockSpec(memory_space=pltpu.SMEM)
 HBM = pl.BlockSpec(memory_space=pltpu.HBM)
-PARTS = 4
+PARTS = 2
 
 
 def call(kernel, outs, specs, flops, args, scratch=()):
@@ -95,12 +95,11 @@
     ids_ref,
     owner_ref,
     margin_ref,
+    loadings_ref,
     limits_ref,
-    split_ref,
     coef_ref,
     size_ref,
     limit_ref,
-    loadings_ref,
     sems,
 ):
     slots, width = coef_ref.shape
@@ -123,29 +122,19 @@
     ]
     for copy in small[:3] + large + small[3:]:
         copy.start()
-    for copy in small[:3]:
-        copy.wait()
-    for r in range(limits_ref.shape[0]):
-        limits_ref[r : r + 1, :] = jnp.full((1, LANES), limit_ref[r])
-    tall = jnp.concatenate([loadings_ref[...]] * DATES, axis=0)
-    wide = jnp.concatenate([tall] * DATES, axis=1)
-    row = lax.broadcasted_iota(jnp.int32, wide.shape, 0) // F
-    column = lax.broadcasted_iota(jnp.int32, wide.shape, 1) // K
-    rest = jnp.where(row == column, wide, 0.0)
-    for i in range(3):
-        part = rest.astype(jnp.bfloat16)
-        split_ref[i] = part
-        rest = rest - part.astype(jnp.float32)
+    small[0].wait()
     sizes = size_ref[...].astype(jnp.float32).T
-    basis = (lax.broadcasted_iota(jnp.int32, (1, width), 1) & (K - 1)).astype(jnp.float32)
+    basis = (lax.broadcasted_iota(jnp.int32, (1, width), 1) & (K - 1)).astype(jnp.float32).astype(jnp.bfloat16)
     for i in range(PARTS):
         large[i].wait()
         for c in range(i * step // LANES, (i + 1) * step // LANES):
             rows = slice(c * LANES, (c + 1) * LANES)
-            coef = coef_ref[rows, :].astype(jnp.float32)
-            used_ref[rows, :] = jnp.where(basis < sizes[:, c : c + 1], coef, 0.0).astype(jnp.bfloat16)
-    for copy in small[3:]:
+            coef = coef_ref[rows, :]
+            used_ref[rows, :] = jnp.where(basis < sizes[:, c : c + 1], coef, jnp.zeros_like(coef))
+    for copy in small[1:]:
         copy.wait()
+    for r in range(limits_ref.shape[0]):
+        limits_ref[r : r + 1, :] = jnp.full((1, LANES), limit_ref[r])
 
 
 def write_onehot(code, set_at, hot_ref):
@@ -205,9 +194,30 @@
 
 
 def rows_kernel(
-    count, own_rows, me_ref, live_ref, ids_ref, owner_ref, margin_ref, set_ref, hot_ref, code_ref, held_ref
+    count,
+    own_rows,
+    me_ref,
+    live_ref,
+    ids_ref,
+    owner_ref,
+    margin_ref,
+    loadings_ref,
+    set_ref,
+    hot_ref,
+    code_ref,
+    held_ref,
+    split_ref,
 ):
     held_margin(count, me_ref[0], margin_ref[...], held_ref)
+    tall = jnp.concatenate([loadings_ref[...]] * DATES, axis=0)
+    wide = jnp.concatenate([tall] * DATES, axis=1)
+    row = lax.broadcasted_iota(jnp.int32, wide.shape, 0) // F
+    column = lax.broadcasted_iota(jnp.int32, wide.shape, 1) // K
+    rest = jnp.where(row == column, wide, 0.0)
+    for i in range(3):
+        part = rest.astype(jnp.bfloat16)
+        split_ref[i] = part
+        rest = rest - part.astype(jnp.float32)
     set_total = owner_ref.shape[1]
     place = lax.broadcasted_iota(jnp.int32, (set_total, 1), 0)
     block = lax.shift_right_logical(place, own_rows.bit_length() - 1)
@@ -294,7 +304,7 @@
     ids = set_ids.reshape(-1, LANES)
     owner = netting_row.reshape(1, -1)
     turned = loadings.T
-    own, used, ids, owner, margin, limits, split = call(
+    own, used, ids, owner, margin, turned, limits = call(
         fetch_kernel,
         [
             shape(factors.shape, bf16),
@@ -302,8 +312,8 @@
             shape(ids.shape, jnp.int32),
             shape(owner.shape, jnp.int32),
             shape(margin_start.shape, f32),
+            shape(turned.shape, f32),
             shape((own_rows, LANES), f32),
-            shape((3, DATES * F, DATES * K), bf16),
         ],
         [HBM] * 8,
         10**8,
@@ -312,24 +322,24 @@
             pltpu.VMEM(trade_coef.shape, bf16),
             pltpu.VMEM(sizes.shape, jnp.int32),
             pltpu.SMEM(threshold.shape, f32),
-            pltpu.VMEM(turned.shape, f32),
             pltpu.SemaphoreType.DMA((PARTS + 7,)),
         ],
     )
     near = join(own, swap(factors, 2, count), 2)
     used, ids, live_count, near = lax.optimization_barrier((used, ids, live_count, near))
     other = swap(used, 1, count)
-    set_at, onehot, code, held = call(
+    set_at, onehot, code, held, split = call(
         lambda *refs: rows_kernel(count, own_rows, *refs),
         [
             shape((set_total, LANES), jnp.int32),
             shape((set_total, slot_total), bf16),
             shape(ids.shape, jnp.int32),
             shape((own_rows, DATES * margin_start.shape[1]), f32),
+            shape((3, DATES * F, DATES * K), bf16),
         ],
-        [SMEM] * 2 + [VMEM] * 3,
+        [SMEM] * 2 + [VMEM] * 4,
         0,
-        (me.astype(jnp.int32).reshape(1), live_count, ids, owner, margin),
+        (me.astype(jnp.int32).reshape(1), live_count, ids, owner, margin, turned),
     )
     (other_hot,) = call(
         other_rows_kernel,

time: 25.4 us -> 25.4 us (level)
  no operation moved by 1% of the time
where the time goes in v7:
time: 25.4 us; the launch traced here: 25.2 us
  starting transfers between devices  13.6 us (54%)
  waiting for transfers between devices  5.94 us (23%)
  Pallas kernels  4.84 us (19%)
  between operations  0.73 us (3%)
    ppermute x9, starting transfers between devices, swap(): return lax.ppermute(x, 'trade', [(i, i ^ (bit | 1)) for i in range(count)])  13.6 us
    ppermute x9, waiting for transfers between devices, swap(): return lax.ppermute(x, 'trade', [(i, i ^ (bit | 1)) for i in range(count)])  5.94 us
    pallas_call x6, Pallas kernels, call(): pl.pallas_call(kernel, out_shape=outs, in_specs=specs, out_specs=[VMEM] *...  4.84 us
  transfers between devices with their start and end apart: 9, of which 6 were waited for; matrix products, arithmetic and copies ran while one was open for 0% of the time, Pallas kernels for 12%

profile of v7, /device:TPU:0, one launch (start us, length us, event | category | flops | bytes accessed | tf_op | source)
XLA Modules:
  0.0 25.2 jit_solution(3839861098051544177)
XLA Ops:
  0.0 2.4 %collective-permute-start = (bf16[4,128]{1,0:T(4,128)(2,1)}, bf16[4,128]{1,0:T(4,128)(2,1)S(1)}, u32[]{:S(2)}, u32[]{:S(2)}) collective-permute-start(bf16[4,128]{1,0:T(4,128)(2,1)} %factors_hbm.1), channel_id=1, source_target_pairs={{0,3},{1,2},{2,1},{3,0},{4,7},{5,6},{6,5},{7,4},{8,11},{9,10},{10,... | collective-permute-start | bytes 3080 | tf_op jit(solution)/shard_map/ppermute | solution.py:38
  2.4 1.6 %shard_map.91 = (bf16[4,128]{1,0:T(4,128)(2,1)S(1)}, bf16[2048,256]{1,0:T(8,128)(2,1)S(1)}, s32[16,128]{1,0:T(8,128)S(1)}, s32[1,32]{1,0:T(1,128)S(1)}, f32[2,64...) custom-call(bf16[4,128]{1,0:T(4,128)(2,1)} %factors_hbm.1, bf16[2048,256]{1,0:T(8,128)(2,1)} %coef_hbm.1, ...), custom_call_target="tpu_custom_call" | custom-call | flops 100000000 | bytes 2130184 | tf_op jit(solution)/shard_map/pallas_call | solution.py:22
  4.0 0.0 collective-permute-done
  4.1 0.7 %collective-permute-start.3 = (bf16[2048,256]{1,0:T(8,128)(2,1)S(1)}, bf16[2048,256]{1,0:T(8,128)(2,1)S(1)}, u32[]{:S(2)}, u32[]{:S(2)}) collective-permute-start(bf16[2048,256]{1,0:T(8,128)(2,1)S(1)} %get-tuple-element.33.used_ref), channel_id=1, source_target_pairs={{0,1},{1,0},{2,3},{3,2},{4,5},{5,4},{6,7},{7,6},{8,9},{9,8},{10,11... | collective-permute-start | bytes 3145736 | tf_op jit(solution)/shard_map/ppermute | solution.py:38
  4.8 1.6 %collective-permute-start.1 = (bf16[8,128]{1,0:T(8,128)(2,1)S(1)}, bf16[8,128]{1,0:T(8,128)(2,1)S(1)}, u32[]{:S(2)}, u32[]{:S(2)}) collective-permute-start(bf16[8,128]{1,0:T(8,128)(2,1)S(1)} %pad_maximum_fusion.2), channel_id=1, source_target_pairs={{0,5},{1,4},{2,7},{3,6},{4,1},{5,0},{6,3},{7,2},{8,13},{9,12},{10,... | collective-permute-start | bytes 6152 | tf_op jit(solution)/shard_map/ppermute | solution.py:38
  7.1 0.2 shard_map.92
  7.3 0.2 collective-permute-start.4
  7.5 0.3 %collective-permute-done.1 = bf16[8,128]{1,0:T(8,128)(2,1)S(1)} collective-permute-done((bf16[8,128]{1,0:T(8,128)(2,1)S(1)}, bf16[8,128]{1,0:T(8,128)(2,1)S(1)}, u32[]{:S(2)}, u32[]{:S(2)}) %collective-permute-start.1) | collective-permute-done | bytes 2080 | tf_op jit(solution)/shard_map/ppermute | solution.py:38
  7.8 2.7 %collective-permute-start.2 = (bf16[16,128]{1,0:T(8,128)(2,1)S(1)}, bf16[16,128]{1,0:T(8,128)(2,1)S(1)}, u32[]{:S(2)}, u32[]{:S(2)}) collective-permute-start(bf16[16,128]{1,0:T(8,128)(2,1)S(1)} %pad_maximum_fusion.paths_ref), channel_id=1, source_target_pairs={{0,9},{1,8},{2,11},{3,10},{4,13},{5,12},{6,15},{7,14},{8,1},{9,0},... | collective-permute-start | bytes 12296 | tf_op jit(solution)/shard_map/ppermute | solution.py:38
  10.5 0.0 collective-permute-done.4.code_ref
  10.5 0.1 shard_map.93.other_hot_ref
  10.6 0.0 collective-permute-done.3.other_ref
  10.6 1.1 %shard_map.94.near_ref = f32[32,128]{1,0:T(8,128)S(1)} custom-call(bf16[16,128]{1,0:T(8,128)(2,1)S(1)} %pad_maximum_fusion.paths_ref, bf16[3,128,256]{2,1,0:T(8,128)(2,1)S(1)} %get-tuple-element.32.split_ref, bf16[2048,256]{1,0:T(8,128)(2,1)S(1)} %get-tuple-element.33.used_ref, bf16[2048,256]{1,0:T(8,128)(2,1)S(1)} %collective-permute-done.3.other_ref, ...), custom_call_target="tpu_custom_call" | custom-call | flops 301989888 | bytes 2576384 | tf_op jit(solution)/shard_map/pallas_call | solution.py:22
  11.7 0.2 collective-permute-done.2.paths_ref
  11.9 1.1 %shard_map.95 = (f32[16,256]{1,0:T(8,128)S(1)}, f32[16,256]{1,0:T(8,128)S(1)}) custom-call(bf16[16,128]{1,0:T(8,128)(2,1)S(1)} %collective-permute-done.2.paths_ref, bf16[3,128,256]{2,1,0:T(8,128)(2,1)S(1)} %get-tuple-element.32.split_ref, bf16[2048,256]{1,0:T(8,128)(2,1)S(1)} %get-tuple-element.33.used_ref, ...), custom_call_target="tpu_custom_call" | custom-call | flops 301989888 | bytes 2609152 | tf_op jit(solution)/shard_map/pallas_call | solution.py:22
  12.9 1.6 %collective-permute-start.5 = (f32[16,256]{1,0:T(8,128)S(1)}, f32[16,256]{1,0:T(8,128)S(1)}, u32[]{:S(2)}, u32[]{:S(2)}) collective-permute-start(f32[16,256]{1,0:T(8,128)S(1)} %get-tuple-element.38), channel_id=1, source_target_pairs={{0,3},{1,2},{2,1},{3,0},{4,7},{5,6},{6,5},{7,4},{8,11},{9,10},{10,... | collective-permute-start | bytes 49160 | tf_op jit(solution)/shard_map/ppermute | solution.py:38
  14.5 1.6 %collective-permute-done.5 = f32[16,256]{1,0:T(8,128)S(1)} collective-permute-done((f32[16,256]{1,0:T(8,128)S(1)}, f32[16,256]{1,0:T(8,128)S(1)}, u32[]{:S(2)}, u32[]{:S(2)}) %collective-permute-start.5) | collective-permute-done | bytes 16416 | tf_op jit(solution)/shard_map/ppermute | solution.py:38
  16.2 1.6 %collective-permute-start.6 = (f32[8,256]{1,0:T(8,128)S(1)}, f32[8,256]{1,0:T(8,128)S(1)}, u32[]{:S(2)}, u32[]{:S(2)}) collective-permute-start(f32[8,256]{1,0:T(8,128)S(1)} %slice.32), channel_id=1, source_target_pairs={{0,5},{1,4},{2,7},{3,6},{4,1},{5,0},{6,3},{7,2},{8,13},{9,12},{10,... | collective-permute-start | bytes 24584 | tf_op jit(solution)/shard_map/ppermute | solution.py:38
  17.7 1.5 %collective-permute-done.6 = f32[8,256]{1,0:T(8,128)S(1)} collective-permute-done((f32[8,256]{1,0:T(8,128)S(1)}, f32[8,256]{1,0:T(8,128)S(1)}, u32[]{:S(2)}, u32[]{:S(2)}) %collective-permute-start.6) | collective-permute-done | bytes 8224 | tf_op jit(solution)/shard_map/ppermute | solution.py:38
  19.3 2.7 %collective-permute-start.7 = (f32[4,256]{1,0:T(4,128)S(1)}, f32[4,256]{1,0:T(4,128)S(1)}, u32[]{:S(2)}, u32[]{:S(2)}) collective-permute-start(f32[4,256]{1,0:T(4,128)S(1)} %pad_maximum_fusion.1), channel_id=1, source_target_pairs={{0,9},{1,8},{2,11},{3,10},{4,13},{5,12},{6,15},{7,14},{8,1},{9,0},... | collective-permute-start | bytes 12296 | tf_op jit(solution)/shard_map/ppermute | solution.py:38
  21.9 1.3 %collective-permute-done.7 = f32[4,256]{1,0:T(4,128)S(1)} collective-permute-done((f32[4,256]{1,0:T(4,128)S(1)}, f32[4,256]{1,0:T(4,128)S(1)}, u32[]{:S(2)}, u32[]{:S(2)}) %collective-permute-start.7) | collective-permute-done | bytes 4128 | tf_op jit(solution)/shard_map/ppermute | solution.py:38
  23.3 0.1 collective-permute-start.8
  23.4 1.0 %collective-permute-done.8.other_ref = f32[2,256]{1,0:T(2,128)S(1)} collective-permute-done((f32[2,256]{1,0:T(2,128)S(1)}, f32[2,256]{1,0:T(2,128)S(1)}, u32[]{:S(2)}, u32[]{:S(2)}) %collective-permute-start.8) | collective-permute-done | bytes 2080 | tf_op jit(solution)/shard_map/ppermute | solution.py:38
  24.4 0.8 %shard_map.96 = f32[2,8]{1,0:T(2,128)} custom-call(f32[2,256]{1,0:T(2,128)S(1)} %get-tuple-element.44.own_ref, f32[2,256]{1,0:T(2,128)S(1)} %collective-permute-done.8.other_ref, f32[2,512]{1,0:T(2,128)S(1)} %get-tuple-element.39.held_ref, f32[2,128]{1,0:T(2,128)S(1)} %get-tuple-element.40.limits_ref), custom_call_target="tpu_custom_call" | custom-call | flops 1000000 | bytes 9280 | tf_op jit(solution)/shard_map/pallas_call | solution.py:22
  (11 shorter events, 0.1 us)
Async XLA Ops:
  0.0 4.0 %collective-permute-start = (bf16[4,128]{1,0:T(4,128)(2,1)}, bf16[4,128]{1,0:T(4,128)(2,1)S(1)}, u32[]{:S(2)}, u32[]{:S(2)}) collective-permute-start(bf16[4,128]{1,0:T(4,128)(2,1)} %factors_hbm.1), channel_id=1, source_target_pairs={{0,3},{1,2},{2,1},{3,0},{4,7},{5,6},{6,5},{7,4},{8,11},{9,10},{10,... | collective-permute-start | bytes 3080 | tf_op jit(solution)/shard_map/ppermute | solution.py:38
  4.1 6.6 %collective-permute-start.3 = (bf16[2048,256]{1,0:T(8,128)(2,1)S(1)}, bf16[2048,256]{1,0:T(8,128)(2,1)S(1)}, u32[]{:S(2)}, u32[]{:S(2)}) collective-permute-start(bf16[2048,256]{1,0:T(8,128)(2,1)S(1)} %get-tuple-element.33.used_ref), channel_id=1, source_target_pairs={{0,1},{1,0},{2,3},{3,2},{4,5},{5,4},{6,7},{7,6},{8,9},{9,8},{10,11... | collective-permute-start | bytes 3145736 | tf_op jit(solution)/shard_map/ppermute | solution.py:38
  4.8 3.0 %collective-permute-start.1 = (bf16[8,128]{1,0:T(8,128)(2,1)S(1)}, bf16[8,128]{1,0:T(8,128)(2,1)S(1)}, u32[]{:S(2)}, u32[]{:S(2)}) collective-permute-start(bf16[8,128]{1,0:T(8,128)(2,1)S(1)} %pad_maximum_fusion.2), channel_id=1, source_target_pairs={{0,5},{1,4},{2,7},{3,6},{4,1},{5,0},{6,3},{7,2},{8,13},{9,12},{10,... | collective-permute-start | bytes 6152 | tf_op jit(solution)/shard_map/ppermute | solution.py:38
  7.3 3.2 %collective-permute-start.4 = (s32[16,128]{1,0:T(8,128)S(1)}, s32[16,128]{1,0:T(8,128)S(1)}, u32[]{:S(2)}, u32[]{:S(2)}) collective-permute-start(s32[16,128]{1,0:T(8,128)S(1)} %get-tuple-element.36), channel_id=1, source_target_pairs={{0,1},{1,0},{2,3},{3,2},{4,5},{5,4},{6,7},{7,6},{8,9},{9,8},{10,11... | collective-permute-start | bytes 24584 | tf_op jit(solution)/shard_map/ppermute | solution.py:38
  7.8 4.0 %collective-permute-start.2 = (bf16[16,128]{1,0:T(8,128)(2,1)S(1)}, bf16[16,128]{1,0:T(8,128)(2,1)S(1)}, u32[]{:S(2)}, u32[]{:S(2)}) collective-permute-start(bf16[16,128]{1,0:T(8,128)(2,1)S(1)} %pad_maximum_fusion.paths_ref), channel_id=1, source_target_pairs={{0,9},{1,8},{2,11},{3,10},{4,13},{5,12},{6,15},{7,14},{8,1},{9,0},... | collective-permute-start | bytes 12296 | tf_op jit(solution)/shard_map/ppermute | solution.py:38
  12.9 3.2 %collective-permute-start.5 = (f32[16,256]{1,0:T(8,128)S(1)}, f32[16,256]{1,0:T(8,128)S(1)}, u32[]{:S(2)}, u32[]{:S(2)}) collective-permute-start(f32[16,256]{1,0:T(8,128)S(1)} %get-tuple-element.38), channel_id=1, source_target_pairs={{0,3},{1,2},{2,1},{3,0},{4,7},{5,6},{6,5},{7,4},{8,11},{9,10},{10,... | collective-permute-start | bytes 49160 | tf_op jit(solution)/shard_map/ppermute | solution.py:38
  16.2 3.1 %collective-permute-start.6 = (f32[8,256]{1,0:T(8,128)S(1)}, f32[8,256]{1,0:T(8,128)S(1)}, u32[]{:S(2)}, u32[]{:S(2)}) collective-permute-start(f32[8,256]{1,0:T(8,128)S(1)} %slice.32), channel_id=1, source_target_pairs={{0,5},{1,4},{2,7},{3,6},{4,1},{5,0},{6,3},{7,2},{8,13},{9,12},{10,... | collective-permute-start | bytes 24584 | tf_op jit(solution)/shard_map/ppermute | solution.py:38
  19.3 4.0 %collective-permute-start.7 = (f32[4,256]{1,0:T(4,128)S(1)}, f32[4,256]{1,0:T(4,128)S(1)}, u32[]{:S(2)}, u32[]{:S(2)}) collective-permute-start(f32[4,256]{1,0:T(4,128)S(1)} %pad_maximum_fusion.1), channel_id=1, source_target_pairs={{0,9},{1,8},{2,11},{3,10},{4,13},{5,12},{6,15},{7,14},{8,1},{9,0},... | collective-permute-start | bytes 12296 | tf_op jit(solution)/shard_map/ppermute | solution.py:38
  23.3 1.2 %collective-permute-start.8 = (f32[2,256]{1,0:T(2,128)S(1)}, f32[2,256]{1,0:T(2,128)S(1)}, u32[]{:S(2)}, u32[]{:S(2)}) collective-permute-start(f32[2,256]{1,0:T(2,128)S(1)} %get-tuple-element.43), channel_id=1, source_target_pairs={{0,1},{1,0},{2,3},{3,2},{4,5},{5,4},{6,7},{7,6},{8,9},{9,8},{10,11... | collective-permute-start | bytes 6152 | tf_op jit(solution)/shard_map/ppermute | solution.py:38

commit v8 on v7

--- a/solution.py
+++ b/solution.py
@@ -170,27 +170,38 @@
                 at += columns
 
 
-def final_kernel(own_ref, other_ref, held_ref, limits_ref, out_ref):
-    rows, width = own_ref.shape
-    side = width // (2 * DATES)
-    block = min(PATH_BLOCK, side)
+def shortfall(net_ref, held_ref, limits_ref, at):
+    rows, width = net_ref.shape
+    block = min(PATH_BLOCK, width // (2 * DATES))
     columns = DATES * block
     limit = jnp.broadcast_to(limits_ref[:, :1], (rows, columns))
     lane = lax.broadcasted_iota(jnp.int32, (rows, columns), 1)
     total = jnp.zeros((rows, columns), jnp.float32)
-    at = 0
-    for net_ref in (own_ref, other_ref):
-        for b in range(width // columns):
-            netted = net_ref[:, b * columns : (b + 1) * columns]
-            before = pltpu.roll(netted, LAG * block, 1)
-            margin = jnp.maximum(before - limit, 0.0)
-            collateral = jnp.where(lane < LAG * block, held_ref[:, at : at + columns], margin)
-            total = total + jnp.maximum(netted - collateral, 0.0)
-            at += columns
-    date = lax.broadcasted_iota(jnp.int32, (columns, DATES), 0) // block
-    pick = jnp.where(date == lax.broadcasted_iota(jnp.int32, (columns, DATES), 1), 1.0, 0.0)
-    out = jnp.dot(total, pick, precision=lax.Precision.HIGHEST, preferred_element_type=jnp.float32)
-    out_ref[...] = out / (4 * side)
+    for b in range(width // columns):
+        netted = net_ref[:, b * columns : (b + 1) * columns]
+        margin = jnp.maximum(pltpu.roll(netted, LAG * block, 1) - limit, 0.0)
+        held = held_ref[:, at + b * columns : at + (b + 1) * columns]
+        collateral = jnp.where(lane < LAG * block, held, margin)
+        total = total + jnp.maximum(netted - collateral, 0.0)
+    return total
+
+
+def own_kernel(own_ref, held_ref, limits_ref, total_ref):
+    total_ref[...] = shortfall(own_ref, held_ref, limits_ref, 0)
+
+
+def final_kernel(other_ref, held_ref, limits_ref, own_ref, out_ref):
+    rows, width = other_ref.shape
+    columns = own_ref.shape[1]
+    rest = own_ref[...] + shortfall(other_ref, held_ref, limits_ref, width)
+    date = lax.broadcasted_iota(jnp.int32, (columns, DATES), 0) // (columns // DATES)
+    pick = jnp.where(date == lax.broadcasted_iota(jnp.int32, (columns, DATES), 1), 1.0, 0.0).astype(jnp.bfloat16)
+    out = jnp.zeros((rows, DATES), jnp.float32)
+    for _ in range(3):
+        part = rest.astype(jnp.bfloat16)
+        out = out + jnp.dot(part, pick, preferred_element_type=jnp.float32)
+        rest = rest - part.astype(jnp.float32)
+    out_ref[...] = out / (2 * width // DATES)
 
 
 def rows_kernel(
@@ -371,12 +382,19 @@
         (far, split, used, other, onehot, other_hot, near_net),
     )
     own_net, other_net = scatter_sums(kept, sent, count)
+    (own_total,) = call(
+        own_kernel,
+        [shape((own_rows, DATES * min(PATH_BLOCK, side_total)), f32)],
+        [VMEM] * 3,
+        10**6,
+        (own_net, held, limits),
+    )
     (expected,) = call(
         final_kernel,
         [shape((own_rows, DATES), f32)],
         [VMEM] * 4,
         10**6,
-        (own_net, other_net, held, limits),
+        (other_net, held, limits, own_total),
     )
     return expected
 

time: 25.4 us -> 25.4 us (level)
    pallas_call x6 -> x7, Pallas kernels: 4.84 us -> 4.9 us  [call(): pl.pallas_call(kernel, out_shape=outs, in_specs=specs, out_specs=[VMEM] *...]
where the time goes in v8:
time: 25.4 us; the launch traced here: 25.2 us
  starting transfers between devices  13.6 us (54%)
  waiting for transfers between devices  5.86 us (23%)
  Pallas kernels  4.9 us (19%)
  between operations  0.73 us (3%)
    ppermute x9, starting transfers between devices, swap(): return lax.ppermute(x, 'trade', [(i, i ^ (bit | 1)) for i in range(count)])  13.6 us
    ppermute x9, waiting for transfers between devices, swap(): return lax.ppermute(x, 'trade', [(i, i ^ (bit | 1)) for i in range(count)])  5.86 us
    pallas_call x7, Pallas kernels, call(): pl.pallas_call(kernel, out_shape=outs, in_specs=specs, out_specs=[VMEM] *...  4.9 us
  transfers between devices with their start and end apart: 9, of which 6 were waited for; matrix products, arithmetic and copies ran while one was open for 0% of the time, Pallas kernels for 12%

profile of v8, /device:TPU:0, one launch (start us, length us, event | category | flops | bytes accessed | tf_op | source)
XLA Modules:
  0.0 25.2 jit_solution(18335471339961791413)
XLA Ops:
  0.0 2.4 %collective-permute-start = (bf16[4,128]{1,0:T(4,128)(2,1)}, bf16[4,128]{1,0:T(4,128)(2,1)S(1)}, u32[]{:S(2)}, u32[]{:S(2)}) collective-permute-start(bf16[4,128]{1,0:T(4,128)(2,1)} %factors_hbm.1), channel_id=1, source_target_pairs={{0,3},{1,2},{2,1},{3,0},{4,7},{5,6},{6,5},{7,4},{8,11},{9,10},{10,... | collective-permute-start | bytes 3080 | tf_op jit(solution)/shard_map/ppermute | solution.py:38
  2.4 1.6 %shard_map.91 = (bf16[4,128]{1,0:T(4,128)(2,1)S(1)}, bf16[2048,256]{1,0:T(8,128)(2,1)S(1)}, s32[16,128]{1,0:T(8,128)S(1)}, s32[1,32]{1,0:T(1,128)S(1)}, f32[2,64...) custom-call(bf16[4,128]{1,0:T(4,128)(2,1)} %factors_hbm.1, bf16[2048,256]{1,0:T(8,128)(2,1)} %coef_hbm.1, ...), custom_call_target="tpu_custom_call" | custom-call | flops 100000000 | bytes 2130184 | tf_op jit(solution)/shard_map/pallas_call | solution.py:22
  4.0 0.0 collective-permute-done
  4.1 0.7 %collective-permute-start.3 = (bf16[2048,256]{1,0:T(8,128)(2,1)S(1)}, bf16[2048,256]{1,0:T(8,128)(2,1)S(1)}, u32[]{:S(2)}, u32[]{:S(2)}) collective-permute-start(bf16[2048,256]{1,0:T(8,128)(2,1)S(1)} %get-tuple-element.33.used_ref), channel_id=1, source_target_pairs={{0,1},{1,0},{2,3},{3,2},{4,5},{5,4},{6,7},{7,6},{8,9},{9,8},{10,11... | collective-permute-start | bytes 3145736 | tf_op jit(solution)/shard_map/ppermute | solution.py:38
  4.8 1.6 %collective-permute-start.1 = (bf16[8,128]{1,0:T(8,128)(2,1)S(1)}, bf16[8,128]{1,0:T(8,128)(2,1)S(1)}, u32[]{:S(2)}, u32[]{:S(2)}) collective-permute-start(bf16[8,128]{1,0:T(8,128)(2,1)S(1)} %pad_maximum_fusion.2), channel_id=1, source_target_pairs={{0,5},{1,4},{2,7},{3,6},{4,1},{5,0},{6,3},{7,2},{8,13},{9,12},{10,... | collective-permute-start | bytes 6152 | tf_op jit(solution)/shard_map/ppermute | solution.py:38
  7.1 0.2 shard_map.92
  7.3 0.2 collective-permute-start.4
  7.5 0.3 %collective-permute-done.1 = bf16[8,128]{1,0:T(8,128)(2,1)S(1)} collective-permute-done((bf16[8,128]{1,0:T(8,128)(2,1)S(1)}, bf16[8,128]{1,0:T(8,128)(2,1)S(1)}, u32[]{:S(2)}, u32[]{:S(2)}) %collective-permute-start.1) | collective-permute-done | bytes 2080 | tf_op jit(solution)/shard_map/ppermute | solution.py:38
  7.8 2.7 %collective-permute-start.2 = (bf16[16,128]{1,0:T(8,128)(2,1)S(1)}, bf16[16,128]{1,0:T(8,128)(2,1)S(1)}, u32[]{:S(2)}, u32[]{:S(2)}) collective-permute-start(bf16[16,128]{1,0:T(8,128)(2,1)S(1)} %pad_maximum_fusion.paths_ref), channel_id=1, source_target_pairs={{0,9},{1,8},{2,11},{3,10},{4,13},{5,12},{6,15},{7,14},{8,1},{9,0},... | collective-permute-start | bytes 12296 | tf_op jit(solution)/shard_map/ppermute | solution.py:38
  10.5 0.0 collective-permute-done.4.code_ref
  10.5 0.1 shard_map.93.other_hot_ref
  10.6 1.1 %shard_map.94.near_ref = f32[32,128]{1,0:T(8,128)S(1)} custom-call(bf16[16,128]{1,0:T(8,128)(2,1)S(1)} %pad_maximum_fusion.paths_ref, bf16[3,128,256]{2,1,0:T(8,128)(2,1)S(1)} %get-tuple-element.32.split_ref, bf16[2048,256]{1,0:T(8,128)(2,1)S(1)} %get-tuple-element.33.used_ref, bf16[2048,256]{1,0:T(8,128)(2,1)S(1)} %collective-permute-done.3.other_ref, ...), custom_call_target="tpu_custom_call" | custom-call | flops 301989888 | bytes 2576384 | tf_op jit(solution)/shard_map/pallas_call | solution.py:22
  11.7 0.2 collective-permute-done.2.paths_ref
  11.9 1.1 %shard_map.95 = (f32[16,256]{1,0:T(8,128)S(1)}, f32[16,256]{1,0:T(8,128)S(1)}) custom-call(bf16[16,128]{1,0:T(8,128)(2,1)S(1)} %collective-permute-done.2.paths_ref, bf16[3,128,256]{2,1,0:T(8,128)(2,1)S(1)} %get-tuple-element.32.split_ref, bf16[2048,256]{1,0:T(8,128)(2,1)S(1)} %get-tuple-element.33.used_ref, ...), custom_call_target="tpu_custom_call" | custom-call | flops 301989888 | bytes 2609152 | tf_op jit(solution)/shard_map/pallas_call | solution.py:22
  12.9 1.6 %collective-permute-start.5 = (f32[16,256]{1,0:T(8,128)S(1)}, f32[16,256]{1,0:T(8,128)S(1)}, u32[]{:S(2)}, u32[]{:S(2)}) collective-permute-start(f32[16,256]{1,0:T(8,128)S(1)} %get-tuple-element.38), channel_id=1, source_target_pairs={{0,3},{1,2},{2,1},{3,0},{4,7},{5,6},{6,5},{7,4},{8,11},{9,10},{10,... | collective-permute-start | bytes 49160 | tf_op jit(solution)/shard_map/ppermute | solution.py:38
  14.5 1.6 %collective-permute-done.5 = f32[16,256]{1,0:T(8,128)S(1)} collective-permute-done((f32[16,256]{1,0:T(8,128)S(1)}, f32[16,256]{1,0:T(8,128)S(1)}, u32[]{:S(2)}, u32[]{:S(2)}) %collective-permute-start.5) | collective-permute-done | bytes 16416 | tf_op jit(solution)/shard_map/ppermute | solution.py:38
  16.2 1.6 %collective-permute-start.6 = (f32[8,256]{1,0:T(8,128)S(1)}, f32[8,256]{1,0:T(8,128)S(1)}, u32[]{:S(2)}, u32[]{:S(2)}) collective-permute-start(f32[8,256]{1,0:T(8,128)S(1)} %slice.32), channel_id=1, source_target_pairs={{0,5},{1,4},{2,7},{3,6},{4,1},{5,0},{6,3},{7,2},{8,13},{9,12},{10,... | collective-permute-start | bytes 24584 | tf_op jit(solution)/shard_map/ppermute | solution.py:38
  17.7 1.5 %collective-permute-done.6 = f32[8,256]{1,0:T(8,128)S(1)} collective-permute-done((f32[8,256]{1,0:T(8,128)S(1)}, f32[8,256]{1,0:T(8,128)S(1)}, u32[]{:S(2)}, u32[]{:S(2)}) %collective-permute-start.6) | collective-permute-done | bytes 8224 | tf_op jit(solution)/shard_map/ppermute | solution.py:38
  19.3 2.7 %collective-permute-start.7 = (f32[4,256]{1,0:T(4,128)S(1)}, f32[4,256]{1,0:T(4,128)S(1)}, u32[]{:S(2)}, u32[]{:S(2)}) collective-permute-start(f32[4,256]{1,0:T(4,128)S(1)} %pad_maximum_fusion.1), channel_id=1, source_target_pairs={{0,9},{1,8},{2,11},{3,10},{4,13},{5,12},{6,15},{7,14},{8,1},{9,0},... | collective-permute-start | bytes 12296 | tf_op jit(solution)/shard_map/ppermute | solution.py:38
  21.9 1.3 %collective-permute-done.7 = f32[4,256]{1,0:T(4,128)S(1)} collective-permute-done((f32[4,256]{1,0:T(4,128)S(1)}, f32[4,256]{1,0:T(4,128)S(1)}, u32[]{:S(2)}, u32[]{:S(2)}) %collective-permute-start.7) | collective-permute-done | bytes 4128 | tf_op jit(solution)/shard_map/ppermute | solution.py:38
  23.3 0.1 collective-permute-start.8
  23.4 0.1 shard_map.96.own_ref
  23.5 0.9 %collective-permute-done.8.other_ref = f32[2,256]{1,0:T(2,128)S(1)} collective-permute-done((f32[2,256]{1,0:T(2,128)S(1)}, f32[2,256]{1,0:T(2,128)S(1)}, u32[]{:S(2)}, u32[]{:S(2)}) %collective-permute-start.8) | collective-permute-done | bytes 2080 | tf_op jit(solution)/shard_map/ppermute | solution.py:38
  24.4 0.8 %shard_map.97 = f32[2,8]{1,0:T(2,128)} custom-call(f32[2,256]{1,0:T(2,128)S(1)} %collective-permute-done.8.other_ref, f32[2,512]{1,0:T(2,128)S(1)} %get-tuple-element.39.held_ref, f32[2,128]{1,0:T(2,128)S(1)} %get-tuple-element.40.limits_ref, f32[2,128]{1,0:T(2,128)S(1)} %shard_map.96.own_ref), custom_call_target="tpu_custom_call" | custom-call | flops 1000000 | bytes 8256 | tf_op jit(solution)/shard_map/pallas_call | solution.py:22
  (12 shorter events, 0.1 us)
Async XLA Ops:
  0.0 4.0 %collective-permute-start = (bf16[4,128]{1,0:T(4,128)(2,1)}, bf16[4,128]{1,0:T(4,128)(2,1)S(1)}, u32[]{:S(2)}, u32[]{:S(2)}) collective-permute-start(bf16[4,128]{1,0:T(4,128)(2,1)} %factors_hbm.1), channel_id=1, source_target_pairs={{0,3},{1,2},{2,1},{3,0},{4,7},{5,6},{6,5},{7,4},{8,11},{9,10},{10,... | collective-permute-start | bytes 3080 | tf_op jit(solution)/shard_map/ppermute | solution.py:38
  4.1 6.6 %collective-permute-start.3 = (bf16[2048,256]{1,0:T(8,128)(2,1)S(1)}, bf16[2048,256]{1,0:T(8,128)(2,1)S(1)}, u32[]{:S(2)}, u32[]{:S(2)}) collective-permute-start(bf16[2048,256]{1,0:T(8,128)(2,1)S(1)} %get-tuple-element.33.used_ref), channel_id=1, source_target_pairs={{0,1},{1,0},{2,3},{3,2},{4,5},{5,4},{6,7},{7,6},{8,9},{9,8},{10,11... | collective-permute-start | bytes 3145736 | tf_op jit(solution)/shard_map/ppermute | solution.py:38
  4.8 3.0 %collective-permute-start.1 = (bf16[8,128]{1,0:T(8,128)(2,1)S(1)}, bf16[8,128]{1,0:T(8,128)(2,1)S(1)}, u32[]{:S(2)}, u32[]{:S(2)}) collective-permute-start(bf16[8,128]{1,0:T(8,128)(2,1)S(1)} %pad_maximum_fusion.2), channel_id=1, source_target_pairs={{0,5},{1,4},{2,7},{3,6},{4,1},{5,0},{6,3},{7,2},{8,13},{9,12},{10,... | collective-permute-start | bytes 6152 | tf_op jit(solution)/shard_map/ppermute | solution.py:38
  7.3 3.2 %collective-permute-start.4 = (s32[16,128]{1,0:T(8,128)S(1)}, s32[16,128]{1,0:T(8,128)S(1)}, u32[]{:S(2)}, u32[]{:S(2)}) collective-permute-start(s32[16,128]{1,0:T(8,128)S(1)} %get-tuple-element.36), channel_id=1, source_target_pairs={{0,1},{1,0},{2,3},{3,2},{4,5},{5,4},{6,7},{7,6},{8,9},{9,8},{10,11... | collective-permute-start | bytes 24584 | tf_op jit(solution)/shard_map/ppermute | solution.py:38
  7.8 4.0 %collective-permute-start.2 = (bf16[16,128]{1,0:T(8,128)(2,1)S(1)}, bf16[16,128]{1,0:T(8,128)(2,1)S(1)}, u32[]{:S(2)}, u32[]{:S(2)}) collective-permute-start(bf16[16,128]{1,0:T(8,128)(2,1)S(1)} %pad_maximum_fusion.paths_ref), channel_id=1, source_target_pairs={{0,9},{1,8},{2,11},{3,10},{4,13},{5,12},{6,15},{7,14},{8,1},{9,0},... | collective-permute-start | bytes 12296 | tf_op jit(solution)/shard_map/ppermute | solution.py:38
  12.9 3.2 %collective-permute-start.5 = (f32[16,256]{1,0:T(8,128)S(1)}, f32[16,256]{1,0:T(8,128)S(1)}, u32[]{:S(2)}, u32[]{:S(2)}) collective-permute-start(f32[16,256]{1,0:T(8,128)S(1)} %get-tuple-element.38), channel_id=1, source_target_pairs={{0,3},{1,2},{2,1},{3,0},{4,7},{5,6},{6,5},{7,4},{8,11},{9,10},{10,... | collective-permute-start | bytes 49160 | tf_op jit(solution)/shard_map/ppermute | solution.py:38
  16.2 3.1 %collective-permute-start.6 = (f32[8,256]{1,0:T(8,128)S(1)}, f32[8,256]{1,0:T(8,128)S(1)}, u32[]{:S(2)}, u32[]{:S(2)}) collective-permute-start(f32[8,256]{1,0:T(8,128)S(1)} %slice.32), channel_id=1, source_target_pairs={{0,5},{1,4},{2,7},{3,6},{4,1},{5,0},{6,3},{7,2},{8,13},{9,12},{10,... | collective-permute-start | bytes 24584 | tf_op jit(solution)/shard_map/ppermute | solution.py:38
  19.3 4.0 %collective-permute-start.7 = (f32[4,256]{1,0:T(4,128)S(1)}, f32[4,256]{1,0:T(4,128)S(1)}, u32[]{:S(2)}, u32[]{:S(2)}) collective-permute-start(f32[4,256]{1,0:T(4,128)S(1)} %pad_maximum_fusion.1), channel_id=1, source_target_pairs={{0,9},{1,8},{2,11},{3,10},{4,13},{5,12},{6,15},{7,14},{8,1},{9,0},... | collective-permute-start | bytes 12296 | tf_op jit(solution)/shard_map/ppermute | solution.py:38
  23.3 1.2 %collective-permute-start.8 = (f32[2,256]{1,0:T(2,128)S(1)}, f32[2,256]{1,0:T(2,128)S(1)}, u32[]{:S(2)}, u32[]{:S(2)}) collective-permute-start(f32[2,256]{1,0:T(2,128)S(1)} %get-tuple-element.44), channel_id=1, source_target_pairs={{0,1},{1,0},{2,3},{3,2},{4,5},{5,4},{6,7},{7,6},{8,9},{9,8},{10,11... | collective-permute-start | bytes 6152 | tf_op jit(solution)/shard_map/ppermute | solution.py:38

commit v9 on v8

--- a/solution.py
+++ b/solution.py
@@ -11,6 +11,7 @@
 LAG = 2
 LANES = 128
 PATH_BLOCK = 32
+SLOT_BLOCK = 1024
 VMEM = pl.BlockSpec(memory_space=pltpu.VMEM)
 SMEM = pl.BlockSpec(memory_space=pltpu.SMEM)
 HBM = pl.BlockSpec(memory_space=pltpu.HBM)
@@ -256,13 +257,15 @@
     table = jnp.where(row == column, tiled, 0.0).astype(jnp.bfloat16)
     result = 0.0
     for used_ref, onehot_ref in trades:
-        values = lax.dot_general(
-            used_ref[...],
-            table,
-            (((1,), (1,)), ((), ())),
-            preferred_element_type=jnp.float32,
-        )
-        values = values.astype(jnp.bfloat16)
+        slots = used_ref.shape[0]
+        step = min(SLOT_BLOCK, slots)
+        values = [
+            lax.dot_general(
+                used_ref[at : at + step, :], table, (((1,), (1,)), ((), ())), preferred_element_type=jnp.float32
+            ).astype(jnp.bfloat16)
+            for at in range(0, slots, step)
+        ]
+        values = jnp.concatenate(values, axis=0)
         result = result + jnp.dot(onehot_ref[...], values, preferred_element_type=jnp.float32)
     return result
 

time: 25.4 us -> 25.4 us (level)
  no operation moved by 1% of the time
where the time goes in v9:
time: 25.4 us; the launch traced here: 25.2 us
  starting transfers between devices  13.6 us (54%)
  waiting for transfers between devices  5.84 us (23%)
  Pallas kernels  4.98 us (20%)
  between operations  0.74 us (3%)
    ppermute x9, starting transfers between devices, swap(): return lax.ppermute(x, 'trade', [(i, i ^ (bit | 1)) for i in range(count)])  13.6 us
    ppermute x9, waiting for transfers between devices, swap(): return lax.ppermute(x, 'trade', [(i, i ^ (bit | 1)) for i in range(count)])  5.84 us
    pallas_call x7, Pallas kernels, call(): pl.pallas_call(kernel, out_shape=outs, in_specs=specs, out_specs=[VMEM] *...  4.98 us
  transfers between devices with their start and end apart: 9, of which 6 were waited for; matrix products, arithmetic and copies ran while one was open for 0% of the time, Pallas kernels for 12%

profile of v9, /device:TPU:0, one launch (start us, length us, event | category | flops | bytes accessed | tf_op | source)
XLA Modules:
  0.0 25.2 jit_solution(3651475833231486572)
XLA Ops:
  0.0 2.4 %collective-permute-start = (bf16[4,128]{1,0:T(4,128)(2,1)}, bf16[4,128]{1,0:T(4,128)(2,1)S(1)}, u32[]{:S(2)}, u32[]{:S(2)}) collective-permute-start(bf16[4,128]{1,0:T(4,128)(2,1)} %factors_hbm.1), channel_id=1, source_target_pairs={{0,3},{1,2},{2,1},{3,0},{4,7},{5,6},{6,5},{7,4},{8,11},{9,10},{10,... | collective-permute-start | bytes 3080 | tf_op jit(solution)/shard_map/ppermute | solution.py:39
  2.4 1.6 %shard_map.91 = (bf16[4,128]{1,0:T(4,128)(2,1)S(1)}, bf16[2048,256]{1,0:T(8,128)(2,1)S(1)}, s32[16,128]{1,0:T(8,128)S(1)}, s32[1,32]{1,0:T(1,128)S(1)}, f32[2,64...) custom-call(bf16[4,128]{1,0:T(4,128)(2,1)} %factors_hbm.1, bf16[2048,256]{1,0:T(8,128)(2,1)} %coef_hbm.1, ...), custom_call_target="tpu_custom_call" | custom-call | flops 100000000 | bytes 2130184 | tf_op jit(solution)/shard_map/pallas_call | solution.py:23
  4.1 0.7 %collective-permute-start.3 = (bf16[2048,256]{1,0:T(8,128)(2,1)S(1)}, bf16[2048,256]{1,0:T(8,128)(2,1)S(1)}, u32[]{:S(2)}, u32[]{:S(2)}) collective-permute-start(bf16[2048,256]{1,0:T(8,128)(2,1)S(1)} %get-tuple-element.33.used_ref), channel_id=1, source_target_pairs={{0,1},{1,0},{2,3},{3,2},{4,5},{5,4},{6,7},{7,6},{8,9},{9,8},{10,11... | collective-permute-start | bytes 3145736 | tf_op jit(solution)/shard_map/ppermute | solution.py:39
  4.8 1.6 %collective-permute-start.1 = (bf16[8,128]{1,0:T(8,128)(2,1)S(1)}, bf16[8,128]{1,0:T(8,128)(2,1)S(1)}, u32[]{:S(2)}, u32[]{:S(2)}) collective-permute-start(bf16[8,128]{1,0:T(8,128)(2,1)S(1)} %pad_maximum_fusion.2), channel_id=1, source_target_pairs={{0,5},{1,4},{2,7},{3,6},{4,1},{5,0},{6,3},{7,2},{8,13},{9,12},{10,... | collective-permute-start | bytes 6152 | tf_op jit(solution)/shard_map/ppermute | solution.py:39
  7.1 0.2 shard_map.92
  7.3 0.2 collective-permute-start.4
  7.5 0.3 %collective-permute-done.1 = bf16[8,128]{1,0:T(8,128)(2,1)S(1)} collective-permute-done((bf16[8,128]{1,0:T(8,128)(2,1)S(1)}, bf16[8,128]{1,0:T(8,128)(2,1)S(1)}, u32[]{:S(2)}, u32[]{:S(2)}) %collective-permute-start.1) | collective-permute-done | bytes 2080 | tf_op jit(solution)/shard_map/ppermute | solution.py:39
  7.8 2.7 %collective-permute-start.2 = (bf16[16,128]{1,0:T(8,128)(2,1)S(1)}, bf16[16,128]{1,0:T(8,128)(2,1)S(1)}, u32[]{:S(2)}, u32[]{:S(2)}) collective-permute-start(bf16[16,128]{1,0:T(8,128)(2,1)S(1)} %pad_maximum_fusion.paths_ref), channel_id=1, source_target_pairs={{0,9},{1,8},{2,11},{3,10},{4,13},{5,12},{6,15},{7,14},{8,1},{9,0},... | collective-permute-start | bytes 12296 | tf_op jit(solution)/shard_map/ppermute | solution.py:39
  10.5 0.0 collective-permute-done.4.code_ref
  10.5 0.1 shard_map.93.other_hot_ref
  10.6 0.0 collective-permute-done.3.other_ref
  10.6 1.1 %shard_map.94.near_ref = f32[32,128]{1,0:T(8,128)S(1)} custom-call(bf16[16,128]{1,0:T(8,128)(2,1)S(1)} %pad_maximum_fusion.paths_ref, bf16[3,128,256]{2,1,0:T(8,128)(2,1)S(1)} %get-tuple-element.32.split_ref, bf16[2048,256]{1,0:T(8,128)(2,1)S(1)} %get-tuple-element.33.used_ref, bf16[2048,256]{1,0:T(8,128)(2,1)S(1)} %collective-permute-done.3.other_ref, ...), custom_call_target="tpu_custom_call" | custom-call | flops 301989888 | bytes 2576384 | tf_op jit(solution)/shard_map/pallas_call | solution.py:23
  11.7 0.1 collective-permute-done.2.paths_ref
  11.9 1.1 %shard_map.95 = (f32[16,256]{1,0:T(8,128)S(1)}, f32[16,256]{1,0:T(8,128)S(1)}) custom-call(bf16[16,128]{1,0:T(8,128)(2,1)S(1)} %collective-permute-done.2.paths_ref, bf16[3,128,256]{2,1,0:T(8,128)(2,1)S(1)} %get-tuple-element.32.split_ref, bf16[2048,256]{1,0:T(8,128)(2,1)S(1)} %get-tuple-element.33.used_ref, ...), custom_call_target="tpu_custom_call" | custom-call | flops 301989888 | bytes 2609152 | tf_op jit(solution)/shard_map/pallas_call | solution.py:23
  13.0 1.6 %collective-permute-start.5 = (f32[16,256]{1,0:T(8,128)S(1)}, f32[16,256]{1,0:T(8,128)S(1)}, u32[]{:S(2)}, u32[]{:S(2)}) collective-permute-start(f32[16,256]{1,0:T(8,128)S(1)} %get-tuple-element.38), channel_id=1, source_target_pairs={{0,3},{1,2},{2,1},{3,0},{4,7},{5,6},{6,5},{7,4},{8,11},{9,10},{10,... | collective-permute-start | bytes 49160 | tf_op jit(solution)/shard_map/ppermute | solution.py:39
  14.6 1.6 %collective-permute-done.5 = f32[16,256]{1,0:T(8,128)S(1)} collective-permute-done((f32[16,256]{1,0:T(8,128)S(1)}, f32[16,256]{1,0:T(8,128)S(1)}, u32[]{:S(2)}, u32[]{:S(2)}) %collective-permute-start.5) | collective-permute-done | bytes 16416 | tf_op jit(solution)/shard_map/ppermute | solution.py:39
  16.2 1.6 %collective-permute-start.6 = (f32[8,256]{1,0:T(8,128)S(1)}, f32[8,256]{1,0:T(8,128)S(1)}, u32[]{:S(2)}, u32[]{:S(2)}) collective-permute-start(f32[8,256]{1,0:T(8,128)S(1)} %slice.32), channel_id=1, source_target_pairs={{0,5},{1,4},{2,7},{3,6},{4,1},{5,0},{6,3},{7,2},{8,13},{9,12},{10,... | collective-permute-start | bytes 24584 | tf_op jit(solution)/shard_map/ppermute | solution.py:39
  17.8 1.5 %collective-permute-done.6 = f32[8,256]{1,0:T(8,128)S(1)} collective-permute-done((f32[8,256]{1,0:T(8,128)S(1)}, f32[8,256]{1,0:T(8,128)S(1)}, u32[]{:S(2)}, u32[]{:S(2)}) %collective-permute-start.6) | collective-permute-done | bytes 8224 | tf_op jit(solution)/shard_map/ppermute | solution.py:39
  19.3 2.7 %collective-permute-start.7 = (f32[4,256]{1,0:T(4,128)S(1)}, f32[4,256]{1,0:T(4,128)S(1)}, u32[]{:S(2)}, u32[]{:S(2)}) collective-permute-start(f32[4,256]{1,0:T(4,128)S(1)} %pad_maximum_fusion.1), channel_id=1, source_target_pairs={{0,9},{1,8},{2,11},{3,10},{4,13},{5,12},{6,15},{7,14},{8,1},{9,0},... | collective-permute-start | bytes 12296 | tf_op jit(solution)/shard_map/ppermute | solution.py:39
  22.0 1.3 %collective-permute-done.7 = f32[4,256]{1,0:T(4,128)S(1)} collective-permute-done((f32[4,256]{1,0:T(4,128)S(1)}, f32[4,256]{1,0:T(4,128)S(1)}, u32[]{:S(2)}, u32[]{:S(2)}) %collective-permute-start.7) | collective-permute-done | bytes 4128 | tf_op jit(solution)/shard_map/ppermute | solution.py:39
  23.3 0.1 collective-permute-start.8
  23.4 0.1 shard_map.96.own_ref
  23.5 1.0 %collective-permute-done.8.other_ref = f32[2,256]{1,0:T(2,128)S(1)} collective-permute-done((f32[2,256]{1,0:T(2,128)S(1)}, f32[2,256]{1,0:T(2,128)S(1)}, u32[]{:S(2)}, u32[]{:S(2)}) %collective-permute-start.8) | collective-permute-done | bytes 2080 | tf_op jit(solution)/shard_map/ppermute | solution.py:39
  24.5 0.8 %shard_map.97 = f32[2,8]{1,0:T(2,128)} custom-call(f32[2,256]{1,0:T(2,128)S(1)} %collective-permute-done.8.other_ref, f32[2,512]{1,0:T(2,128)S(1)} %get-tuple-element.39.held_ref, f32[2,128]{1,0:T(2,128)S(1)} %get-tuple-element.40.limits_ref, f32[2,128]{1,0:T(2,128)S(1)} %shard_map.96.own_ref), custom_call_target="tpu_custom_call" | custom-call | flops 1000000 | bytes 8256 | tf_op jit(solution)/shard_map/pallas_call | solution.py:23
  (12 shorter events, 0.1 us)
Async XLA Ops:
  0.0 4.0 %collective-permute-start = (bf16[4,128]{1,0:T(4,128)(2,1)}, bf16[4,128]{1,0:T(4,128)(2,1)S(1)}, u32[]{:S(2)}, u32[]{:S(2)}) collective-permute-start(bf16[4,128]{1,0:T(4,128)(2,1)} %factors_hbm.1), channel_id=1, source_target_pairs={{0,3},{1,2},{2,1},{3,0},{4,7},{5,6},{6,5},{7,4},{8,11},{9,10},{10,... | collective-permute-start | bytes 3080 | tf_op jit(solution)/shard_map/ppermute | solution.py:39
  4.1 6.6 %collective-permute-start.3 = (bf16[2048,256]{1,0:T(8,128)(2,1)S(1)}, bf16[2048,256]{1,0:T(8,128)(2,1)S(1)}, u32[]{:S(2)}, u32[]{:S(2)}) collective-permute-start(bf16[2048,256]{1,0:T(8,128)(2,1)S(1)} %get-tuple-element.33.used_ref), channel_id=1, source_target_pairs={{0,1},{1,0},{2,3},{3,2},{4,5},{5,4},{6,7},{7,6},{8,9},{9,8},{10,11... | collective-permute-start | bytes 3145736 | tf_op jit(solution)/shard_map/ppermute | solution.py:39
  4.8 3.0 %collective-permute-start.1 = (bf16[8,128]{1,0:T(8,128)(2,1)S(1)}, bf16[8,128]{1,0:T(8,128)(2,1)S(1)}, u32[]{:S(2)}, u32[]{:S(2)}) collective-permute-start(bf16[8,128]{1,0:T(8,128)(2,1)S(1)} %pad_maximum_fusion.2), channel_id=1, source_target_pairs={{0,5},{1,4},{2,7},{3,6},{4,1},{5,0},{6,3},{7,2},{8,13},{9,12},{10,... | collective-permute-start | bytes 6152 | tf_op jit(solution)/shard_map/ppermute | solution.py:39
  7.3 3.2 %collective-permute-start.4 = (s32[16,128]{1,0:T(8,128)S(1)}, s32[16,128]{1,0:T(8,128)S(1)}, u32[]{:S(2)}, u32[]{:S(2)}) collective-permute-start(s32[16,128]{1,0:T(8,128)S(1)} %get-tuple-element.36), channel_id=1, source_target_pairs={{0,1},{1,0},{2,3},{3,2},{4,5},{5,4},{6,7},{7,6},{8,9},{9,8},{10,11... | collective-permute-start | bytes 24584 | tf_op jit(solution)/shard_map/ppermute | solution.py:39
  7.8 4.0 %collective-permute-start.2 = (bf16[16,128]{1,0:T(8,128)(2,1)S(1)}, bf16[16,128]{1,0:T(8,128)(2,1)S(1)}, u32[]{:S(2)}, u32[]{:S(2)}) collective-permute-start(bf16[16,128]{1,0:T(8,128)(2,1)S(1)} %pad_maximum_fusion.paths_ref), channel_id=1, source_target_pairs={{0,9},{1,8},{2,11},{3,10},{4,13},{5,12},{6,15},{7,14},{8,1},{9,0},... | collective-permute-start | bytes 12296 | tf_op jit(solution)/shard_map/ppermute | solution.py:39
  13.0 3.2 %collective-permute-start.5 = (f32[16,256]{1,0:T(8,128)S(1)}, f32[16,256]{1,0:T(8,128)S(1)}, u32[]{:S(2)}, u32[]{:S(2)}) collective-permute-start(f32[16,256]{1,0:T(8,128)S(1)} %get-tuple-element.38), channel_id=1, source_target_pairs={{0,3},{1,2},{2,1},{3,0},{4,7},{5,6},{6,5},{7,4},{8,11},{9,10},{10,... | collective-permute-start | bytes 49160 | tf_op jit(solution)/shard_map/ppermute | solution.py:39
  16.2 3.1 %collective-permute-start.6 = (f32[8,256]{1,0:T(8,128)S(1)}, f32[8,256]{1,0:T(8,128)S(1)}, u32[]{:S(2)}, u32[]{:S(2)}) collective-permute-start(f32[8,256]{1,0:T(8,128)S(1)} %slice.32), channel_id=1, source_target_pairs={{0,5},{1,4},{2,7},{3,6},{4,1},{5,0},{6,3},{7,2},{8,13},{9,12},{10,... | collective-permute-start | bytes 24584 | tf_op jit(solution)/shard_map/ppermute | solution.py:39
  19.3 4.0 %collective-permute-start.7 = (f32[4,256]{1,0:T(4,128)S(1)}, f32[4,256]{1,0:T(4,128)S(1)}, u32[]{:S(2)}, u32[]{:S(2)}) collective-permute-start(f32[4,256]{1,0:T(4,128)S(1)} %pad_maximum_fusion.1), channel_id=1, source_target_pairs={{0,9},{1,8},{2,11},{3,10},{4,13},{5,12},{6,15},{7,14},{8,1},{9,0},... | collective-permute-start | bytes 12296 | tf_op jit(solution)/shard_map/ppermute | solution.py:39
  23.3 1.2 %collective-permute-start.8 = (f32[2,256]{1,0:T(2,128)S(1)}, f32[2,256]{1,0:T(2,128)S(1)}, u32[]{:S(2)}, u32[]{:S(2)}) collective-permute-start(f32[2,256]{1,0:T(2,128)S(1)} %get-tuple-element.44), channel_id=1, source_target_pairs={{0,1},{1,0},{2,3},{3,2},{4,5},{5,4},{6,7},{7,6},{8,9},{9,8},{10,11... | collective-permute-start | bytes 6152 | tf_op jit(solution)/shard_map/ppermute | solution.py:39

commit v10 on v8

--- a/solution.py
+++ b/solution.py
@@ -243,10 +243,6 @@
     write_onehot(code, set_at, hot_ref)
 
 
-def other_rows_kernel(set_ref, code_ref, hot_ref):
-    write_onehot(code_ref[...], set_ref[:, :1], hot_ref)
-
-
 def net_block(paths, split_ref, trades):
     total = paths.shape[0]
     loaded = sum(jnp.dot(paths, split_ref[i], preferred_element_type=jnp.float32) for i in (2, 1, 0))
@@ -267,7 +263,8 @@
     return result
 
 
-def near_kernel(paths_ref, split_ref, used_ref, other_ref, onehot_ref, other_hot_ref, net_ref):
+def near_kernel(paths_ref, split_ref, used_ref, other_ref, onehot_ref, set_ref, code_ref, net_ref, other_hot_ref):
+    write_onehot(code_ref[...], set_ref[:, :1], other_hot_ref)
     trades = ((used_ref, onehot_ref), (other_ref, other_hot_ref))
     block = min(PATH_BLOCK, paths_ref.shape[0])
     for b in range(paths_ref.shape[0] // block):
@@ -352,13 +349,7 @@
         0,
         (me.astype(jnp.int32).reshape(1), live_count, ids, owner, margin, turned),
     )
-    (other_hot,) = call(
-        other_rows_kernel,
-        [shape((set_total, slot_total), bf16)],
-        [VMEM] * 2,
-        10**8,
-        (set_at, swap(code, 1, count)),
-    )
+    other_code = swap(code, 1, count)
     bit = 4
     while bit < count // 2:
         near = join(near, swap(near, bit, count), bit)
@@ -367,12 +358,12 @@
     side_total = near.shape[0]
     columns = DATES * side_total
     work = 4 * columns * slot_total * (width + set_total)
-    (near_net,) = call(
+    near_net, other_hot = call(
         near_kernel,
-        [shape((set_total, columns), f32)],
-        [VMEM] * 6,
+        [shape((set_total, columns), f32), shape((set_total, slot_total), bf16)],
+        [VMEM] * 7,
         work,
-        (near, split, used, other, onehot, other_hot),
+        (near, split, used, other, onehot, set_at, other_code),
     )
     kept, sent = call(
         far_kernel,

time: 25.4 us -> 25.4 us (level)
    pallas_call x7 -> x6, Pallas kernels: 4.9 us -> 4.82 us  [call(): pl.pallas_call(kernel, out_shape=outs, in_specs=specs, out_specs=[VMEM] *...]
where the time goes in v10:
time: 25.4 us; the launch traced here: 25.2 us
  starting transfers between devices  13.6 us (54%)
  waiting for transfers between devices  5.97 us (24%)
  Pallas kernels  4.82 us (19%)
  between operations  0.72 us (3%)
    ppermute x9, starting transfers between devices, swap(): return lax.ppermute(x, 'trade', [(i, i ^ (bit | 1)) for i in range(count)])  13.6 us
    ppermute x9, waiting for transfers between devices, swap(): return lax.ppermute(x, 'trade', [(i, i ^ (bit | 1)) for i in range(count)])  5.97 us
    pallas_call x6, Pallas kernels, call(): pl.pallas_call(kernel, out_shape=outs, in_specs=specs, out_specs=[VMEM] *...  4.82 us
  transfers between devices with their start and end apart: 9, of which 6 were waited for; matrix products, arithmetic and copies ran while one was open for 0% of the time, Pallas kernels for 12%

profile of v10, /device:TPU:0, one launch (start us, length us, event | category | flops | bytes accessed | tf_op | source)
XLA Modules:
  0.0 25.2 jit_solution(11107205706100216651)
XLA Ops:
  0.0 2.4 %collective-permute-start = (bf16[4,128]{1,0:T(4,128)(2,1)}, bf16[4,128]{1,0:T(4,128)(2,1)S(1)}, u32[]{:S(2)}, u32[]{:S(2)}) collective-permute-start(bf16[4,128]{1,0:T(4,128)(2,1)} %factors_hbm.1), channel_id=1, source_target_pairs={{0,3},{1,2},{2,1},{3,0},{4,7},{5,6},{6,5},{7,4},{8,11},{9,10},{10,... | collective-permute-start | bytes 3080 | tf_op jit(solution)/shard_map/ppermute | solution.py:38
  2.4 1.6 %shard_map.91 = (bf16[4,128]{1,0:T(4,128)(2,1)S(1)}, bf16[2048,256]{1,0:T(8,128)(2,1)S(1)}, s32[16,128]{1,0:T(8,128)S(1)}, s32[1,32]{1,0:T(1,128)S(1)}, f32[2,64...) custom-call(bf16[4,128]{1,0:T(4,128)(2,1)} %factors_hbm.1, bf16[2048,256]{1,0:T(8,128)(2,1)} %coef_hbm.1, ...), custom_call_target="tpu_custom_call" | custom-call | flops 100000000 | bytes 2130184 | tf_op jit(solution)/shard_map/pallas_call | solution.py:22
  4.0 0.0 collective-permute-done
  4.1 0.7 %collective-permute-start.3 = (bf16[2048,256]{1,0:T(8,128)(2,1)S(1)}, bf16[2048,256]{1,0:T(8,128)(2,1)S(1)}, u32[]{:S(2)}, u32[]{:S(2)}) collective-permute-start(bf16[2048,256]{1,0:T(8,128)(2,1)S(1)} %get-tuple-element.35.used_ref), channel_id=1, source_target_pairs={{0,1},{1,0},{2,3},{3,2},{4,5},{5,4},{6,7},{7,6},{8,9},{9,8},{10,11... | collective-permute-start | bytes 3145736 | tf_op jit(solution)/shard_map/ppermute | solution.py:38
  4.8 1.6 %collective-permute-start.1 = (bf16[8,128]{1,0:T(8,128)(2,1)S(1)}, bf16[8,128]{1,0:T(8,128)(2,1)S(1)}, u32[]{:S(2)}, u32[]{:S(2)}) collective-permute-start(bf16[8,128]{1,0:T(8,128)(2,1)S(1)} %pad_maximum_fusion.2), channel_id=1, source_target_pairs={{0,5},{1,4},{2,7},{3,6},{4,1},{5,0},{6,3},{7,2},{8,13},{9,12},{10,... | collective-permute-start | bytes 6152 | tf_op jit(solution)/shard_map/ppermute | solution.py:38
  7.1 0.2 shard_map.92
  7.3 0.2 collective-permute-start.4
  7.5 0.3 %collective-permute-done.1 = bf16[8,128]{1,0:T(8,128)(2,1)S(1)} collective-permute-done((bf16[8,128]{1,0:T(8,128)(2,1)S(1)}, bf16[8,128]{1,0:T(8,128)(2,1)S(1)}, u32[]{:S(2)}, u32[]{:S(2)}) %collective-permute-start.1) | collective-permute-done | bytes 2080 | tf_op jit(solution)/shard_map/ppermute | solution.py:38
  7.8 2.7 %collective-permute-start.2 = (bf16[16,128]{1,0:T(8,128)(2,1)S(1)}, bf16[16,128]{1,0:T(8,128)(2,1)S(1)}, u32[]{:S(2)}, u32[]{:S(2)}) collective-permute-start(bf16[16,128]{1,0:T(8,128)(2,1)S(1)} %pad_maximum_fusion.paths_ref), channel_id=1, source_target_pairs={{0,9},{1,8},{2,11},{3,10},{4,13},{5,12},{6,15},{7,14},{8,1},{9,0},... | collective-permute-start | bytes 12296 | tf_op jit(solution)/shard_map/ppermute | solution.py:38
  10.5 0.0 collective-permute-done.4.code_ref
  10.5 0.0 collective-permute-done.3.other_ref
  10.5 1.1 %shard_map.93 = (f32[32,128]{1,0:T(8,128)S(1)}, bf16[32,2048]{1,0:T(8,128)(2,1)S(1)}) custom-call(bf16[16,128]{1,0:T(8,128)(2,1)S(1)} %pad_maximum_fusion.paths_ref, bf16[3,128,256]{2,1,0:T(8,128)(2,1)S(1)} %get-tuple-element.34.split_ref, bf16[2048,256]{1,0:T(8,128)(2,1)S(1)} %get-tuple-element.35.used_ref, ...), custom_call_target="tpu_custom_call" | custom-call | flops 301989888 | bytes 2600960 | tf_op jit(solution)/shard_map/pallas_call | solution.py:22
  11.6 0.2 collective-permute-done.2.paths_ref
  11.9 1.1 %shard_map.94 = (f32[16,256]{1,0:T(8,128)S(1)}, f32[16,256]{1,0:T(8,128)S(1)}) custom-call(bf16[16,128]{1,0:T(8,128)(2,1)S(1)} %collective-permute-done.2.paths_ref, bf16[3,128,256]{2,1,0:T(8,128)(2,1)S(1)} %get-tuple-element.34.split_ref, bf16[2048,256]{1,0:T(8,128)(2,1)S(1)} %get-tuple-element.35.used_ref, ...), custom_call_target="tpu_custom_call" | custom-call | flops 301989888 | bytes 2609152 | tf_op jit(solution)/shard_map/pallas_call | solution.py:22
  12.9 1.6 %collective-permute-start.5 = (f32[16,256]{1,0:T(8,128)S(1)}, f32[16,256]{1,0:T(8,128)S(1)}, u32[]{:S(2)}, u32[]{:S(2)}) collective-permute-start(f32[16,256]{1,0:T(8,128)S(1)} %get-tuple-element.42), channel_id=1, source_target_pairs={{0,3},{1,2},{2,1},{3,0},{4,7},{5,6},{6,5},{7,4},{8,11},{9,10},{10,... | collective-permute-start | bytes 49160 | tf_op jit(solution)/shard_map/ppermute | solution.py:38
  14.5 1.6 %collective-permute-done.5 = f32[16,256]{1,0:T(8,128)S(1)} collective-permute-done((f32[16,256]{1,0:T(8,128)S(1)}, f32[16,256]{1,0:T(8,128)S(1)}, u32[]{:S(2)}, u32[]{:S(2)}) %collective-permute-start.5) | collective-permute-done | bytes 16416 | tf_op jit(solution)/shard_map/ppermute | solution.py:38
  16.2 1.6 %collective-permute-start.6 = (f32[8,256]{1,0:T(8,128)S(1)}, f32[8,256]{1,0:T(8,128)S(1)}, u32[]{:S(2)}, u32[]{:S(2)}) collective-permute-start(f32[8,256]{1,0:T(8,128)S(1)} %slice.32), channel_id=1, source_target_pairs={{0,5},{1,4},{2,7},{3,6},{4,1},{5,0},{6,3},{7,2},{8,13},{9,12},{10,... | collective-permute-start | bytes 24584 | tf_op jit(solution)/shard_map/ppermute | solution.py:38
  17.8 1.5 %collective-permute-done.6 = f32[8,256]{1,0:T(8,128)S(1)} collective-permute-done((f32[8,256]{1,0:T(8,128)S(1)}, f32[8,256]{1,0:T(8,128)S(1)}, u32[]{:S(2)}, u32[]{:S(2)}) %collective-permute-start.6) | collective-permute-done | bytes 8224 | tf_op jit(solution)/shard_map/ppermute | solution.py:38
  19.3 2.7 %collective-permute-start.7 = (f32[4,256]{1,0:T(4,128)S(1)}, f32[4,256]{1,0:T(4,128)S(1)}, u32[]{:S(2)}, u32[]{:S(2)}) collective-permute-start(f32[4,256]{1,0:T(4,128)S(1)} %pad_maximum_fusion.1), channel_id=1, source_target_pairs={{0,9},{1,8},{2,11},{3,10},{4,13},{5,12},{6,15},{7,14},{8,1},{9,0},... | collective-permute-start | bytes 12296 | tf_op jit(solution)/shard_map/ppermute | solution.py:38
  21.9 1.3 %collective-permute-done.7 = f32[4,256]{1,0:T(4,128)S(1)} collective-permute-done((f32[4,256]{1,0:T(4,128)S(1)}, f32[4,256]{1,0:T(4,128)S(1)}, u32[]{:S(2)}, u32[]{:S(2)}) %collective-permute-start.7) | collective-permute-done | bytes 4128 | tf_op jit(solution)/shard_map/ppermute | solution.py:38
  23.3 0.1 collective-permute-start.8
  23.4 0.1 shard_map.95.own_ref
  23.5 0.9 %collective-permute-done.8.other_ref = f32[2,256]{1,0:T(2,128)S(1)} collective-permute-done((f32[2,256]{1,0:T(2,128)S(1)}, f32[2,256]{1,0:T(2,128)S(1)}, u32[]{:S(2)}, u32[]{:S(2)}) %collective-permute-start.8) | collective-permute-done | bytes 2080 | tf_op jit(solution)/shard_map/ppermute | solution.py:38
  24.4 0.8 %shard_map.96 = f32[2,8]{1,0:T(2,128)} custom-call(f32[2,256]{1,0:T(2,128)S(1)} %collective-permute-done.8.other_ref, f32[2,512]{1,0:T(2,128)S(1)} %get-tuple-element.43.held_ref, f32[2,128]{1,0:T(2,128)S(1)} %get-tuple-element.44.limits_ref, f32[2,128]{1,0:T(2,128)S(1)} %shard_map.95.own_ref), custom_call_target="tpu_custom_call" | custom-call | flops 1000000 | bytes 8256 | tf_op jit(solution)/shard_map/pallas_call | solution.py:22
  (11 shorter events, 0.1 us)
Async XLA Ops:
  0.0 4.0 %collective-permute-start = (bf16[4,128]{1,0:T(4,128)(2,1)}, bf16[4,128]{1,0:T(4,128)(2,1)S(1)}, u32[]{:S(2)}, u32[]{:S(2)}) collective-permute-start(bf16[4,128]{1,0:T(4,128)(2,1)} %factors_hbm.1), channel_id=1, source_target_pairs={{0,3},{1,2},{2,1},{3,0},{4,7},{5,6},{6,5},{7,4},{8,11},{9,10},{10,... | collective-permute-start | bytes 3080 | tf_op jit(solution)/shard_map/ppermute | solution.py:38
  4.1 6.5 %collective-permute-start.3 = (bf16[2048,256]{1,0:T(8,128)(2,1)S(1)}, bf16[2048,256]{1,0:T(8,128)(2,1)S(1)}, u32[]{:S(2)}, u32[]{:S(2)}) collective-permute-start(bf16[2048,256]{1,0:T(8,128)(2,1)S(1)} %get-tuple-element.35.used_ref), channel_id=1, source_target_pairs={{0,1},{1,0},{2,3},{3,2},{4,5},{5,4},{6,7},{7,6},{8,9},{9,8},{10,11... | collective-permute-start | bytes 3145736 | tf_op jit(solution)/shard_map/ppermute | solution.py:38
  4.8 3.0 %collective-permute-start.1 = (bf16[8,128]{1,0:T(8,128)(2,1)S(1)}, bf16[8,128]{1,0:T(8,128)(2,1)S(1)}, u32[]{:S(2)}, u32[]{:S(2)}) collective-permute-start(bf16[8,128]{1,0:T(8,128)(2,1)S(1)} %pad_maximum_fusion.2), channel_id=1, source_target_pairs={{0,5},{1,4},{2,7},{3,6},{4,1},{5,0},{6,3},{7,2},{8,13},{9,12},{10,... | collective-permute-start | bytes 6152 | tf_op jit(solution)/shard_map/ppermute | solution.py:38
  7.3 3.2 %collective-permute-start.4 = (s32[16,128]{1,0:T(8,128)S(1)}, s32[16,128]{1,0:T(8,128)S(1)}, u32[]{:S(2)}, u32[]{:S(2)}) collective-permute-start(s32[16,128]{1,0:T(8,128)S(1)} %get-tuple-element.38), channel_id=1, source_target_pairs={{0,1},{1,0},{2,3},{3,2},{4,5},{5,4},{6,7},{7,6},{8,9},{9,8},{10,11... | collective-permute-start | bytes 24584 | tf_op jit(solution)/shard_map/ppermute | solution.py:38
  7.8 4.0 %collective-permute-start.2 = (bf16[16,128]{1,0:T(8,128)(2,1)S(1)}, bf16[16,128]{1,0:T(8,128)(2,1)S(1)}, u32[]{:S(2)}, u32[]{:S(2)}) collective-permute-start(bf16[16,128]{1,0:T(8,128)(2,1)S(1)} %pad_maximum_fusion.paths_ref), channel_id=1, source_target_pairs={{0,9},{1,8},{2,11},{3,10},{4,13},{5,12},{6,15},{7,14},{8,1},{9,0},... | collective-permute-start | bytes 12296 | tf_op jit(solution)/shard_map/ppermute | solution.py:38
  12.9 3.2 %collective-permute-start.5 = (f32[16,256]{1,0:T(8,128)S(1)}, f32[16,256]{1,0:T(8,128)S(1)}, u32[]{:S(2)}, u32[]{:S(2)}) collective-permute-start(f32[16,256]{1,0:T(8,128)S(1)} %get-tuple-element.42), channel_id=1, source_target_pairs={{0,3},{1,2},{2,1},{3,0},{4,7},{5,6},{6,5},{7,4},{8,11},{9,10},{10,... | collective-permute-start | bytes 49160 | tf_op jit(solution)/shard_map/ppermute | solution.py:38
  16.2 3.1 %collective-permute-start.6 = (f32[8,256]{1,0:T(8,128)S(1)}, f32[8,256]{1,0:T(8,128)S(1)}, u32[]{:S(2)}, u32[]{:S(2)}) collective-permute-start(f32[8,256]{1,0:T(8,128)S(1)} %slice.32), channel_id=1, source_target_pairs={{0,5},{1,4},{2,7},{3,6},{4,1},{5,0},{6,3},{7,2},{8,13},{9,12},{10,... | collective-permute-start | bytes 24584 | tf_op jit(solution)/shard_map/ppermute | solution.py:38
  19.3 4.0 %collective-permute-start.7 = (f32[4,256]{1,0:T(4,128)S(1)}, f32[4,256]{1,0:T(4,128)S(1)}, u32[]{:S(2)}, u32[]{:S(2)}) collective-permute-start(f32[4,256]{1,0:T(4,128)S(1)} %pad_maximum_fusion.1), channel_id=1, source_target_pairs={{0,9},{1,8},{2,11},{3,10},{4,13},{5,12},{6,15},{7,14},{8,1},{9,0},... | collective-permute-start | bytes 12296 | tf_op jit(solution)/shard_map/ppermute | solution.py:38
  23.3 1.2 %collective-permute-start.8 = (f32[2,256]{1,0:T(2,128)S(1)}, f32[2,256]{1,0:T(2,128)S(1)}, u32[]{:S(2)}, u32[]{:S(2)}) collective-permute-start(f32[2,256]{1,0:T(2,128)S(1)} %get-tuple-element.48), channel_id=1, source_target_pairs={{0,1},{1,0},{2,3},{3,2},{4,5},{5,4},{6,7},{7,6},{8,9},{9,8},{10,11... | collective-permute-start | bytes 6152 | tf_op jit(solution)/shard_map/ppermute | solution.py:38
